TPU v7x, 1024 devices: a whole 4x8x16 slice. The times are simulated.
1024 devices in a mesh: blk: 32 (over z, x_hi), grp: 32 (over x_lo, y, core).
Axes of the slice: x: 4 (x_hi: 2, x_lo: 2; x = x_hi * 2 + x_lo), y: 8, z: 16, core: 2. Of those that a mesh axis runs over, the one named last changes fastest.
Arguments:
- counts: bfloat16 [4, 32768, 8192], P(None, 'blk', 'grp'), may hold values from 0 to 200
- row_sums: int32 [32768], P('blk'), may hold values from 1000 to 29999
- col_sums: int32 [262144], P(('blk', 'grp')), may hold values from 1000 to 29999
- row_emb: float32 [300, 32768], P(None, 'blk'), may hold values from -1.5 to 1.5
- row_acc: float32 [300, 32768], P(None, 'blk'), may hold values from 0.05 to 0.5
- col_emb: float32 [300, 262144], P(None, ('blk', 'grp')), may hold values from -1.5 to 1.5
- col_acc: float32 [300, 262144], P(None, ('blk', 'grp')), may hold values from 0.05 to 0.5
Outputs:
- new_row_emb: float32 [300, 32768], P(None, ('blk', 'grp'))
- new_row_acc: float32 [300, 32768], P(None, ('blk', 'grp'))
- new_col_emb: float32 [300, 262144], P(None, ('blk', 'grp'))
- new_col_acc: float32 [300, 262144], P(None, ('blk', 'grp'))
All inputs are finite; a program needn't handle non-finite values.
Results may differ from a plain program's by a relative error of at most 0.0003.
Values sent between devices are 32-bit elements; how exact they have to be, the bound alone decides.
No kernel may reach another device: no remote copies, remote signals or barrier semaphores. Data moves between devices by JAX's collectives and lax.ppermute only.
A program may use at most 32 MiB of HBM per device.

v0:
```python
import jax
import jax.numpy as jnp
from jax import lax
from jax.sharding import PartitionSpec as P

log_total = 20.0
loss_scale = 1.0 / 256.0
step_rate = 0.1


def shifted(value, axis, steps):
    count = lax.axis_size(axis)
    pairs = [(source, (source + steps) % count) for source in range(count)]
    return lax.ppermute(value, axis, pairs)


def cell_grads(row_vecs, col_vecs, row_logs, col_logs, tile_counts):
    scores = jnp.dot(
        row_vecs.T, col_vecs, precision=lax.Precision.HIGHEST, preferred_element_type=jnp.float32
    )
    counts_real = tile_counts.astype(jnp.float32)
    target = (
        jnp.log(jnp.maximum(counts_real, 1.0)) + log_total - row_logs[:, None] - col_logs[None, :]
    )
    weight = 0.1 + 0.25 * jnp.sqrt(counts_real)
    residue = scores - target
    return loss_scale * jnp.where(counts_real > 0.5, weight * residue, jax.nn.sigmoid(residue))


def shards(counts, row_sums, col_sums, row_emb, row_acc, col_emb, col_acc):
    visits = counts.shape[0]
    row_logs = jnp.log(row_sums.astype(jnp.float32))
    moving = (col_emb, col_acc, jnp.log(col_sums.astype(jnp.float32)))
    row_total = jnp.zeros_like(row_emb)
    for turn_index in range(visits):
        if turn_index > 0:
            moving = shifted((moving[0], moving[1], moving[2]), "blk", 1)
        col_vecs, col_moment, col_logs = moving
        cell_grad = cell_grads(row_emb, col_vecs, row_logs, col_logs, counts[turn_index])
        row_total = row_total + jnp.dot(
            col_vecs,
            cell_grad.T,
            precision=lax.Precision.HIGHEST,
            preferred_element_type=jnp.float32,
        )
        col_grad = jnp.dot(
            row_emb, cell_grad, precision=lax.Precision.HIGHEST, preferred_element_type=jnp.float32
        )
        new_moment = col_moment + col_grad * col_grad
        new_vecs = col_vecs - step_rate * col_grad / jnp.sqrt(new_moment)
        moving = (new_vecs, new_moment, col_logs)
    groups = lax.axis_size("grp")
    share_width = row_emb.shape[1] // groups
    start = lax.axis_index("grp") * share_width
    summed = lax.psum(row_total, "grp")
    row_grad = lax.dynamic_slice_in_dim(summed, start, share_width, 1)
    own_vecs = lax.dynamic_slice_in_dim(row_emb, start, share_width, 1)
    own_moment = lax.dynamic_slice_in_dim(row_acc, start, share_width, 1)
    new_row_moment = own_moment + row_grad * row_grad
    new_row_vecs = own_vecs - step_rate * row_grad / jnp.sqrt(new_row_moment)
    return (new_row_vecs, new_row_moment, moving[0], moving[1])


def solution(mesh):
    return jax.shard_map(
        shards,
        mesh=mesh,
        in_specs=(
            P(None, "blk", "grp"),
            P("blk"),
            P(("blk", "grp")),
            P(None, "blk"),
            P(None, "blk"),
            P(None, ("blk", "grp")),
            P(None, ("blk", "grp")),
        ),
        out_specs=(
            P(None, ("blk", "grp")),
            P(None, ("blk", "grp")),
            P(None, ("blk", "grp")),
            P(None, ("blk", "grp")),
        ),
        check_vma=False,
    )
```

profile of v0, /device:TPU:2, one launch (start us, length us, event | category | flops | bytes accessed | tf_op | source)
XLA Modules:
  0.0 337.0 jit_solution(8461654131903580504)
XLA Ops:
  8.6 5.1 %fusion.8 = f32[1024,256]{1,0:T(8,128)S(1)} fusion(f32[300,1024]{1,0:T(8,128)} %param.10, f32[300,256]{1,0:T(8,128)} %param.12, f32[256]{0:T(256)S(1)} %convert_log_fusion.1, f32[1024]{0:T(1024)S(1)} %convert_log_fusion, bf16[4,1024,256]{2,1,0:T(8,128)(2,1)} %param.7), kind=kOutput, calls=%fused_computation.26 | convolution fusion | flops 947650560 | bytes 3113984 | tf_op jit(solution)/shard_map/dot_general | solution.py:18
  13.7 1.2 fusion.56
  15.0 4.0 %collective-permute-start = (f32[300,256]{1,0:T(8,128)S(1)}, f32[300,256]{1,0:T(8,128)S(1)}, u32[]{:S(2)}, u32[]{:S(2)}) collective-permute-start(f32[300,256]{1,0:T(8,128)S(1)} %get-tuple-element.16), channel_id=1, source_target_pairs={{0,32},{32,64},{64,96},{96,128},{128,160},{160,192},{192,224},{224... | collective-permute-start | bytes 921608 | tf_op jit(solution)/shard_map/ppermute | solution.py:14
  19.0 5.1 %collective-permute-start.1 = (f32[256]{0:T(256)S(1)}, f32[256]{0:T(256)S(1)}, u32[]{:S(2)}, u32[]{:S(2)}) collective-permute-start(f32[256]{0:T(256)S(1)} %convert_log_fusion.1), channel_id=1, source_target_pairs={{0,32},{32,64},{64,96},{96,128},{128,160},{160,192},{192,224},{224... | collective-permute-start | bytes 3080 | tf_op jit(solution)/shard_map/ppermute | solution.py:14
  24.1 4.0 %collective-permute-start.2 = (f32[300,256]{1,0:T(8,128)S(1)}, f32[300,256]{1,0:T(8,128)S(1)}, u32[]{:S(2)}, u32[]{:S(2)}) collective-permute-start(f32[300,256]{1,0:T(8,128)S(1)} %get-tuple-element.17), channel_id=1, source_target_pairs={{0,32},{32,64},{64,96},{96,128},{128,160},{160,192},{192,224},{224... | collective-permute-start | bytes 921608 | tf_op jit(solution)/shard_map/ppermute | solution.py:14
  28.2 14.8 %collective-permute-done.1 = f32[256]{0:T(256)S(1)} collective-permute-done((f32[256]{0:T(256)S(1)}, f32[256]{0:T(256)S(1)}, u32[]{:S(2)}, u32[]{:S(2)}) %collective-permute-start.1) | collective-permute-done | bytes 1056 | tf_op jit(solution)/shard_map/ppermute | solution.py:14
  43.0 3.5 %fusion.19 = f32[1024,256]{1,0:T(8,128)S(1)} fusion(f32[300,256]{1,0:T(8,128)S(1)} %collective-permute-done, f32[300,1024]{1,0:T(8,128)S(1)} %copy-done, f32[256]{0:T(256)S(1)} %collective-permute-done.1, bf16[4,1024,256]{2,1,0:T(8,128)(2,1)S(1)} %copy-done.3, f32[1024]{0:T(1024)S(1)} %convert_log_fusion), kind=kOutput, calls=%fused_computation.37 | convolution fusion | flops 947650560 | bytes 3113984 | tf_op jit(solution)/shard_map/dot_general | solution.py:18
  46.5 2.3 collective-permute-done.2
  50.1 1.9 collective-permute-start.3
  52.0 1.9 collective-permute-start.4
  53.9 2.1 collective-permute-start.5
  56.0 9.9 %collective-permute-done.4 = f32[256]{0:T(256)S(1)} collective-permute-done((f32[256]{0:T(256)S(1)}, f32[256]{0:T(256)S(1)}, u32[]{:S(2)}, u32[]{:S(2)}) %collective-permute-start.4) | collective-permute-done | bytes 1056 | tf_op jit(solution)/shard_map/ppermute | solution.py:14
  65.9 3.5 %fusion.30 = f32[1024,256]{1,0:T(8,128)S(1)} fusion(f32[256]{0:T(256)S(1)} %collective-permute-done.4, bf16[4,1024,256]{2,1,0:T(8,128)(2,1)S(1)} %copy-done.3, f32[1024]{0:T(1024)S(1)} %convert_log_fusion, f32[300,256]{1,0:T(8,128)S(1)} %collective-permute-done.3, f32[300,1024]{1,0:T(8,128)S(1)} %copy-done), kind=kOutput, calls=%fused_computation.48 | convolution fusion | flops 947650560 | bytes 3113984 | tf_op jit(solution)/shard_map/dot_general | solution.py:18
  69.4 1.4 collective-permute-done.5
  70.8 1.2 fusion.54
  72.1 1.9 collective-permute-start.6
  75.2 2.1 collective-permute-start.7
  78.6 6.7 %collective-permute-done.7 = f32[256]{0:T(256)S(1)} collective-permute-done((f32[256]{0:T(256)S(1)}, f32[256]{0:T(256)S(1)}, u32[]{:S(2)}, u32[]{:S(2)}) %collective-permute-start.7) | collective-permute-done | bytes 1056 | tf_op jit(solution)/shard_map/ppermute | solution.py:14
  85.2 3.4 %fusion.42 = f32[1024,256]{1,0:T(8,128)S(1)} fusion(f32[256]{0:T(256)S(1)} %collective-permute-done.7, bf16[4,1024,256]{2,1,0:T(8,128)(2,1)S(1)} %copy-done.3, f32[1024]{0:T(1024)S(1)} %convert_log_fusion, f32[300,256]{1,0:T(8,128)S(1)} %collective-permute-done.6, f32[300,1024]{1,0:T(8,128)S(1)} %copy-done), kind=kOutput, calls=%fused_computation.60 | convolution fusion | flops 947650560 | bytes 3113984 | tf_op jit(solution)/shard_map/dot_general | solution.py:18
  89.9 2.4 fusion.1
  92.3 1.9 collective-permute-start.8
  94.3 10.5 %collective-permute-done.8 = f32[300,256]{1,0:T(8,128)S(1)} collective-permute-done((f32[300,256]{1,0:T(8,128)S(1)}, f32[300,256]{1,0:T(8,128)S(1)}, u32[]{:S(2)}, u32[]{:S(2)}) %collective-permute-start.8) | collective-permute-done | bytes 307232 | tf_op jit(solution)/shard_map/ppermute | solution.py:14
  104.7 2.1 fusion.53
  106.8 220.8 %all-reduce.2.cloned.1.call-done = f32[300,1024]{1,0:T(8,128)} async-done(((f32[300,1024]{1,0:T(8,128)}), f32[300,1024]{1,0:T(8,128)}) %all-reduce.2.cloned.1.call-update) | async-done | bytes 1228816 | tf_op jit(solution)/shard_map/psum | solution.py:55
  (22 shorter events, 9.0 us)
Async XLA Ops:
  7.2 320.4 %all-reduce.2.cloned.1.call-start = ((), (), s32[]{:S(2)}) async-start(), calls=%async_computation | async-start | bytes 2490368 | tf_op jit(solution)/shard_map/psum | solution.py:55
  8.6 5.1 %copy-start = (f32[300,1024]{1,0:T(8,128)S(1)}, f32[300,1024]{1,0:T(8,128)}, u32[]{:S(2)}) copy-start(f32[300,1024]{1,0:T(8,128)} %param.10) | copy-start | bytes 3686404
  8.6 5.1 %copy-start.1 = (f32[300,256]{1,0:T(8,128)S(1)}, f32[300,256]{1,0:T(8,128)}, u32[]{:S(2)}) copy-start(f32[300,256]{1,0:T(8,128)} %param.12) | copy-start | bytes 921604
  8.6 5.1 %copy-start.2 = (f32[300,256]{1,0:T(8,128)S(1)}, f32[300,256]{1,0:T(8,128)}, u32[]{:S(2)}) copy-start(f32[300,256]{1,0:T(8,128)} %param.13) | copy-start | bytes 921604
  13.7 29.3 %copy-start.3 = (bf16[4,1024,256]{2,1,0:T(8,128)(2,1)S(1)}, bf16[4,1024,256]{2,1,0:T(8,128)(2,1)}, u32[]{:S(2)}) copy-start(bf16[4,1024,256]{2,1,0:T(8,128)(2,1)} %param.7) | copy-start | bytes 6291460
  15.0 28.0 %collective-permute-start = (f32[300,256]{1,0:T(8,128)S(1)}, f32[300,256]{1,0:T(8,128)S(1)}, u32[]{:S(2)}, u32[]{:S(2)}) collective-permute-start(f32[300,256]{1,0:T(8,128)S(1)} %get-tuple-element.16), channel_id=1, source_target_pairs={{0,32},{32,64},{64,96},{96,128},{128,160},{160,192},{192,224},{224... | collective-permute-start | bytes 921608 | tf_op jit(solution)/shard_map/ppermute | solution.py:14
  19.0 24.0 %collective-permute-start.1 = (f32[256]{0:T(256)S(1)}, f32[256]{0:T(256)S(1)}, u32[]{:S(2)}, u32[]{:S(2)}) collective-permute-start(f32[256]{0:T(256)S(1)} %convert_log_fusion.1), channel_id=1, source_target_pairs={{0,32},{32,64},{64,96},{96,128},{128,160},{160,192},{192,224},{224... | collective-permute-start | bytes 3080 | tf_op jit(solution)/shard_map/ppermute | solution.py:14
  24.1 24.7 %collective-permute-start.2 = (f32[300,256]{1,0:T(8,128)S(1)}, f32[300,256]{1,0:T(8,128)S(1)}, u32[]{:S(2)}, u32[]{:S(2)}) collective-permute-start(f32[300,256]{1,0:T(8,128)S(1)} %get-tuple-element.17), channel_id=1, source_target_pairs={{0,32},{32,64},{64,96},{96,128},{128,160},{160,192},{192,224},{224... | collective-permute-start | bytes 921608 | tf_op jit(solution)/shard_map/ppermute | solution.py:14
  50.1 15.9 %collective-permute-start.3 = (f32[300,256]{1,0:T(8,128)S(1)}, f32[300,256]{1,0:T(8,128)S(1)}, u32[]{:S(2)}, u32[]{:S(2)}) collective-permute-start(f32[300,256]{1,0:T(8,128)S(1)} %get-tuple-element.14), channel_id=1, source_target_pairs={{0,32},{32,64},{64,96},{96,128},{128,160},{160,192},{192,224},{224... | collective-permute-start | bytes 921608 | tf_op jit(solution)/shard_map/ppermute | solution.py:14
  52.0 13.9 %collective-permute-start.4 = (f32[256]{0:T(256)S(1)}, f32[256]{0:T(256)S(1)}, u32[]{:S(2)}, u32[]{:S(2)}) collective-permute-start(f32[256]{0:T(256)S(1)} %collective-permute-done.1), channel_id=1, source_target_pairs={{0,32},{32,64},{64,96},{96,128},{128,160},{160,192},{192,224},{224... | collective-permute-start | bytes 3080 | tf_op jit(solution)/shard_map/ppermute | solution.py:14
  53.9 16.9 %collective-permute-start.5 = (f32[300,256]{1,0:T(8,128)S(1)}, f32[300,256]{1,0:T(8,128)S(1)}, u32[]{:S(2)}, u32[]{:S(2)}) collective-permute-start(f32[300,256]{1,0:T(8,128)S(1)} %get-tuple-element.15), channel_id=1, source_target_pairs={{0,32},{32,64},{64,96},{96,128},{128,160},{160,192},{192,224},{224... | collective-permute-start | bytes 921608 | tf_op jit(solution)/shard_map/ppermute | solution.py:14
  72.1 13.2 %collective-permute-start.6 = (f32[300,256]{1,0:T(8,128)S(1)}, f32[300,256]{1,0:T(8,128)S(1)}, u32[]{:S(2)}, u32[]{:S(2)}) collective-permute-start(f32[300,256]{1,0:T(8,128)S(1)} %get-tuple-element.12), channel_id=1, source_target_pairs={{0,32},{32,64},{64,96},{96,128},{128,160},{160,192},{192,224},{224... | collective-permute-start | bytes 921608 | tf_op jit(solution)/shard_map/ppermute | solution.py:14
  75.2 10.0 %collective-permute-start.7 = (f32[256]{0:T(256)S(1)}, f32[256]{0:T(256)S(1)}, u32[]{:S(2)}, u32[]{:S(2)}) collective-permute-start(f32[256]{0:T(256)S(1)} %collective-permute-done.4), channel_id=1, source_target_pairs={{0,32},{32,64},{64,96},{96,128},{128,160},{160,192},{192,224},{224... | collective-permute-start | bytes 3080 | tf_op jit(solution)/shard_map/ppermute | solution.py:14
  92.3 12.4 %collective-permute-start.8 = (f32[300,256]{1,0:T(8,128)S(1)}, f32[300,256]{1,0:T(8,128)S(1)}, u32[]{:S(2)}, u32[]{:S(2)}) collective-permute-start(f32[300,256]{1,0:T(8,128)S(1)} %get-tuple-element.13), channel_id=1, source_target_pairs={{0,32},{32,64},{64,96},{96,128},{128,160},{160,192},{192,224},{224... | collective-permute-start | bytes 921608 | tf_op jit(solution)/shard_map/ppermute | solution.py:14
Sparse Core Ops, SparseCore 0:
  92.5 235.0 all-reduce.1
where the time goes:
time: 337 us
  waiting for transfers between devices  266 us (79%)
  matrix products  27.3 us (8%)
  starting transfers between devices  25.2 us (7%)
  between operations  14.2 us (4%)
    psum x1, waiting for transfers between devices, shards(): summed = lax.psum(row_total, 'grp')  221 us
    ppermute x9, waiting for transfers between devices, shifted(): return lax.ppermute(value, axis, pairs)  45.6 us
    ppermute x9, starting transfers between devices, shifted(): return lax.ppermute(value, axis, pairs)  25.1 us
    dot_general x4, matrix products, cell_grads(): jnp.dot(row_vecs.T, col_vecs, precision=lax.Precision.HIGHEST, preferred_...  15.4 us
  transfers between devices with their start and end apart: 10, of which 7 were waited for; matrix products, arithmetic and copies ran while one was open for 3% of the time, Pallas kernels for 0%

commit v1 on v0

v1 whole, which is shorter than its diff:
```python
import jax
import jax.numpy as jnp
from jax import lax
from jax.experimental import pallas as pl
from jax.experimental.pallas import tpu as pltpu
from jax.sharding import PartitionSpec as P

log_total = 20.0
loss_scale = 1.0 / 256.0
step_rate = 0.1

WIDTH = 300
PADW = 304
LANES = 384
ROWS = 1024
HALF = 128
TILE = 256
SHARE = 32
PACK = 40

f32 = jnp.float32
bf16 = jnp.bfloat16
VM = pl.BlockSpec(memory_space=pltpu.VMEM)
FAR = pl.BlockSpec(memory_space=pl.ANY)


def split(value):
    high = value.astype(bf16)
    return high, (value - high.astype(f32)).astype(bf16)


def dot(left, right):
    return jnp.dot(left, right, preferred_element_type=f32)


def call(name, body, out, operands, scratch=(), far=0, room=4):
    specs = [FAR] * far + [VM] * (len(operands) - far)
    spaces = [pltpu.HBM] * far + [pltpu.VMEM] * (len(operands) - far)
    placed = [pltpu.with_memory_space_constraint(each, space) for each, space in zip(operands, spaces)]
    return pl.pallas_call(
        body,
        out_shape=out,
        in_specs=specs,
        out_specs=jax.tree.map(lambda _: VM, out),
        scratch_shapes=list(scratch),
        compiler_params=pltpu.CompilerParams(vmem_limit_bytes=room * 1024 * 1024),
        cost_estimate=pl.CostEstimate(flops=1 << 20, bytes_accessed=1 << 10, transcendentals=0),
        name=name,
    )(*placed)


def near(*dims, of=f32):
    return pltpu.VMEM(dims, of)


def free(*dims, of=f32):
    return jax.ShapeDtypeStruct(dims, of)


def fetch(source, target, done):
    copy = pltpu.make_async_copy(source, target, done)
    copy.start()
    return copy


def count_tables(counts_ref, logs_ref, target_ref, weight_ref):
    for at in range(0, ROWS, TILE):
        base = logs_ref[at : at + TILE, :]
        for side in range(0, 2 * HALF, HALF):
            counts = counts_ref[at : at + TILE, side : side + HALF].astype(f32)
            target_ref[at : at + TILE, side : side + HALF] = jnp.log(jnp.maximum(counts, 1.0)) + base
            weight = loss_scale * (0.1 + 0.25 * jnp.sqrt(counts))
            weight_ref[at : at + TILE, side : side + HALF] = jnp.where(counts > 0.5, weight, 0.0)


def prep_body(
    row_hbm, counts_hbm, vecs_hbm, moment_hbm, row_sums_ref, col_sums_ref,
    hi_ref, lo_ref, turned_hi_ref, turned_lo_ref, logs_ref, target_ref, weight_ref, left_ref, right_ref,
    given_ref, row_ref, counts_ref, vecs_ref, moment_ref, done,
):
    get_counts = fetch(counts_hbm.at[0], counts_ref, done.at[0])
    get_rows = fetch(row_hbm, given_ref, done.at[1])
    get_vecs = fetch(vecs_hbm, vecs_ref, done.at[2])
    get_moment = fetch(moment_hbm, moment_ref, done.at[3])
    logs = log_total - jnp.log(row_sums_ref[...].astype(f32))
    logs_ref[...] = jnp.broadcast_to(logs, (HALF, ROWS)).T
    row_ref[WIDTH:, :] = jnp.zeros((LANES - WIDTH, ROWS), f32)
    get_counts.wait()
    count_tables(counts_ref, logs_ref, target_ref, weight_ref)
    get_rows.wait()
    row_ref[0:WIDTH, :] = given_ref[...]
    high, low = split(given_ref[...])
    hi_ref[...] = high
    lo_ref[...] = low
    for at in range(0, ROWS, TILE):
        high, low = split(row_ref[:, at : at + TILE].T)
        turned_hi_ref[at : at + TILE, :] = high
        turned_lo_ref[at : at + TILE, :] = low
    get_vecs.wait()
    get_moment.wait()
    for side, ref in enumerate((left_ref, right_ref)):
        lanes = slice(side * HALF, (side + 1) * HALF)
        ref[0:WIDTH, :] = vecs_ref[:, lanes]
        ref[WIDTH:PADW, :] = jnp.broadcast_to(jnp.log(col_sums_ref[:, lanes].astype(f32)), (PADW - WIDTH, HALF))
        ref[PADW : PADW + WIDTH, :] = moment_ref[:, lanes]
        ref[PADW + WIDTH :, :] = jnp.zeros((PADW - WIDTH, HALF), f32)


def shares_body(row_hbm, acc_hbm, vecs_ref, moment_ref, given_ref, block_ref, turned_ref, done):
    group = lax.axis_index("grp")
    lanes = pl.ds(pl.multiple_of((group >> 2) * 128, 128), 128)
    gets = [fetch(source.at[:, lanes], given_ref.at[at], done.at[at]) for at, source in enumerate((row_hbm, acc_hbm))]
    for at, ref in enumerate((vecs_ref, moment_ref)):
        gets[at].wait()
        block_ref[0:WIDTH, :] = given_ref[at]
        block_ref[WIDTH:, :] = jnp.zeros((LANES - WIDTH, 128), f32)
        turned_ref[...] = block_ref[...].T
        ref[...] = turned_ref[pl.ds(pl.multiple_of((group & 3) * SHARE, SHARE), SHARE), 0:WIDTH]


def split_columns(vecs, both_ref):
    inside = lax.broadcasted_iota(jnp.int32, (PADW, HALF), 0) < WIDTH
    high, low = split(jnp.where(inside, vecs, 0.0))
    both_ref[0:PADW, 0:HALF] = high
    both_ref[0:PADW, HALF:] = low
    both_ref[PADW:, :] = jnp.zeros((LANES - PADW, 2 * HALF), bf16)


def cells(col_logs, both_ref, turned_hi_ref, turned_lo_ref, target_ref, weight_ref, grad_ref, side):
    for at in range(0, ROWS, TILE):
        rows = slice(at, at + TILE)
        lanes = slice(side * HALF, (side + 1) * HALF)
        wide = dot(turned_hi_ref[rows, :], both_ref[...])
        scores = wide[:, :HALF] + wide[:, HALF:] + dot(turned_lo_ref[rows, :], both_ref[:, :HALF])
        residue = scores - (target_ref[rows, lanes] - col_logs)
        weight = weight_ref[rows, lanes]
        seen = weight * residue
        unseen = loss_scale / (1.0 + jnp.exp(-residue))
        high, low = split(jnp.where(weight > 0.0, seen, unseen))
        grad_ref[rows, :HALF] = high
        grad_ref[rows, HALF:] = low


def col_grads(hi_ref, lo_ref, grad_ref):
    wide = dot(hi_ref[...], grad_ref[...])
    return wide[:, :HALF] + wide[:, HALF:] + dot(lo_ref[...], grad_ref[:, :HALF])


def updated(vecs, moment, grad):
    new_moment = moment + grad * grad
    return vecs - step_rate * grad / jnp.sqrt(new_moment), new_moment


def visit_body(side, apart, state_ref, turned_hi_ref, turned_lo_ref, hi_ref, lo_ref, target_ref, weight_ref, *refs):
    grad_ref, both_ref = refs[-2:]
    if not apart:
        next_ref = refs[0]
        moment_ref = next_ref.at[PADW:]
    elif side == 0:
        next_ref, moment_ref = refs[:2]
    else:
        next_ref, pair_ref = refs[1:3]
        pair_ref[0:PADW, :] = refs[0][...]
        moment_ref = pair_ref.at[PADW:]
    split_columns(state_ref[0:PADW, :], both_ref)
    cells(state_ref[WIDTH : WIDTH + 1, :], both_ref, turned_hi_ref, turned_lo_ref, target_ref, weight_ref, grad_ref, side)
    grad = col_grads(hi_ref, lo_ref, grad_ref)
    vecs, moment = updated(state_ref[0:WIDTH, :], state_ref[PADW : PADW + WIDTH, :], grad)
    next_ref[0:WIDTH, :] = vecs
    next_ref[WIDTH:PADW, :] = state_ref[WIDTH:PADW, :]
    moment_ref[0:WIDTH, :] = moment
    moment_ref[WIDTH:, :] = jnp.zeros((PADW - WIDTH, HALF), f32)


def last_update_body(vecs_a_ref, vecs_b_ref, moments_ref, grad_a_ref, grad_b_ref, hi_ref, lo_ref, new_ref, new_moment_ref):
    for side, (vecs_ref, grad_ref) in enumerate(((vecs_a_ref, grad_a_ref), (vecs_b_ref, grad_b_ref))):
        grad = col_grads(hi_ref, lo_ref, grad_ref)
        vecs, moment = updated(vecs_ref[0:WIDTH, :], moments_ref[side * PADW : side * PADW + WIDTH, :], grad)
        new_ref[:, side * HALF : (side + 1) * HALF] = vecs
        new_moment_ref[:, side * HALF : (side + 1) * HALF] = moment


def spread(vecs_ref, high_ref, low_ref):
    main_high, main_low = split(vecs_ref[0:256, :])
    tail = vecs_ref[256:PADW, :]
    inside = lax.broadcasted_iota(jnp.int32, (PADW - 256, HALF), 0) < WIDTH - 256
    tail_high, tail_low = split(jnp.where(inside, tail, 0.0))
    gap = jnp.zeros((64 - (PADW - 256), HALF), bf16)
    places = ((high_ref, 0, main_high, tail_high), (high_ref, HALF, main_high, tail_high), (low_ref, 0, main_low, tail_low))
    for ref, at, main, rest in places:
        ref[0:256, at : at + HALF] = main
        for start in (256, 320):
            ref[start : start + PADW - 256, at : at + HALF] = rest
            ref[start + PADW - 256 : start + 64, at : at + HALF] = gap


def row_part(grad_ref, high_ref, low_ref, rows):
    by_columns = (((1,), (1,)), ((), ()))
    part = lax.dot_general(grad_ref[rows, :], high_ref[...], by_columns, preferred_element_type=f32)
    return part + lax.dot_general(grad_ref[rows, :HALF], low_ref[...], by_columns, preferred_element_type=f32)


SPREAD = [pltpu.VMEM((LANES, 2 * HALF), bf16), pltpu.VMEM((LANES, HALF), bf16)]


def beside_body(
    turn, counts_hbm, vecs_a_ref, vecs_b_ref, grad_a_ref, grad_b_ref, logs_ref, *refs
):
    before_ref = refs[0] if turn else None
    total_ref, target_ref, weight_ref, counts_ref, high_a_ref, low_a_ref, high_b_ref, low_b_ref, done = refs[1 if turn else 0 :]
    get_counts = fetch(counts_hbm.at[turn + 1], counts_ref, done)
    spread(vecs_a_ref, high_a_ref, low_a_ref)
    spread(vecs_b_ref, high_b_ref, low_b_ref)
    for at in range(0, ROWS, TILE):
        rows = slice(at, at + TILE)
        part = row_part(grad_a_ref, high_a_ref, low_a_ref, rows) + row_part(grad_b_ref, high_b_ref, low_b_ref, rows)
        total_ref[rows, :] = before_ref[rows, :] + part if turn else part
    get_counts.wait()
    count_tables(counts_ref, logs_ref, target_ref, weight_ref)


def last_half(side, vecs_ref, turned_hi_ref, turned_lo_ref, target_ref, weight_ref, before_ref, grad_ref, total_ref, both_ref, high_ref, low_ref):
    split_columns(vecs_ref[0:PADW, :], both_ref)
    cells(vecs_ref[WIDTH : WIDTH + 1, :], both_ref, turned_hi_ref, turned_lo_ref, target_ref, weight_ref, grad_ref, side)
    spread(vecs_ref, high_ref, low_ref)
    for at in range(0, ROWS, TILE):
        rows = slice(at, at + TILE)
        total_ref[rows, :] = before_ref[rows, :] + row_part(grad_ref, high_ref, low_ref, rows)


def last_body(side, vecs_ref, turned_hi_ref, turned_lo_ref, target_ref, weight_ref, before_ref, grad_ref, keep_ref, send_ref, total_ref, *scratch):
    last_half(side, vecs_ref, turned_hi_ref, turned_lo_ref, target_ref, weight_ref, before_ref, grad_ref, total_ref, *scratch)
    core = lax.axis_index("grp") & 1
    left = lax.broadcasted_iota(jnp.int32, (8, 128), 1) < 64
    for ref, half in ((keep_ref, core), (send_ref, 1 - core)):
        for slot in range(16):
            base = pl.multiple_of(slot * 2 * SHARE + half * SHARE, SHARE)
            block = total_ref[pl.ds(base, SHARE), :]
            ref[slot * PACK : slot * PACK + SHARE, :] = block[:, :256]
            for pair in range(2):
                upper = block[pair * 16 : pair * 16 + 8, 256:]
                lower = block[pair * 16 + 8 : pair * 16 + 16, 256:]
                ref[slot * PACK + SHARE : (slot + 1) * PACK, pair * 128 : (pair + 1) * 128] = jnp.where(left, upper, lower)


def halves_body(keep_ref, got_ref, leaving_ref, staying_ref):
    half = 8 * PACK
    along_x = lax.axis_index("grp") >> 4
    for ref, at in ((leaving_ref, 1 - along_x), (staying_ref, along_x)):
        rows = pl.ds(pl.multiple_of(at * half, half), half)
        ref[...] = keep_ref[rows, :] + got_ref[rows, :]


def sum_body(new_ref, new_moment_ref, left_ref, right_ref, out_ref):
    for slot in range(8):
        rows = slice(slot * PACK, (slot + 1) * PACK)
        out_ref[slot] = left_ref[rows, :] + right_ref[rows, :]


def finish_body(parts_ref, vecs_ref, moment_ref, new_ref, new_moment_ref, grad_ref):
    total = parts_ref[0]
    for at in range(1, parts_ref.shape[0]):
        total = total + parts_ref[at]
    grad_ref[:, :256] = total[0:SHARE, :]
    for group in range(4):
        rest = total[SHARE:PACK, (group // 2) * 128 : (group // 2 + 1) * 128]
        if group % 2:
            rest = pltpu.roll(rest, 64, 1)
        grad_ref[group * 8 : (group + 1) * 8, 256:] = rest
    vecs, moment = updated(vecs_ref[...], moment_ref[...], grad_ref[:, :WIDTH])
    new_ref[...] = vecs
    new_moment_ref[...] = moment


def shifted(value):
    count = lax.axis_size("blk")
    return lax.ppermute(value, "blk", [(source, (source + 1) % count) for source in range(count)])


def swapped(value, bit):
    count = lax.axis_size("grp")
    return lax.ppermute(value, "grp", [(source, source ^ bit) for source in range(count)])


def shards(counts, row_sums, col_sums, row_emb, row_acc, col_emb, col_acc):
    visits = counts.shape[0]
    cell_half = near(ROWS, 2 * HALF, of=bf16)
    table = near(ROWS, 2 * HALF)
    both = pltpu.VMEM((LANES, 2 * HALF), bf16)

    hi, lo, turned_hi, turned_lo, row_logs, target, weight, *states = call(
        "prep",
        prep_body,
        (near(WIDTH, ROWS, of=bf16),) * 2 + (near(ROWS, LANES, of=bf16),) * 2 + (near(ROWS, HALF), table, table) + (near(2 * PADW, HALF),) * 2,
        (row_emb, counts, col_emb, col_acc, row_sums.reshape(1, ROWS), col_sums.reshape(1, 2 * HALF)),
        [
            pltpu.VMEM((WIDTH, ROWS), f32),
            pltpu.VMEM((LANES, ROWS), f32),
            pltpu.VMEM((ROWS, 2 * HALF), bf16),
            pltpu.VMEM((WIDTH, 2 * HALF), f32),
            pltpu.VMEM((WIDTH, 2 * HALF), f32),
            pltpu.SemaphoreType.DMA((4,)),
        ],
        far=4,
        room=6,
    )

    total = ()
    for turn in range(visits - 1):
        nexts, grads = [], []
        apart = turn == visits - 2
        first = ()
        for side in range(2):
            outs = (near(2 * PADW, HALF),)
            if apart:
                outs = (near(PADW, HALF), near((1 + side) * PADW, HALF))
            after, *moment, grad = call(
                "visit",
                lambda *refs, side=side, apart=apart: visit_body(side, apart, *refs),
                outs + (cell_half,),
                (states[side], turned_hi, turned_lo, hi, lo, target, weight, *first),
                [both],
            )
            grads.append(grad)
            nexts.append(shifted(after))
            first = moment
        *total, target, weight = call(
            "beside",
            lambda *refs, turn=turn: beside_body(turn, *refs),
            (near(ROWS, LANES), table, table),
            (counts, states[0], states[1], grads[0], grads[1], row_logs, *total),
            [pltpu.VMEM((ROWS, 2 * HALF), bf16)] + SPREAD * 2 + [pltpu.SemaphoreType.DMA(())],
            far=1,
        )
        states = nexts

    vecs = states
    moments = shifted(moment[0])
    grad_a, part = call(
        "last_first",
        lambda *refs: last_half(0, *refs),
        (cell_half, near(ROWS, LANES)),
        (vecs[0], turned_hi, turned_lo, target, weight, *total),
        [both] + SPREAD,
    )
    grad_b, keep, send = call(
        "last_second",
        lambda *refs: last_body(1, *refs),
        (cell_half, near(16 * PACK, 256), near(16 * PACK, 256)),
        (vecs[1], turned_hi, turned_lo, target, weight, part),
        [pltpu.VMEM((ROWS, LANES), f32), both] + SPREAD,
        room=6,
    )
    new_col_emb, new_col_acc = call(
        "last_update",
        last_update_body,
        (free(WIDTH, 2 * HALF), free(WIDTH, 2 * HALF)),
        (vecs[0], vecs[1], moments, grad_a, grad_b, hi, lo),
    )

    got = swapped(send, 1)
    leaving, staying = call(
        "halves",
        halves_body,
        (near(8 * PACK, 256), near(8 * PACK, 256)),
        (keep, got),
    )
    arrived = swapped(leaving, 16)
    share = call("sum", sum_body, near(8, PACK, 256), (new_col_emb, new_col_acc, staying, arrived), far=2)
    rings = [[along_x * 16 + along_y * 2 + core for along_y in range(8)] for along_x in range(2) for core in range(2)]
    parts = lax.all_to_all(share, "grp", 0, 0, axis_index_groups=rings)

    own_vecs, own_moment = call(
        "shares",
        shares_body,
        (near(SHARE, WIDTH), near(SHARE, WIDTH)),
        (row_emb, row_acc),
        [pltpu.VMEM((2, WIDTH, 128), f32), pltpu.VMEM((LANES, 128), f32), pltpu.VMEM((128, LANES), f32), pltpu.SemaphoreType.DMA((2,))],
        far=2,
    )
    new_rows, new_row_moment = call(
        "finish",
        finish_body,
        (free(SHARE, WIDTH), free(SHARE, WIDTH)),
        (parts, own_vecs, own_moment),
        [pltpu.VMEM((SHARE, LANES), f32)],
    )
    return (new_rows.T, new_row_moment.T, new_col_emb, new_col_acc)


def solution(mesh):
    return jax.shard_map(
        shards,
        mesh=mesh,
        in_specs=(
            P(None, "blk", "grp"),
            P("blk"),
            P(("blk", "grp")),
            P(None, "blk"),
            P(None, "blk"),
            P(None, ("blk", "grp")),
            P(None, ("blk", "grp")),
        ),
        out_specs=(
            P(None, ("blk", "grp")),
            P(None, ("blk", "grp")),
            P(None, ("blk", "grp")),
            P(None, ("blk", "grp")),
        ),
        check_vma=False,
    )
```

time: 337 us -> 115 us (0.34)
  the two profiles are of different devices: /device:TPU:2 before, /device:TPU:6 now
where the time goes in v1:
time: 115 us; the launch traced here: 114 us
  waiting for transfers between devices  51.7 us (45%)
  starting transfers between devices  37.8 us (33%)
  Pallas kernels  22.4 us (19%)
  local copies, waits for them, and re-layouts  1.36 us (1%)
    ppermute x7, waiting for transfers between devices, shifted(): lax.ppermute(value, 'blk', [(source, (source + 1) % count) for source in...  38.1 us
    ppermute x7, starting transfers between devices, shifted(): lax.ppermute(value, 'blk', [(source, (source + 1) % count) for source in...  26 us
    pallas_call x17, Pallas kernels, call(): pl.pallas_call(body, out_shape=out, in_specs=specs, out_specs=jax.tree.ma...  22.4 us
    all_to_all x1, waiting for transfers between devices, shards(): parts = lax.all_to_all(share, 'grp', 0, 0, axis_index_groups=rings)  11.5 us
    all_to_all x1, starting transfers between devices, shards(): parts = lax.all_to_all(share, 'grp', 0, 0, axis_index_groups=rings)  7.09 us
    ppermute x2, starting transfers between devices, swapped(): lax.ppermute(value, 'grp', [(source, source ^ bit) for source in range(co...  4.66 us
  transfers between devices with their start and end apart: 10, of which 7 were waited for; matrix products, arithmetic and copies ran while one was open for 0% of the time, Pallas kernels for 14%

profile of v1, /device:TPU:6, one launch (start us, length us, event | category | flops | bytes accessed | tf_op | source)
XLA Modules:
  0.0 114.0 jit_solution(4129332412914814535)
XLA Ops:
  2.0 2.5 %prep.1 = (bf16[300,1024]{1,0:T(8,128)(2,1)S(1)}, bf16[300,1024]{1,0:T(8,128)(2,1)S(1)}, bf16[1024,384]{1,0:T(8,128)(2,1)S(1)}, bf16[1024,384]{1,0:T(8,128)(2,1)...) custom-call(f32[300,1024]{1,0:T(8,128)} %row_hbm.3, ...), custom_call_target="tpu_custom_call" | custom-call | flops 1048576 | bytes 1024 | tf_op jit(solution)/shard_map/prep/pallas_call | solution.py:40
  5.6 5.1 %collective-permute-start = (f32[608,128]{1,0:T(8,128)S(1)}, f32[608,128]{1,0:T(8,128)S(1)}, u32[]{:S(2)}, u32[]{:S(2)}) collective-permute-start(f32[608,128]{1,0:T(8,128)S(1)} %get-tuple-element.56), channel_id=1, source_target_pairs={{0,32},{32,64},{64,96},{96,128},{128,160},{160,192},{192,224},{224... | collective-permute-start | bytes 933896 | tf_op jit(solution)/shard_map/ppermute | solution.py:277
  11.8 4.0 %collective-permute-start.2 = (f32[608,128]{1,0:T(8,128)S(1)}, f32[608,128]{1,0:T(8,128)S(1)}, u32[]{:S(2)}, u32[]{:S(2)}) collective-permute-start(f32[608,128]{1,0:T(8,128)S(1)} %get-tuple-element.64), channel_id=1, source_target_pairs={{0,32},{32,64},{64,96},{96,128},{128,160},{160,192},{192,224},{224... | collective-permute-start | bytes 933896 | tf_op jit(solution)/shard_map/ppermute | solution.py:277
  15.8 2.7 %beside.3 = (f32[1024,384]{1,0:T(8,128)S(1)}, f32[1024,256]{1,0:T(8,128)S(1)}, f32[1024,256]{1,0:T(8,128)S(1)}) custom-call(bf16[4,1024,256]{2,1,0:T(8,128)(2,1)} %refs_0_.5, f32[608,128]{1,0:T(8,128)S(1)} %get-tuple-element.49.refs_0_.refs_1_, f32[608,128]{1,0:T(8,128)S(1)} %get-tuple-element.57.refs_0_.refs_2_, ...), custom_call_target="tpu_custom_call" | custom-call | flops 1048576 | bytes 1024 | tf_op jit(solution)/shard_map/beside/pallas_call | solution.py:40
  19.8 6.5 %collective-permute-start.1 = (f32[608,128]{1,0:T(8,128)S(1)}, f32[608,128]{1,0:T(8,128)S(1)}, u32[]{:S(2)}, u32[]{:S(2)}) collective-permute-start(f32[608,128]{1,0:T(8,128)S(1)} %get-tuple-element.63), channel_id=1, source_target_pairs={{0,32},{32,64},{64,96},{96,128},{128,160},{160,192},{192,224},{224... | collective-permute-start | bytes 933896 | tf_op jit(solution)/shard_map/ppermute | solution.py:277
  27.4 4.4 %collective-permute-start.4 = (f32[608,128]{1,0:T(8,128)S(1)}, f32[608,128]{1,0:T(8,128)S(1)}, u32[]{:S(2)}, u32[]{:S(2)}) collective-permute-start(f32[608,128]{1,0:T(8,128)S(1)} %get-tuple-element.71), channel_id=1, source_target_pairs={{0,32},{32,64},{64,96},{96,128},{128,160},{160,192},{192,224},{224... | collective-permute-start | bytes 933896 | tf_op jit(solution)/shard_map/ppermute | solution.py:277
  31.9 1.8 %beside.4 = (f32[1024,384]{1,0:T(8,128)S(1)}, f32[1024,256]{1,0:T(8,128)S(1)}, f32[1024,256]{1,0:T(8,128)S(1)}) custom-call(bf16[4,1024,256]{2,1,0:T(8,128)(2,1)} %refs_0_.5, f32[608,128]{1,0:T(8,128)S(1)} %collective-permute-done.refs_0_.refs_1_, f32[608,128]{1,0:T(8,128)S(1)} %collective-permute-done.2.refs_0_.refs_2_, ...), custom_call_target="tpu_custom_call" | custom-call | flops 1048576 | bytes 1024 | tf_op jit(solution)/shard_map/beside/pallas_call | solution.py:40
  33.6 10.3 %collective-permute-done.1.refs_0_.refs_1_ = f32[608,128]{1,0:T(8,128)S(1)} collective-permute-done((f32[608,128]{1,0:T(8,128)S(1)}, f32[608,128]{1,0:T(8,128)S(1)}, u32[]{:S(2)}, u32[]{:S(2)}) %collective-permute-start.1) | collective-permute-done | bytes 311328 | tf_op jit(solution)/shard_map/ppermute | solution.py:277
  45.0 1.9 %collective-permute-start.3 = (f32[304,128]{1,0:T(8,128)S(1)}, f32[304,128]{1,0:T(8,128)S(1)}, u32[]{:S(2)}, u32[]{:S(2)}) collective-permute-start(f32[304,128]{1,0:T(8,128)S(1)} %get-tuple-element.70), channel_id=1, source_target_pairs={{0,32},{32,64},{64,96},{96,128},{128,160},{160,192},{192,224},{224... | collective-permute-start | bytes 466952 | tf_op jit(solution)/shard_map/ppermute | solution.py:277
  46.9 3.7 %collective-permute-done.4.refs_0_.refs_2_ = f32[608,128]{1,0:T(8,128)S(1)} collective-permute-done((f32[608,128]{1,0:T(8,128)S(1)}, f32[608,128]{1,0:T(8,128)S(1)}, u32[]{:S(2)}, u32[]{:S(2)}) %collective-permute-start.4) | collective-permute-done | bytes 311328 | tf_op jit(solution)/shard_map/ppermute | solution.py:277
  51.7 2.1 %collective-permute-start.5 = (f32[304,128]{1,0:T(8,128)S(1)}, f32[304,128]{1,0:T(8,128)S(1)}, u32[]{:S(2)}, u32[]{:S(2)}) collective-permute-start(f32[304,128]{1,0:T(8,128)S(1)} %get-tuple-element.73), channel_id=1, source_target_pairs={{0,32},{32,64},{64,96},{96,128},{128,160},{160,192},{192,224},{224... | collective-permute-start | bytes 466952 | tf_op jit(solution)/shard_map/ppermute | solution.py:277
  53.8 1.8 %beside.5 = (f32[1024,384]{1,0:T(8,128)S(1)}, f32[1024,256]{1,0:T(8,128)S(1)}, f32[1024,256]{1,0:T(8,128)S(1)}) custom-call(bf16[4,1024,256]{2,1,0:T(8,128)(2,1)} %refs_0_.5, f32[608,128]{1,0:T(8,128)S(1)} %collective-permute-done.1.refs_0_.refs_1_, f32[608,128]{1,0:T(8,128)S(1)} %collective-permute-done.4.refs_0_.refs_2_, ...), custom_call_target="tpu_custom_call" | custom-call | flops 1048576 | bytes 1024 | tf_op jit(solution)/shard_map/beside/pallas_call | solution.py:40
  55.6 1.2 %last_first.1 = (bf16[1024,256]{1,0:T(8,128)(2,1)S(1)}, f32[1024,384]{1,0:T(8,128)S(1)}) custom-call(f32[304,128]{1,0:T(8,128)S(1)} %collective-permute-done.3.refs_0_.vecs_a_ref, bf16[1024,384]{1,0:T(8,128)(2,1)S(1)} %get-tuple-element.50.refs_1_, bf16[1024,384]{1,0:T(8,128)(2,1)S(1)} %get-tuple-element.51.refs_2_, ...), custom_call_target="tpu_custom_call" | custom-call | flops 1048576 | bytes 1024 | tf_op jit(solution)/shard_map/last_first/pallas_call | solution.py:40
  56.8 5.3 %collective-permute-done.5.refs_0_.vecs_b_ref = f32[304,128]{1,0:T(8,128)S(1)} collective-permute-done((f32[304,128]{1,0:T(8,128)S(1)}, f32[304,128]{1,0:T(8,128)S(1)}, u32[]{:S(2)}, u32[]{:S(2)}) %collective-permute-start.5) | collective-permute-done | bytes 155680 | tf_op jit(solution)/shard_map/ppermute | solution.py:277
  62.1 1.5 %last_second.1 = (bf16[1024,256]{1,0:T(8,128)(2,1)S(1)}, f32[640,256]{1,0:T(8,128)S(1)}, f32[640,256]{1,0:T(8,128)S(1)}) custom-call(f32[304,128]{1,0:T(8,128)S(1)} %collective-permute-done.5.refs_0_.vecs_b_ref, bf16[1024,384]{1,0:T(8,128)(2,1)S(1)} %get-tuple-element.50.refs_1_, bf16[1024,384]{1,0:T(8,128)(2,1)S(1)} %get-tuple-element.51.refs_2_, ...), custom_call_target="tpu_custom_call" | custom-call | flops 1048576 | bytes 1024 | tf_op jit(solution)/shard_map/last_second/pallas_call | solution.py:40
  63.6 1.9 %collective-permute-start.7 = (f32[640,256]{1,0:T(8,128)S(1)}, f32[640,256]{1,0:T(8,128)S(1)}, u32[]{:S(2)}, u32[]{:S(2)}) collective-permute-start(f32[640,256]{1,0:T(8,128)S(1)} %get-tuple-element.87), channel_id=1, source_target_pairs={{0,1},{1,0},{2,3},{3,2},{4,5},{5,4},{6,7},{7,6},{8,9},{9,8},{10,11... | collective-permute-start | bytes 1966088 | tf_op jit(solution)/shard_map/ppermute | solution.py:282
  65.5 2.1 %collective-permute-done.7.got_ref = f32[640,256]{1,0:T(8,128)S(1)} collective-permute-done((f32[640,256]{1,0:T(8,128)S(1)}, f32[640,256]{1,0:T(8,128)S(1)}, u32[]{:S(2)}, u32[]{:S(2)}) %collective-permute-start.7) | collective-permute-done | bytes 655392 | tf_op jit(solution)/shard_map/ppermute | solution.py:282
  67.7 2.7 %collective-permute-start.8 = (f32[320,256]{1,0:T(8,128)S(1)}, f32[320,256]{1,0:T(8,128)S(1)}, u32[]{:S(2)}, u32[]{:S(2)}) collective-permute-start(f32[320,256]{1,0:T(8,128)S(1)} %get-tuple-element.89), channel_id=1, source_target_pairs={{0,16},{1,17},{2,18},{3,19},{4,20},{5,21},{6,22},{7,23},{8,24},{9,... | collective-permute-start | bytes 983048 | tf_op jit(solution)/shard_map/ppermute | solution.py:282
  70.4 1.9 %collective-permute-start.6 = (f32[608,128]{1,0:T(8,128)S(1)}, f32[608,128]{1,0:T(8,128)S(1)}, u32[]{:S(2)}, u32[]{:S(2)}) collective-permute-start(f32[608,128]{1,0:T(8,128)S(1)} %get-tuple-element.74), channel_id=1, source_target_pairs={{0,32},{32,64},{64,96},{96,128},{128,160},{160,192},{192,224},{224... | collective-permute-start | bytes 933896 | tf_op jit(solution)/shard_map/ppermute | solution.py:277
  72.3 18.7 %collective-permute-done.6.moments_ref = f32[608,128]{1,0:T(8,128)S(1)} collective-permute-done((f32[608,128]{1,0:T(8,128)S(1)}, f32[608,128]{1,0:T(8,128)S(1)}, u32[]{:S(2)}, u32[]{:S(2)}) %collective-permute-start.6) | collective-permute-done | bytes 311328 | tf_op jit(solution)/shard_map/ppermute | solution.py:277
  91.0 1.7 %last_update.1 = (f32[300,256]{1,0:T(8,128)}, f32[300,256]{1,0:T(8,128)}) custom-call(f32[304,128]{1,0:T(8,128)S(1)} %collective-permute-done.3.refs_0_.vecs_a_ref, f32[304,128]{1,0:T(8,128)S(1)} %collective-permute-done.5.refs_0_.vecs_b_ref, f32[608,128]{1,0:T(8,128)S(1)} %collective-permute-done.6.moments_ref, ...), custom_call_target="tpu_custom_call" | custom-call | flops 1048576 | bytes 1024 | tf_op jit(solution)/shard_map/last_update/pallas_call | solution.py:40
  93.5 7.1 %all-to-all-start = ((f32[8,40,256]{2,1,0:T(8,128)}), f32[8,40,256]{2,1,0:T(8,128)S(1)}, u32[]{:S(2)}, u32[]{:S(2)}) async-start(f32[8,40,256]{2,1,0:T(8,128)} %sum.1), calls=%async_computation | async-start | bytes 655360 | tf_op jit(solution)/shard_map/all_to_all | solution.py:371
  100.6 1.2 %shares.1 = (f32[32,300]{1,0:T(8,128)S(1)}, f32[32,300]{1,0:T(8,128)S(1)}) custom-call(f32[300,1024]{1,0:T(8,128)} %row_hbm.3, f32[300,1024]{1,0:T(8,128)} %acc_hbm.1), custom_call_target="tpu_custom_call" | custom-call | flops 1048576 | bytes 1024 | tf_op jit(solution)/shard_map/shares/pallas_call | solution.py:40
  101.8 11.5 %all-to-all-done.parts_ref = f32[8,40,256]{2,1,0:T(8,128)S(1)} async-done(((f32[8,40,256]{2,1,0:T(8,128)}), f32[8,40,256]{2,1,0:T(8,128)S(1)}, u32[]{:S(2)}, u32[]{:S(2)}) %all-to-all-start) | async-done | bytes 327712 | tf_op jit(solution)/shard_map/all_to_all | solution.py:371
  (17 shorter events, 9.7 us)
Async XLA Ops:
  0.6 0.7 copy-start
  1.3 0.7 copy-start.1
  5.6 13.2 %collective-permute-start = (f32[608,128]{1,0:T(8,128)S(1)}, f32[608,128]{1,0:T(8,128)S(1)}, u32[]{:S(2)}, u32[]{:S(2)}) collective-permute-start(f32[608,128]{1,0:T(8,128)S(1)} %get-tuple-element.56), channel_id=1, source_target_pairs={{0,32},{32,64},{64,96},{96,128},{128,160},{160,192},{192,224},{224... | collective-permute-start | bytes 933896 | tf_op jit(solution)/shard_map/ppermute | solution.py:277
  11.8 14.5 %collective-permute-start.2 = (f32[608,128]{1,0:T(8,128)S(1)}, f32[608,128]{1,0:T(8,128)S(1)}, u32[]{:S(2)}, u32[]{:S(2)}) collective-permute-start(f32[608,128]{1,0:T(8,128)S(1)} %get-tuple-element.64), channel_id=1, source_target_pairs={{0,32},{32,64},{64,96},{96,128},{128,160},{160,192},{192,224},{224... | collective-permute-start | bytes 933896 | tf_op jit(solution)/shard_map/ppermute | solution.py:277
  19.8 24.1 %collective-permute-start.1 = (f32[608,128]{1,0:T(8,128)S(1)}, f32[608,128]{1,0:T(8,128)S(1)}, u32[]{:S(2)}, u32[]{:S(2)}) collective-permute-start(f32[608,128]{1,0:T(8,128)S(1)} %get-tuple-element.63), channel_id=1, source_target_pairs={{0,32},{32,64},{64,96},{96,128},{128,160},{160,192},{192,224},{224... | collective-permute-start | bytes 933896 | tf_op jit(solution)/shard_map/ppermute | solution.py:277
  27.4 23.1 %collective-permute-start.4 = (f32[608,128]{1,0:T(8,128)S(1)}, f32[608,128]{1,0:T(8,128)S(1)}, u32[]{:S(2)}, u32[]{:S(2)}) collective-permute-start(f32[608,128]{1,0:T(8,128)S(1)} %get-tuple-element.71), channel_id=1, source_target_pairs={{0,32},{32,64},{64,96},{96,128},{128,160},{160,192},{192,224},{224... | collective-permute-start | bytes 933896 | tf_op jit(solution)/shard_map/ppermute | solution.py:277
  45.0 10.6 %collective-permute-start.3 = (f32[304,128]{1,0:T(8,128)S(1)}, f32[304,128]{1,0:T(8,128)S(1)}, u32[]{:S(2)}, u32[]{:S(2)}) collective-permute-start(f32[304,128]{1,0:T(8,128)S(1)} %get-tuple-element.70), channel_id=1, source_target_pairs={{0,32},{32,64},{64,96},{96,128},{128,160},{160,192},{192,224},{224... | collective-permute-start | bytes 466952 | tf_op jit(solution)/shard_map/ppermute | solution.py:277
  51.7 10.5 %collective-permute-start.5 = (f32[304,128]{1,0:T(8,128)S(1)}, f32[304,128]{1,0:T(8,128)S(1)}, u32[]{:S(2)}, u32[]{:S(2)}) collective-permute-start(f32[304,128]{1,0:T(8,128)S(1)} %get-tuple-element.73), channel_id=1, source_target_pairs={{0,32},{32,64},{64,96},{96,128},{128,160},{160,192},{192,224},{224... | collective-permute-start | bytes 466952 | tf_op jit(solution)/shard_map/ppermute | solution.py:277
  63.6 4.0 %collective-permute-start.7 = (f32[640,256]{1,0:T(8,128)S(1)}, f32[640,256]{1,0:T(8,128)S(1)}, u32[]{:S(2)}, u32[]{:S(2)}) collective-permute-start(f32[640,256]{1,0:T(8,128)S(1)} %get-tuple-element.87), channel_id=1, source_target_pairs={{0,1},{1,0},{2,3},{3,2},{4,5},{5,4},{6,7},{7,6},{8,9},{9,8},{10,11... | collective-permute-start | bytes 1966088 | tf_op jit(solution)/shard_map/ppermute | solution.py:282
  67.7 25.0 %collective-permute-start.8 = (f32[320,256]{1,0:T(8,128)S(1)}, f32[320,256]{1,0:T(8,128)S(1)}, u32[]{:S(2)}, u32[]{:S(2)}) collective-permute-start(f32[320,256]{1,0:T(8,128)S(1)} %get-tuple-element.89), channel_id=1, source_target_pairs={{0,16},{1,17},{2,18},{3,19},{4,20},{5,21},{6,22},{7,23},{8,24},{9,... | collective-permute-start | bytes 983048 | tf_op jit(solution)/shard_map/ppermute | solution.py:282
  70.4 20.6 %collective-permute-start.6 = (f32[608,128]{1,0:T(8,128)S(1)}, f32[608,128]{1,0:T(8,128)S(1)}, u32[]{:S(2)}, u32[]{:S(2)}) collective-permute-start(f32[608,128]{1,0:T(8,128)S(1)} %get-tuple-element.74), channel_id=1, source_target_pairs={{0,32},{32,64},{64,96},{96,128},{128,160},{160,192},{192,224},{224... | collective-permute-start | bytes 933896 | tf_op jit(solution)/shard_map/ppermute | solution.py:277
  93.5 19.9 %all-to-all-start = ((f32[8,40,256]{2,1,0:T(8,128)}), f32[8,40,256]{2,1,0:T(8,128)S(1)}, u32[]{:S(2)}, u32[]{:S(2)}) async-start(f32[8,40,256]{2,1,0:T(8,128)} %sum.1), calls=%async_computation | async-start | bytes 655360 | tf_op jit(solution)/shard_map/all_to_all | solution.py:371

commit v2 on v1

--- a/solution.py
+++ b/solution.py
@@ -74,14 +74,17 @@
 
 
 def prep_body(
-    row_hbm, counts_hbm, vecs_hbm, moment_hbm, row_sums_ref, col_sums_ref,
+    row_hbm, counts_hbm, vecs_hbm, moment_hbm, row_sums_hbm, col_sums_hbm,
     hi_ref, lo_ref, turned_hi_ref, turned_lo_ref, logs_ref, target_ref, weight_ref, left_ref, right_ref,
-    given_ref, row_ref, counts_ref, vecs_ref, moment_ref, done,
+    given_ref, row_ref, counts_ref, vecs_ref, moment_ref, row_sums_ref, col_sums_ref, done,
 ):
+    get_row_sums = fetch(row_sums_hbm, row_sums_ref, done.at[4])
     get_counts = fetch(counts_hbm.at[0], counts_ref, done.at[0])
     get_rows = fetch(row_hbm, given_ref, done.at[1])
     get_vecs = fetch(vecs_hbm, vecs_ref, done.at[2])
     get_moment = fetch(moment_hbm, moment_ref, done.at[3])
+    get_col_sums = fetch(col_sums_hbm, col_sums_ref, done.at[5])
+    get_row_sums.wait()
     logs = log_total - jnp.log(row_sums_ref[...].astype(f32))
     logs_ref[...] = jnp.broadcast_to(logs, (HALF, ROWS)).T
     row_ref[WIDTH:, :] = jnp.zeros((LANES - WIDTH, ROWS), f32)
@@ -98,6 +101,7 @@
         turned_lo_ref[at : at + TILE, :] = low
     get_vecs.wait()
     get_moment.wait()
+    get_col_sums.wait()
     for side, ref in enumerate((left_ref, right_ref)):
         lanes = slice(side * HALF, (side + 1) * HALF)
         ref[0:WIDTH, :] = vecs_ref[:, lanes]
@@ -151,31 +155,21 @@
     return vecs - step_rate * grad / jnp.sqrt(new_moment), new_moment
 
 
-def visit_body(side, apart, state_ref, turned_hi_ref, turned_lo_ref, hi_ref, lo_ref, target_ref, weight_ref, *refs):
-    grad_ref, both_ref = refs[-2:]
-    if not apart:
-        next_ref = refs[0]
-        moment_ref = next_ref.at[PADW:]
-    elif side == 0:
-        next_ref, moment_ref = refs[:2]
-    else:
-        next_ref, pair_ref = refs[1:3]
-        pair_ref[0:PADW, :] = refs[0][...]
-        moment_ref = pair_ref.at[PADW:]
+def visit_body(side, state_ref, turned_hi_ref, turned_lo_ref, hi_ref, lo_ref, target_ref, weight_ref, next_ref, grad_ref, both_ref):
     split_columns(state_ref[0:PADW, :], both_ref)
     cells(state_ref[WIDTH : WIDTH + 1, :], both_ref, turned_hi_ref, turned_lo_ref, target_ref, weight_ref, grad_ref, side)
     grad = col_grads(hi_ref, lo_ref, grad_ref)
     vecs, moment = updated(state_ref[0:WIDTH, :], state_ref[PADW : PADW + WIDTH, :], grad)
     next_ref[0:WIDTH, :] = vecs
     next_ref[WIDTH:PADW, :] = state_ref[WIDTH:PADW, :]
-    moment_ref[0:WIDTH, :] = moment
-    moment_ref[WIDTH:, :] = jnp.zeros((PADW - WIDTH, HALF), f32)
-
-
-def last_update_body(vecs_a_ref, vecs_b_ref, moments_ref, grad_a_ref, grad_b_ref, hi_ref, lo_ref, new_ref, new_moment_ref):
-    for side, (vecs_ref, grad_ref) in enumerate(((vecs_a_ref, grad_a_ref), (vecs_b_ref, grad_b_ref))):
+    next_ref[PADW : PADW + WIDTH, :] = moment
+    next_ref[PADW + WIDTH :, :] = jnp.zeros((PADW - WIDTH, HALF), f32)
+
+
+def last_update_body(state_a_ref, state_b_ref, grad_a_ref, grad_b_ref, hi_ref, lo_ref, new_ref, new_moment_ref):
+    for side, (state_ref, grad_ref) in enumerate(((state_a_ref, grad_a_ref), (state_b_ref, grad_b_ref))):
         grad = col_grads(hi_ref, lo_ref, grad_ref)
-        vecs, moment = updated(vecs_ref[0:WIDTH, :], moments_ref[side * PADW : side * PADW + WIDTH, :], grad)
+        vecs, moment = updated(state_ref[0:WIDTH, :], state_ref[PADW : PADW + WIDTH, :], grad)
         new_ref[:, side * HALF : (side + 1) * HALF] = vecs
         new_moment_ref[:, side * HALF : (side + 1) * HALF] = moment
 
@@ -234,7 +228,8 @@
     left = lax.broadcasted_iota(jnp.int32, (8, 128), 1) < 64
     for ref, half in ((keep_ref, core), (send_ref, 1 - core)):
         for slot in range(16):
-            base = pl.multiple_of(slot * 2 * SHARE + half * SHARE, SHARE)
+            place = (slot & 8) + 2 * (slot & 3) + ((slot >> 2) & 1)
+            base = pl.multiple_of(place * 2 * SHARE + half * SHARE, SHARE)
             block = total_ref[pl.ds(base, SHARE), :]
             ref[slot * PACK : slot * PACK + SHARE, :] = block[:, :256]
             for pair in range(2):
@@ -243,24 +238,24 @@
                 ref[slot * PACK + SHARE : (slot + 1) * PACK, pair * 128 : (pair + 1) * 128] = jnp.where(left, upper, lower)
 
 
-def halves_body(keep_ref, got_ref, leaving_ref, staying_ref):
-    half = 8 * PACK
-    along_x = lax.axis_index("grp") >> 4
-    for ref, at in ((leaving_ref, 1 - along_x), (staying_ref, along_x)):
-        rows = pl.ds(pl.multiple_of(at * half, half), half)
+def quarters_body(keep_ref, got_ref, own_ref, *others):
+    group = lax.axis_index("grp")
+    quarter = 2 * (group >> 4) + ((group >> 1) & 1)
+    size = 4 * PACK
+    for at, ref in enumerate((own_ref, *others)):
+        rows = pl.ds(pl.multiple_of((quarter ^ at) * size, size), size)
         ref[...] = keep_ref[rows, :] + got_ref[rows, :]
 
 
-def sum_body(new_ref, new_moment_ref, left_ref, right_ref, out_ref):
-    for slot in range(8):
-        rows = slice(slot * PACK, (slot + 1) * PACK)
-        out_ref[slot] = left_ref[rows, :] + right_ref[rows, :]
-
-
-def finish_body(parts_ref, vecs_ref, moment_ref, new_ref, new_moment_ref, grad_ref):
-    total = parts_ref[0]
-    for at in range(1, parts_ref.shape[0]):
-        total = total + parts_ref[at]
+def pieces_body(new_ref, new_moment_ref, vecs_ref, acc_ref, own_ref, first_ref, second_ref, third_ref, *outs):
+    high = (lax.axis_index("grp") >> 2) & 3
+    for at, ref in enumerate(outs):
+        rows = pl.ds(pl.multiple_of((high ^ at) * PACK, PACK), PACK)
+        ref[...] = (own_ref[rows, :] + first_ref[rows, :]) + (second_ref[rows, :] + third_ref[rows, :])
+
+
+def finish_body(own_ref, first_ref, second_ref, third_ref, vecs_ref, moment_ref, new_ref, new_moment_ref, grad_ref):
+    total = (own_ref[...] + first_ref[...]) + (second_ref[...] + third_ref[...])
     grad_ref[:, :256] = total[0:SHARE, :]
     for group in range(4):
         rest = total[SHARE:PACK, (group // 2) * 128 : (group // 2 + 1) * 128]
@@ -299,31 +294,27 @@
             pltpu.VMEM((ROWS, 2 * HALF), bf16),
             pltpu.VMEM((WIDTH, 2 * HALF), f32),
             pltpu.VMEM((WIDTH, 2 * HALF), f32),
-            pltpu.SemaphoreType.DMA((4,)),
+            pltpu.VMEM((1, ROWS), jnp.int32),
+            pltpu.VMEM((1, 2 * HALF), jnp.int32),
+            pltpu.SemaphoreType.DMA((6,)),
         ],
-        far=4,
+        far=6,
         room=6,
     )
 
     total = ()
     for turn in range(visits - 1):
         nexts, grads = [], []
-        apart = turn == visits - 2
-        first = ()
         for side in range(2):
-            outs = (near(2 * PADW, HALF),)
-            if apart:
-                outs = (near(PADW, HALF), near((1 + side) * PADW, HALF))
-            after, *moment, grad = call(
+            after, grad = call(
                 "visit",
-                lambda *refs, side=side, apart=apart: visit_body(side, apart, *refs),
-                outs + (cell_half,),
-                (states[side], turned_hi, turned_lo, hi, lo, target, weight, *first),
+                lambda *refs, side=side: visit_body(side, *refs),
+                (near(2 * PADW, HALF), cell_half),
+                (states[side], turned_hi, turned_lo, hi, lo, target, weight),
                 [both],
             )
             grads.append(grad)
             nexts.append(shifted(after))
-            first = moment
         *total, target, weight = call(
             "beside",
             lambda *refs, turn=turn: beside_body(turn, *refs),
@@ -334,20 +325,18 @@
         )
         states = nexts
 
-    vecs = states
-    moments = shifted(moment[0])
     grad_a, part = call(
         "last_first",
         lambda *refs: last_half(0, *refs),
         (cell_half, near(ROWS, LANES)),
-        (vecs[0], turned_hi, turned_lo, target, weight, *total),
+        (states[0], turned_hi, turned_lo, target, weight, *total),
         [both] + SPREAD,
     )
     grad_b, keep, send = call(
         "last_second",
         lambda *refs: last_body(1, *refs),
         (cell_half, near(16 * PACK, 256), near(16 * PACK, 256)),
-        (vecs[1], turned_hi, turned_lo, target, weight, part),
+        (states[1], turned_hi, turned_lo, target, weight, part),
         [pltpu.VMEM((ROWS, LANES), f32), both] + SPREAD,
         room=6,
     )
@@ -355,20 +344,8 @@
         "last_update",
         last_update_body,
         (free(WIDTH, 2 * HALF), free(WIDTH, 2 * HALF)),
-        (vecs[0], vecs[1], moments, grad_a, grad_b, hi, lo),
-    )
-
-    got = swapped(send, 1)
-    leaving, staying = call(
-        "halves",
-        halves_body,
-        (near(8 * PACK, 256), near(8 * PACK, 256)),
-        (keep, got),
-    )
-    arrived = swapped(leaving, 16)
-    share = call("sum", sum_body, near(8, PACK, 256), (new_col_emb, new_col_acc, staying, arrived), far=2)
-    rings = [[along_x * 16 + along_y * 2 + core for along_y in range(8)] for along_x in range(2) for core in range(2)]
-    parts = lax.all_to_all(share, "grp", 0, 0, axis_index_groups=rings)
+        (states[0], states[1], grad_a, grad_b, hi, lo),
+    )
 
     own_vecs, own_moment = call(
         "shares",
@@ -378,11 +355,18 @@
         [pltpu.VMEM((2, WIDTH, 128), f32), pltpu.VMEM((LANES, 128), f32), pltpu.VMEM((128, LANES), f32), pltpu.SemaphoreType.DMA((2,))],
         far=2,
     )
+    got = swapped(send, 1)
+    own, *others = call("quarters", quarters_body, (near(4 * PACK, 256),) * 4, (keep, got))
+    arrived = [swapped(each, bits) for each, bits in zip(others[::-1], (18, 16, 2))]
+    before = (new_col_emb, new_col_acc, own_vecs, own_moment)
+    own, *others = call("pieces", pieces_body, (near(PACK, 256),) * 4, (*before, own, *arrived), far=2)
+    parts = [own] + [swapped(each, bits) for each, bits in zip(others, (4, 8, 12))]
+
     new_rows, new_row_moment = call(
         "finish",
         finish_body,
         (free(SHARE, WIDTH), free(SHARE, WIDTH)),
-        (parts, own_vecs, own_moment),
+        (*parts, own_vecs, own_moment),
         [pltpu.VMEM((SHARE, LANES), f32)],
     )
     return (new_rows.T, new_row_moment.T, new_col_emb, new_col_acc)

time: 115 us -> 107 us (0.930)
  the two profiles are of different devices: /device:TPU:6 before, /device:TPU:8 now
where the time goes in v2:
time: 107 us
  waiting for transfers between devices  44.1 us (41%)
  starting transfers between devices  40.5 us (38%)
  Pallas kernels  21.2 us (20%)
    ppermute x6, waiting for transfers between devices, shifted(): lax.ppermute(value, 'blk', [(source, (source + 1) % count) for source in...  34.3 us
    ppermute x7, starting transfers between devices, swapped(): lax.ppermute(value, 'grp', [(source, source ^ bit) for source in range(co...  23.5 us
    pallas_call x17, Pallas kernels, call(): pl.pallas_call(body, out_shape=out, in_specs=specs, out_specs=jax.tree.ma...  21.2 us
    ppermute x6, starting transfers between devices, shifted(): lax.ppermute(value, 'blk', [(source, (source + 1) % count) for source in...  17 us
    ppermute x7, waiting for transfers between devices, swapped(): lax.ppermute(value, 'grp', [(source, source ^ bit) for source in range(co...  9.77 us
  transfers between devices with their start and end apart: 13, of which 11 were waited for; matrix products, arithmetic and copies ran while one was open for 0% of the time, Pallas kernels for 14%

profile of v2, /device:TPU:8, one launch (start us, length us, event | category | flops | bytes accessed | tf_op | source)
XLA Modules:
  0.0 106.6 jit_solution(7166651498635951263)
XLA Ops:
  0.6 2.5 %prep.1 = (bf16[300,1024]{1,0:T(8,128)(2,1)S(1)}, bf16[300,1024]{1,0:T(8,128)(2,1)S(1)}, bf16[1024,384]{1,0:T(8,128)(2,1)S(1)}, bf16[1024,384]{1,0:T(8,128)(2,1)...) custom-call(f32[300,1024]{1,0:T(8,128)} %row_hbm.3, ...), custom_call_target="tpu_custom_call" | custom-call | flops 1048576 | bytes 1024 | tf_op jit(solution)/shard_map/prep/pallas_call | solution.py:40
  4.2 4.9 %collective-permute-start = (f32[608,128]{1,0:T(8,128)S(1)}, f32[608,128]{1,0:T(8,128)S(1)}, u32[]{:S(2)}, u32[]{:S(2)}) collective-permute-start(f32[608,128]{1,0:T(8,128)S(1)} %get-tuple-element.60), channel_id=1, source_target_pairs={{0,32},{32,64},{64,96},{96,128},{128,160},{160,192},{192,224},{224... | collective-permute-start | bytes 933896 | tf_op jit(solution)/shard_map/ppermute | solution.py:272
  10.2 4.2 %collective-permute-start.2 = (f32[608,128]{1,0:T(8,128)S(1)}, f32[608,128]{1,0:T(8,128)S(1)}, u32[]{:S(2)}, u32[]{:S(2)}) collective-permute-start(f32[608,128]{1,0:T(8,128)S(1)} %get-tuple-element.68), channel_id=1, source_target_pairs={{0,32},{32,64},{64,96},{96,128},{128,160},{160,192},{192,224},{224... | collective-permute-start | bytes 933896 | tf_op jit(solution)/shard_map/ppermute | solution.py:272
  14.4 2.7 %beside.3 = (f32[1024,384]{1,0:T(8,128)S(1)}, f32[1024,256]{1,0:T(8,128)S(1)}, f32[1024,256]{1,0:T(8,128)S(1)}) custom-call(bf16[4,1024,256]{2,1,0:T(8,128)(2,1)} %refs_0_.5, f32[608,128]{1,0:T(8,128)S(1)} %get-tuple-element.53.refs_0_.refs_1_, f32[608,128]{1,0:T(8,128)S(1)} %get-tuple-element.61.refs_0_.refs_2_, ...), custom_call_target="tpu_custom_call" | custom-call | flops 1048576 | bytes 1024 | tf_op jit(solution)/shard_map/beside/pallas_call | solution.py:40
  17.1 16.0 %collective-permute-done.refs_0_.refs_1_ = f32[608,128]{1,0:T(8,128)S(1)} collective-permute-done((f32[608,128]{1,0:T(8,128)S(1)}, f32[608,128]{1,0:T(8,128)S(1)}, u32[]{:S(2)}, u32[]{:S(2)}) %collective-permute-start) | collective-permute-done | bytes 311328 | tf_op jit(solution)/shard_map/ppermute | solution.py:272
  34.1 1.9 %collective-permute-start.1 = (f32[608,128]{1,0:T(8,128)S(1)}, f32[608,128]{1,0:T(8,128)S(1)}, u32[]{:S(2)}, u32[]{:S(2)}) collective-permute-start(f32[608,128]{1,0:T(8,128)S(1)} %get-tuple-element.67), channel_id=1, source_target_pairs={{0,32},{32,64},{64,96},{96,128},{128,160},{160,192},{192,224},{224... | collective-permute-start | bytes 933896 | tf_op jit(solution)/shard_map/ppermute | solution.py:272
  36.0 2.9 %collective-permute-done.2.refs_0_.refs_2_ = f32[608,128]{1,0:T(8,128)S(1)} collective-permute-done((f32[608,128]{1,0:T(8,128)S(1)}, f32[608,128]{1,0:T(8,128)S(1)}, u32[]{:S(2)}, u32[]{:S(2)}) %collective-permute-start.2) | collective-permute-done | bytes 311328 | tf_op jit(solution)/shard_map/ppermute | solution.py:272
  39.9 1.9 %collective-permute-start.4 = (f32[608,128]{1,0:T(8,128)S(1)}, f32[608,128]{1,0:T(8,128)S(1)}, u32[]{:S(2)}, u32[]{:S(2)}) collective-permute-start(f32[608,128]{1,0:T(8,128)S(1)} %get-tuple-element.75), channel_id=1, source_target_pairs={{0,32},{32,64},{64,96},{96,128},{128,160},{160,192},{192,224},{224... | collective-permute-start | bytes 933896 | tf_op jit(solution)/shard_map/ppermute | solution.py:272
  43.6 3.7 %collective-permute-done.1.refs_0_.refs_1_ = f32[608,128]{1,0:T(8,128)S(1)} collective-permute-done((f32[608,128]{1,0:T(8,128)S(1)}, f32[608,128]{1,0:T(8,128)S(1)}, u32[]{:S(2)}, u32[]{:S(2)}) %collective-permute-start.1) | collective-permute-done | bytes 311328 | tf_op jit(solution)/shard_map/ppermute | solution.py:272
  48.4 1.9 %collective-permute-start.3 = (f32[608,128]{1,0:T(8,128)S(1)}, f32[608,128]{1,0:T(8,128)S(1)}, u32[]{:S(2)}, u32[]{:S(2)}) collective-permute-start(f32[608,128]{1,0:T(8,128)S(1)} %get-tuple-element.74), channel_id=1, source_target_pairs={{0,32},{32,64},{64,96},{96,128},{128,160},{160,192},{192,224},{224... | collective-permute-start | bytes 933896 | tf_op jit(solution)/shard_map/ppermute | solution.py:272
  50.3 3.7 %collective-permute-done.4.refs_0_.refs_2_ = f32[608,128]{1,0:T(8,128)S(1)} collective-permute-done((f32[608,128]{1,0:T(8,128)S(1)}, f32[608,128]{1,0:T(8,128)S(1)}, u32[]{:S(2)}, u32[]{:S(2)}) %collective-permute-start.4) | collective-permute-done | bytes 311328 | tf_op jit(solution)/shard_map/ppermute | solution.py:272
  55.0 2.1 %collective-permute-start.5 = (f32[608,128]{1,0:T(8,128)S(1)}, f32[608,128]{1,0:T(8,128)S(1)}, u32[]{:S(2)}, u32[]{:S(2)}) collective-permute-start(f32[608,128]{1,0:T(8,128)S(1)} %get-tuple-element.76), channel_id=1, source_target_pairs={{0,32},{32,64},{64,96},{96,128},{128,160},{160,192},{192,224},{224... | collective-permute-start | bytes 933896 | tf_op jit(solution)/shard_map/ppermute | solution.py:272
  58.9 1.9 %collective-permute-done.3.refs_0_.state_a_ref = f32[608,128]{1,0:T(8,128)S(1)} collective-permute-done((f32[608,128]{1,0:T(8,128)S(1)}, f32[608,128]{1,0:T(8,128)S(1)}, u32[]{:S(2)}, u32[]{:S(2)}) %collective-permute-start.3) | collective-permute-done | bytes 311328 | tf_op jit(solution)/shard_map/ppermute | solution.py:272
  62.0 6.2 %collective-permute-done.5.refs_0_.state_b_ref = f32[608,128]{1,0:T(8,128)S(1)} collective-permute-done((f32[608,128]{1,0:T(8,128)S(1)}, f32[608,128]{1,0:T(8,128)S(1)}, u32[]{:S(2)}, u32[]{:S(2)}) %collective-permute-start.5) | collective-permute-done | bytes 311328 | tf_op jit(solution)/shard_map/ppermute | solution.py:272
  69.6 1.9 %collective-permute-start.6 = (f32[640,256]{1,0:T(8,128)S(1)}, f32[640,256]{1,0:T(8,128)S(1)}, u32[]{:S(2)}, u32[]{:S(2)}) collective-permute-start(f32[640,256]{1,0:T(8,128)S(1)} %get-tuple-element.91), channel_id=1, source_target_pairs={{0,1},{1,0},{2,3},{3,2},{4,5},{5,4},{6,7},{7,6},{8,9},{9,8},{10,11... | collective-permute-start | bytes 1966088 | tf_op jit(solution)/shard_map/ppermute | solution.py:277
  71.5 2.1 %collective-permute-done.6.got_ref = f32[640,256]{1,0:T(8,128)S(1)} collective-permute-done((f32[640,256]{1,0:T(8,128)S(1)}, f32[640,256]{1,0:T(8,128)S(1)}, u32[]{:S(2)}, u32[]{:S(2)}) %collective-permute-start.6) | collective-permute-done | bytes 655392 | tf_op jit(solution)/shard_map/ppermute | solution.py:277
  73.7 2.4 %collective-permute-start.7 = (f32[160,256]{1,0:T(8,128)S(1)}, f32[160,256]{1,0:T(8,128)S(1)}, u32[]{:S(2)}, u32[]{:S(2)}) collective-permute-start(f32[160,256]{1,0:T(8,128)S(1)} %get-tuple-element.93), channel_id=1, source_target_pairs={{0,18},{1,19},{2,16},{3,17},{4,22},{5,23},{6,20},{7,21},{8,26},{9,... | collective-permute-start | bytes 491528 | tf_op jit(solution)/shard_map/ppermute | solution.py:277
  76.0 3.3 %collective-permute-start.8 = (f32[160,256]{1,0:T(8,128)S(1)}, f32[160,256]{1,0:T(8,128)S(1)}, u32[]{:S(2)}, u32[]{:S(2)}) collective-permute-start(f32[160,256]{1,0:T(8,128)S(1)} %get-tuple-element.94), channel_id=1, source_target_pairs={{0,16},{1,17},{2,18},{3,19},{4,20},{5,21},{6,22},{7,23},{8,24},{9,... | collective-permute-start | bytes 491528 | tf_op jit(solution)/shard_map/ppermute | solution.py:277
  79.4 3.5 %collective-permute-start.9 = (f32[160,256]{1,0:T(8,128)S(1)}, f32[160,256]{1,0:T(8,128)S(1)}, u32[]{:S(2)}, u32[]{:S(2)}) collective-permute-start(f32[160,256]{1,0:T(8,128)S(1)} %get-tuple-element.95), channel_id=1, source_target_pairs={{0,2},{1,3},{2,0},{3,1},{4,6},{5,7},{6,4},{7,5},{8,10},{9,11},{10,... | collective-permute-start | bytes 491528 | tf_op jit(solution)/shard_map/ppermute | solution.py:277
  87.0 4.5 %collective-permute-start.10 = (f32[40,256]{1,0:T(8,128)S(1)}, f32[40,256]{1,0:T(8,128)S(1)}, u32[]{:S(2)}, u32[]{:S(2)}) collective-permute-start(f32[40,256]{1,0:T(8,128)S(1)} %get-tuple-element.97), channel_id=1, source_target_pairs={{0,4},{1,5},{2,6},{3,7},{4,0},{5,1},{6,2},{7,3},{8,12},{9,13},{10,... | collective-permute-start | bytes 122888 | tf_op jit(solution)/shard_map/ppermute | solution.py:277
  91.5 5.9 %collective-permute-start.11 = (f32[40,256]{1,0:T(8,128)S(1)}, f32[40,256]{1,0:T(8,128)S(1)}, u32[]{:S(2)}, u32[]{:S(2)}) collective-permute-start(f32[40,256]{1,0:T(8,128)S(1)} %get-tuple-element.98), channel_id=1, source_target_pairs={{0,8},{1,9},{2,10},{3,11},{4,12},{5,13},{6,14},{7,15},{8,0},{9,1},... | collective-permute-start | bytes 122888 | tf_op jit(solution)/shard_map/ppermute | solution.py:277
  97.5 1.9 %collective-permute-start.12 = (f32[40,256]{1,0:T(8,128)S(1)}, f32[40,256]{1,0:T(8,128)S(1)}, u32[]{:S(2)}, u32[]{:S(2)}) collective-permute-start(f32[40,256]{1,0:T(8,128)S(1)} %get-tuple-element.99), channel_id=1, source_target_pairs={{0,12},{1,13},{2,14},{3,15},{4,8},{5,9},{6,10},{7,11},{8,4},{9,5},... | collective-permute-start | bytes 122888 | tf_op jit(solution)/shard_map/ppermute | solution.py:277
  99.4 2.2 %collective-permute-done.11.second_ref = f32[40,256]{1,0:T(8,128)S(1)} collective-permute-done((f32[40,256]{1,0:T(8,128)S(1)}, f32[40,256]{1,0:T(8,128)S(1)}, u32[]{:S(2)}, u32[]{:S(2)}) %collective-permute-start.11) | collective-permute-done | bytes 40992 | tf_op jit(solution)/shard_map/ppermute | solution.py:277
  101.6 4.3 %collective-permute-done.12.third_ref = f32[40,256]{1,0:T(8,128)S(1)} collective-permute-done((f32[40,256]{1,0:T(8,128)S(1)}, f32[40,256]{1,0:T(8,128)S(1)}, u32[]{:S(2)}, u32[]{:S(2)}) %collective-permute-start.12) | collective-permute-done | bytes 40992 | tf_op jit(solution)/shard_map/ppermute | solution.py:277
  (19 shorter events, 17.3 us)
Async XLA Ops:
  4.2 28.9 %collective-permute-start = (f32[608,128]{1,0:T(8,128)S(1)}, f32[608,128]{1,0:T(8,128)S(1)}, u32[]{:S(2)}, u32[]{:S(2)}) collective-permute-start(f32[608,128]{1,0:T(8,128)S(1)} %get-tuple-element.60), channel_id=1, source_target_pairs={{0,32},{32,64},{64,96},{96,128},{128,160},{160,192},{192,224},{224... | collective-permute-start | bytes 933896 | tf_op jit(solution)/shard_map/ppermute | solution.py:272
  10.2 28.7 %collective-permute-start.2 = (f32[608,128]{1,0:T(8,128)S(1)}, f32[608,128]{1,0:T(8,128)S(1)}, u32[]{:S(2)}, u32[]{:S(2)}) collective-permute-start(f32[608,128]{1,0:T(8,128)S(1)} %get-tuple-element.68), channel_id=1, source_target_pairs={{0,32},{32,64},{64,96},{96,128},{128,160},{160,192},{192,224},{224... | collective-permute-start | bytes 933896 | tf_op jit(solution)/shard_map/ppermute | solution.py:272
  34.1 13.2 %collective-permute-start.1 = (f32[608,128]{1,0:T(8,128)S(1)}, f32[608,128]{1,0:T(8,128)S(1)}, u32[]{:S(2)}, u32[]{:S(2)}) collective-permute-start(f32[608,128]{1,0:T(8,128)S(1)} %get-tuple-element.67), channel_id=1, source_target_pairs={{0,32},{32,64},{64,96},{96,128},{128,160},{160,192},{192,224},{224... | collective-permute-start | bytes 933896 | tf_op jit(solution)/shard_map/ppermute | solution.py:272
  39.9 14.1 %collective-permute-start.4 = (f32[608,128]{1,0:T(8,128)S(1)}, f32[608,128]{1,0:T(8,128)S(1)}, u32[]{:S(2)}, u32[]{:S(2)}) collective-permute-start(f32[608,128]{1,0:T(8,128)S(1)} %get-tuple-element.75), channel_id=1, source_target_pairs={{0,32},{32,64},{64,96},{96,128},{128,160},{160,192},{192,224},{224... | collective-permute-start | bytes 933896 | tf_op jit(solution)/shard_map/ppermute | solution.py:272
  48.4 12.4 %collective-permute-start.3 = (f32[608,128]{1,0:T(8,128)S(1)}, f32[608,128]{1,0:T(8,128)S(1)}, u32[]{:S(2)}, u32[]{:S(2)}) collective-permute-start(f32[608,128]{1,0:T(8,128)S(1)} %get-tuple-element.74), channel_id=1, source_target_pairs={{0,32},{32,64},{64,96},{96,128},{128,160},{160,192},{192,224},{224... | collective-permute-start | bytes 933896 | tf_op jit(solution)/shard_map/ppermute | solution.py:272
  55.0 13.1 %collective-permute-start.5 = (f32[608,128]{1,0:T(8,128)S(1)}, f32[608,128]{1,0:T(8,128)S(1)}, u32[]{:S(2)}, u32[]{:S(2)}) collective-permute-start(f32[608,128]{1,0:T(8,128)S(1)} %get-tuple-element.76), channel_id=1, source_target_pairs={{0,32},{32,64},{64,96},{96,128},{128,160},{160,192},{192,224},{224... | collective-permute-start | bytes 933896 | tf_op jit(solution)/shard_map/ppermute | solution.py:272
  69.6 4.0 %collective-permute-start.6 = (f32[640,256]{1,0:T(8,128)S(1)}, f32[640,256]{1,0:T(8,128)S(1)}, u32[]{:S(2)}, u32[]{:S(2)}) collective-permute-start(f32[640,256]{1,0:T(8,128)S(1)} %get-tuple-element.91), channel_id=1, source_target_pairs={{0,1},{1,0},{2,3},{3,2},{4,5},{5,4},{6,7},{7,6},{8,9},{9,8},{10,11... | collective-permute-start | bytes 1966088 | tf_op jit(solution)/shard_map/ppermute | solution.py:277
  73.7 12.1 %collective-permute-start.7 = (f32[160,256]{1,0:T(8,128)S(1)}, f32[160,256]{1,0:T(8,128)S(1)}, u32[]{:S(2)}, u32[]{:S(2)}) collective-permute-start(f32[160,256]{1,0:T(8,128)S(1)} %get-tuple-element.93), channel_id=1, source_target_pairs={{0,18},{1,19},{2,16},{3,17},{4,22},{5,23},{6,20},{7,21},{8,26},{9,... | collective-permute-start | bytes 491528 | tf_op jit(solution)/shard_map/ppermute | solution.py:277
  76.0 10.2 %collective-permute-start.8 = (f32[160,256]{1,0:T(8,128)S(1)}, f32[160,256]{1,0:T(8,128)S(1)}, u32[]{:S(2)}, u32[]{:S(2)}) collective-permute-start(f32[160,256]{1,0:T(8,128)S(1)} %get-tuple-element.94), channel_id=1, source_target_pairs={{0,16},{1,17},{2,18},{3,19},{4,20},{5,21},{6,22},{7,23},{8,24},{9,... | collective-permute-start | bytes 491528 | tf_op jit(solution)/shard_map/ppermute | solution.py:277
  79.4 7.6 %collective-permute-start.9 = (f32[160,256]{1,0:T(8,128)S(1)}, f32[160,256]{1,0:T(8,128)S(1)}, u32[]{:S(2)}, u32[]{:S(2)}) collective-permute-start(f32[160,256]{1,0:T(8,128)S(1)} %get-tuple-element.95), channel_id=1, source_target_pairs={{0,2},{1,3},{2,0},{3,1},{4,6},{5,7},{6,4},{7,5},{8,10},{9,11},{10,... | collective-permute-start | bytes 491528 | tf_op jit(solution)/shard_map/ppermute | solution.py:277
  87.0 12.4 %collective-permute-start.10 = (f32[40,256]{1,0:T(8,128)S(1)}, f32[40,256]{1,0:T(8,128)S(1)}, u32[]{:S(2)}, u32[]{:S(2)}) collective-permute-start(f32[40,256]{1,0:T(8,128)S(1)} %get-tuple-element.97), channel_id=1, source_target_pairs={{0,4},{1,5},{2,6},{3,7},{4,0},{5,1},{6,2},{7,3},{8,12},{9,13},{10,... | collective-permute-start | bytes 122888 | tf_op jit(solution)/shard_map/ppermute | solution.py:277
  91.5 10.1 %collective-permute-start.11 = (f32[40,256]{1,0:T(8,128)S(1)}, f32[40,256]{1,0:T(8,128)S(1)}, u32[]{:S(2)}, u32[]{:S(2)}) collective-permute-start(f32[40,256]{1,0:T(8,128)S(1)} %get-tuple-element.98), channel_id=1, source_target_pairs={{0,8},{1,9},{2,10},{3,11},{4,12},{5,13},{6,14},{7,15},{8,0},{9,1},... | collective-permute-start | bytes 122888 | tf_op jit(solution)/shard_map/ppermute | solution.py:277
  97.5 8.4 %collective-permute-start.12 = (f32[40,256]{1,0:T(8,128)S(1)}, f32[40,256]{1,0:T(8,128)S(1)}, u32[]{:S(2)}, u32[]{:S(2)}) collective-permute-start(f32[40,256]{1,0:T(8,128)S(1)} %get-tuple-element.99), channel_id=1, source_target_pairs={{0,12},{1,13},{2,14},{3,15},{4,8},{5,9},{6,10},{7,11},{8,4},{9,5},... | collective-permute-start | bytes 122888 | tf_op jit(solution)/shard_map/ppermute | solution.py:277

commit v3 on v2

--- a/solution.py
+++ b/solution.py
@@ -33,7 +33,7 @@
     return jnp.dot(left, right, preferred_element_type=f32)
 
 
-def call(name, body, out, operands, scratch=(), far=0, room=4):
+def call(name, body, out, operands, scratch=(), far=0, room=4, flops=1 << 32):
     specs = [FAR] * far + [VM] * (len(operands) - far)
     spaces = [pltpu.HBM] * far + [pltpu.VMEM] * (len(operands) - far)
     placed = [pltpu.with_memory_space_constraint(each, space) for each, space in zip(operands, spaces)]
@@ -44,7 +44,7 @@
         out_specs=jax.tree.map(lambda _: VM, out),
         scratch_shapes=list(scratch),
         compiler_params=pltpu.CompilerParams(vmem_limit_bytes=room * 1024 * 1024),
-        cost_estimate=pl.CostEstimate(flops=1 << 20, bytes_accessed=1 << 10, transcendentals=0),
+        cost_estimate=pl.CostEstimate(flops=flops, bytes_accessed=1 << 10, transcendentals=0),
         name=name,
     )(*placed)
 
@@ -155,21 +155,43 @@
     return vecs - step_rate * grad / jnp.sqrt(new_moment), new_moment
 
 
-def visit_body(side, state_ref, turned_hi_ref, turned_lo_ref, hi_ref, lo_ref, target_ref, weight_ref, next_ref, grad_ref, both_ref):
+def first_visit_body(side, state_ref, turned_hi_ref, turned_lo_ref, hi_ref, lo_ref, target_ref, weight_ref, vecs_ref, moment_ref, grad_ref, both_ref):
     split_columns(state_ref[0:PADW, :], both_ref)
     cells(state_ref[WIDTH : WIDTH + 1, :], both_ref, turned_hi_ref, turned_lo_ref, target_ref, weight_ref, grad_ref, side)
     grad = col_grads(hi_ref, lo_ref, grad_ref)
     vecs, moment = updated(state_ref[0:WIDTH, :], state_ref[PADW : PADW + WIDTH, :], grad)
-    next_ref[0:WIDTH, :] = vecs
-    next_ref[WIDTH:PADW, :] = state_ref[WIDTH:PADW, :]
-    next_ref[PADW : PADW + WIDTH, :] = moment
-    next_ref[PADW + WIDTH :, :] = jnp.zeros((PADW - WIDTH, HALF), f32)
-
-
-def last_update_body(state_a_ref, state_b_ref, grad_a_ref, grad_b_ref, hi_ref, lo_ref, new_ref, new_moment_ref):
-    for side, (state_ref, grad_ref) in enumerate(((state_a_ref, grad_a_ref), (state_b_ref, grad_b_ref))):
+    vecs_ref[0:WIDTH, :] = vecs
+    vecs_ref[WIDTH:, :] = state_ref[WIDTH:PADW, :]
+    moment_ref[0:WIDTH, :] = moment
+    moment_ref[WIDTH:, :] = jnp.zeros((PADW - WIDTH, HALF), f32)
+
+
+def second_visit_body(side, vecs_ref, turned_hi_ref, turned_lo_ref, hi_ref, lo_ref, target_ref, weight_ref, out_ref, grad_ref, both_ref):
+    split_columns(vecs_ref[...], both_ref)
+    cells(vecs_ref[WIDTH : WIDTH + 1, :], both_ref, turned_hi_ref, turned_lo_ref, target_ref, weight_ref, grad_ref, side)
+    out_ref[0:WIDTH, :] = col_grads(hi_ref, lo_ref, grad_ref)
+    out_ref[WIDTH:, :] = jnp.zeros((PADW - WIDTH, HALF), f32)
+
+
+def third_visit_body(side, whole_ref, sent_ref, turned_hi_ref, turned_lo_ref, hi_ref, lo_ref, target_ref, weight_ref, *refs):
+    now_ref, vecs_ref, moment_ref, grad_ref, both_ref = refs
+    at = side * 2 * PADW
+    vecs, moment = updated(whole_ref[at : at + WIDTH, :], whole_ref[at + PADW : at + PADW + WIDTH, :], sent_ref[0:WIDTH, :])
+    now_ref[0:WIDTH, :] = vecs
+    now_ref[WIDTH:, :] = whole_ref[at + WIDTH : at + PADW, :]
+    split_columns(now_ref[...], both_ref)
+    cells(now_ref[WIDTH : WIDTH + 1, :], both_ref, turned_hi_ref, turned_lo_ref, target_ref, weight_ref, grad_ref, side)
+    vecs, moment = updated(now_ref[0:WIDTH, :], moment, col_grads(hi_ref, lo_ref, grad_ref))
+    vecs_ref[0:WIDTH, :] = vecs
+    vecs_ref[WIDTH:, :] = now_ref[WIDTH:, :]
+    moment_ref[0:WIDTH, :] = moment
+    moment_ref[WIDTH:, :] = jnp.zeros((PADW - WIDTH, HALF), f32)
+
+
+def last_update_body(vecs_a_ref, vecs_b_ref, moments_ref, grad_a_ref, grad_b_ref, hi_ref, lo_ref, new_ref, new_moment_ref):
+    for side, (vecs_ref, grad_ref) in enumerate(((vecs_a_ref, grad_a_ref), (vecs_b_ref, grad_b_ref))):
         grad = col_grads(hi_ref, lo_ref, grad_ref)
-        vecs, moment = updated(state_ref[0:WIDTH, :], state_ref[PADW : PADW + WIDTH, :], grad)
+        vecs, moment = updated(vecs_ref[0:WIDTH, :], moments_ref[side * PADW : side * PADW + WIDTH, :], grad)
         new_ref[:, side * HALF : (side + 1) * HALF] = vecs
         new_moment_ref[:, side * HALF : (side + 1) * HALF] = moment
 
@@ -197,12 +219,13 @@
 SPREAD = [pltpu.VMEM((LANES, 2 * HALF), bf16), pltpu.VMEM((LANES, HALF), bf16)]
 
 
-def beside_body(
-    turn, counts_hbm, vecs_a_ref, vecs_b_ref, grad_a_ref, grad_b_ref, logs_ref, *refs
-):
-    before_ref = refs[0] if turn else None
-    total_ref, target_ref, weight_ref, counts_ref, high_a_ref, low_a_ref, high_b_ref, low_b_ref, done = refs[1 if turn else 0 :]
+def beside_body(turn, packs, counts_hbm, vecs_a_ref, vecs_b_ref, grad_a_ref, grad_b_ref, logs_ref, *refs):
+    before_ref = refs[packs] if turn else None
+    packed_ref = refs[-10] if packs else None
+    total_ref, target_ref, weight_ref, counts_ref, high_a_ref, low_a_ref, high_b_ref, low_b_ref, done = refs[-9:]
     get_counts = fetch(counts_hbm.at[turn + 1], counts_ref, done)
+    for at in range(packs):
+        packed_ref[at * PADW : (at + 1) * PADW, :] = refs[at][...]
     spread(vecs_a_ref, high_a_ref, low_a_ref)
     spread(vecs_b_ref, high_b_ref, low_b_ref)
     for at in range(0, ROWS, TILE):
@@ -228,8 +251,7 @@
     left = lax.broadcasted_iota(jnp.int32, (8, 128), 1) < 64
     for ref, half in ((keep_ref, core), (send_ref, 1 - core)):
         for slot in range(16):
-            place = (slot & 8) + 2 * (slot & 3) + ((slot >> 2) & 1)
-            base = pl.multiple_of(place * 2 * SHARE + half * SHARE, SHARE)
+            base = pl.multiple_of(slot * 2 * SHARE + half * SHARE, SHARE)
             block = total_ref[pl.ds(base, SHARE), :]
             ref[slot * PACK : slot * PACK + SHARE, :] = block[:, :256]
             for pair in range(2):
@@ -238,24 +260,16 @@
                 ref[slot * PACK + SHARE : (slot + 1) * PACK, pair * 128 : (pair + 1) * 128] = jnp.where(left, upper, lower)
 
 
-def quarters_body(keep_ref, got_ref, own_ref, *others):
-    group = lax.axis_index("grp")
-    quarter = 2 * (group >> 4) + ((group >> 1) & 1)
-    size = 4 * PACK
-    for at, ref in enumerate((own_ref, *others)):
-        rows = pl.ds(pl.multiple_of((quarter ^ at) * size, size), size)
-        ref[...] = keep_ref[rows, :] + got_ref[rows, :]
-
-
-def pieces_body(new_ref, new_moment_ref, vecs_ref, acc_ref, own_ref, first_ref, second_ref, third_ref, *outs):
-    high = (lax.axis_index("grp") >> 2) & 3
-    for at, ref in enumerate(outs):
-        rows = pl.ds(pl.multiple_of((high ^ at) * PACK, PACK), PACK)
-        ref[...] = (own_ref[rows, :] + first_ref[rows, :]) + (second_ref[rows, :] + third_ref[rows, :])
-
-
-def finish_body(own_ref, first_ref, second_ref, third_ref, vecs_ref, moment_ref, new_ref, new_moment_ref, grad_ref):
-    total = (own_ref[...] + first_ref[...]) + (second_ref[...] + third_ref[...])
+def sum_body(new_ref, new_moment_ref, keep_ref, got_ref, out_ref):
+    for slot in range(16):
+        rows = slice(slot * PACK, (slot + 1) * PACK)
+        out_ref[slot] = keep_ref[rows, :] + got_ref[rows, :]
+
+
+def finish_body(parts_ref, vecs_ref, moment_ref, new_ref, new_moment_ref, grad_ref):
+    total = parts_ref[0]
+    for at in range(1, parts_ref.shape[0]):
+        total = total + parts_ref[at]
     grad_ref[:, :256] = total[0:SHARE, :]
     for group in range(4):
         rest = total[SHARE:PACK, (group // 2) * 128 : (group // 2 + 1) * 128]
@@ -267,9 +281,9 @@
     new_moment_ref[...] = moment
 
 
-def shifted(value):
+def shifted(value, steps=1):
     count = lax.axis_size("blk")
-    return lax.ppermute(value, "blk", [(source, (source + 1) % count) for source in range(count)])
+    return lax.ppermute(value, "blk", [(source, (source + steps) % count) for source in range(count)])
 
 
 def swapped(value, bit):
@@ -278,7 +292,6 @@
 
 
 def shards(counts, row_sums, col_sums, row_emb, row_acc, col_emb, col_acc):
-    visits = counts.shape[0]
     cell_half = near(ROWS, 2 * HALF, of=bf16)
     table = near(ROWS, 2 * HALF)
     both = pltpu.VMEM((LANES, 2 * HALF), bf16)
@@ -302,41 +315,70 @@
         room=6,
     )
 
-    total = ()
-    for turn in range(visits - 1):
-        nexts, grads = [], []
-        for side in range(2):
-            after, grad = call(
-                "visit",
-                lambda *refs, side=side: visit_body(side, *refs),
-                (near(2 * PADW, HALF), cell_half),
-                (states[side], turned_hi, turned_lo, hi, lo, target, weight),
-                [both],
-            )
-            grads.append(grad)
-            nexts.append(shifted(after))
-        *total, target, weight = call(
+    rows = (turned_hi, turned_lo, hi, lo)
+
+    def beside(turn, vecs, grads, packs, *more):
+        packed = (near(len(packs) * PADW, HALF),) if packs else ()
+        return call(
             "beside",
-            lambda *refs, turn=turn: beside_body(turn, *refs),
-            (near(ROWS, LANES), table, table),
-            (counts, states[0], states[1], grads[0], grads[1], row_logs, *total),
+            lambda *refs: beside_body(turn, len(packs), *refs),
+            (*packed, near(ROWS, LANES), table, table),
+            (counts, *vecs, *grads, row_logs, *packs, *more),
             [pltpu.VMEM((ROWS, 2 * HALF), bf16)] + SPREAD * 2 + [pltpu.SemaphoreType.DMA(())],
             far=1,
         )
-        states = nexts
+
+    near_vecs = near(PADW, HALF)
+    vecs, moments, grads = [None] * 2, [None] * 2, [None] * 2
+    for side in range(2):
+        vecs[side], moments[side], grads[side] = call(
+            "first_visit",
+            lambda *refs, side=side: first_visit_body(side, *refs),
+            (near_vecs, near_vecs, cell_half),
+            (states[side], *rows, target, weight),
+            [both],
+        )
+    whole, total, target, weight = beside(0, states, grads, (vecs[0], moments[0], vecs[1], moments[1]))
+    whole = shifted(whole, 2)
+    vecs = [shifted(each) for each in vecs]
+
+    sent, grads = [None] * 2, [None] * 2
+    for side in range(2):
+        sent[side], grads[side] = call(
+            "second_visit",
+            lambda *refs, side=side: second_visit_body(side, *refs),
+            (near_vecs, cell_half),
+            (vecs[side], *rows, target, weight),
+            [both],
+        )
+        sent[side] = shifted(sent[side])
+    total, target, weight = beside(1, vecs, grads, (), total)
+
+    now, vecs, grads = [None] * 2, [None] * 2, [None] * 2
+    for side in range(2):
+        now[side], vecs[side], moments[side], grads[side] = call(
+            "third_visit",
+            lambda *refs, side=side: third_visit_body(side, *refs),
+            (near_vecs, near_vecs, near_vecs, cell_half),
+            (whole, sent[side], *rows, target, weight),
+            [both],
+        )
+        vecs[side] = shifted(vecs[side])
+    moments, total, target, weight = beside(2, now, grads, moments, total)
+    moments = shifted(moments)
 
     grad_a, part = call(
         "last_first",
         lambda *refs: last_half(0, *refs),
         (cell_half, near(ROWS, LANES)),
-        (states[0], turned_hi, turned_lo, target, weight, *total),
+        (vecs[0], turned_hi, turned_lo, target, weight, total),
         [both] + SPREAD,
     )
     grad_b, keep, send = call(
         "last_second",
         lambda *refs: last_body(1, *refs),
         (cell_half, near(16 * PACK, 256), near(16 * PACK, 256)),
-        (states[1], turned_hi, turned_lo, target, weight, part),
+        (vecs[1], turned_hi, turned_lo, target, weight, part),
         [pltpu.VMEM((ROWS, LANES), f32), both] + SPREAD,
         room=6,
     )
@@ -344,7 +386,8 @@
         "last_update",
         last_update_body,
         (free(WIDTH, 2 * HALF), free(WIDTH, 2 * HALF)),
-        (states[0], states[1], grad_a, grad_b, hi, lo),
+        (vecs[0], vecs[1], moments, grad_a, grad_b, hi, lo),
+        flops=1 << 33,
     )
 
     own_vecs, own_moment = call(
@@ -356,17 +399,15 @@
         far=2,
     )
     got = swapped(send, 1)
-    own, *others = call("quarters", quarters_body, (near(4 * PACK, 256),) * 4, (keep, got))
-    arrived = [swapped(each, bits) for each, bits in zip(others[::-1], (18, 16, 2))]
-    before = (new_col_emb, new_col_acc, own_vecs, own_moment)
-    own, *others = call("pieces", pieces_body, (near(PACK, 256),) * 4, (*before, own, *arrived), far=2)
-    parts = [own] + [swapped(each, bits) for each, bits in zip(others, (4, 8, 12))]
+    share = call("sum", sum_body, near(16, PACK, 256), (new_col_emb, new_col_acc, keep, got), far=2)
+    chips = [[2 * chip + core for chip in range(16)] for core in range(2)]
+    parts = lax.all_to_all(share, "grp", 0, 0, axis_index_groups=chips)
 
     new_rows, new_row_moment = call(
         "finish",
         finish_body,
         (free(SHARE, WIDTH), free(SHARE, WIDTH)),
-        (*parts, own_vecs, own_moment),
+        (parts, own_vecs, own_moment),
         [pltpu.VMEM((SHARE, LANES), f32)],
     )
     return (new_rows.T, new_row_moment.T, new_col_emb, new_col_acc)

time: 107 us -> 100 us (0.935)
  starting transfers between devices: 40.5 us -> 32.7 us
  Pallas kernels: 21.2 us -> 22.6 us
    ppermute x7 -> x1, starting transfers between devices: 23.5 us -> 1.92 us  [swapped(): lax.ppermute(value, 'grp', [(source, source ^ bit) for source in range(co...]
    all_to_all x0 -> x1, waiting for transfers between devices: none -> 14.9 us  [shards(): parts = lax.all_to_all(share, 'grp', 0, 0, axis_index_groups=chips)]
    ppermute x7 -> x1, waiting for transfers between devices: 9.77 us -> 0.01 us  [swapped(): lax.ppermute(value, 'grp', [(source, source ^ bit) for source in range(co...]
    all_to_all x0 -> x1, starting transfers between devices: none -> 7.59 us  [shards(): parts = lax.all_to_all(share, 'grp', 0, 0, axis_index_groups=chips)]
    ppermute x6 -> x8, starting transfers between devices: 17 us -> 23.2 us  [shifted(): lax.ppermute(value, 'blk', [(source, (source + steps) % count) for source...]
    ppermute x6 -> x8, waiting for transfers between devices: 34.3 us -> 28.6 us  [shifted(): lax.ppermute(value, 'blk', [(source, (source + steps) % count) for source...]
    pallas_call x17 -> x16, Pallas kernels: 21.2 us -> 22.6 us  [call(): pl.pallas_call(body, out_shape=out, in_specs=specs, out_specs=jax.tree.ma...]
  transfers between devices with their start and end apart: 13 -> 10, of which waited for: 11 -> 7; matrix products, arithmetic and copies ran while one was open for 0% -> 0% of each run, Pallas kernels for 14% -> 17%
where the time goes in v3:
time: 100 us; the launch traced here: 99.7 us
  waiting for transfers between devices  43.6 us (44%)
  starting transfers between devices  32.7 us (33%)
  Pallas kernels  22.6 us (23%)
    ppermute x8, waiting for transfers between devices, shifted(): lax.ppermute(value, 'blk', [(source, (source + steps) % count) for source...  28.6 us
    ppermute x8, starting transfers between devices, shifted(): lax.ppermute(value, 'blk', [(source, (source + steps) % count) for source...  23.2 us
    pallas_call x16, Pallas kernels, call(): pl.pallas_call(body, out_shape=out, in_specs=specs, out_specs=jax.tree.ma...  22.6 us
    all_to_all x1, waiting for transfers between devices, shards(): parts = lax.all_to_all(share, 'grp', 0, 0, axis_index_groups=chips)  14.9 us
    all_to_all x1, starting transfers between devices, shards(): parts = lax.all_to_all(share, 'grp', 0, 0, axis_index_groups=chips)  7.59 us
  transfers between devices with their start and end apart: 10, of which 7 were waited for; matrix products, arithmetic and copies ran while one was open for 0% of the time, Pallas kernels for 17%

profile of v3, /device:TPU:8, one launch (start us, length us, event | category | flops | bytes accessed | tf_op | source)
XLA Modules:
  0.0 99.7 jit_solution(15037872204462158220)
XLA Ops:
  0.6 2.5 %prep.1 = (bf16[300,1024]{1,0:T(8,128)(2,1)S(1)}, bf16[300,1024]{1,0:T(8,128)(2,1)S(1)}, bf16[1024,384]{1,0:T(8,128)(2,1)S(1)}, bf16[1024,384]{1,0:T(8,128)(2,1)...) custom-call(f32[300,1024]{1,0:T(8,128)} %row_hbm.3, ...), custom_call_target="tpu_custom_call" | custom-call | flops 4294967296 | bytes 1024 | tf_op jit(solution)/shard_map/prep/pallas_call | solution.py:40
  4.2 4.9 %collective-permute-start.1 = (f32[304,128]{1,0:T(8,128)S(1)}, f32[304,128]{1,0:T(8,128)S(1)}, u32[]{:S(2)}, u32[]{:S(2)}) collective-permute-start(f32[304,128]{1,0:T(8,128)S(1)} %get-tuple-element.64.refs_6_), channel_id=1, source_target_pairs={{0,32},{32,64},{64,96},{96,128},{128,160},{160,192},{192,224},{224... | collective-permute-start | bytes 466952 | tf_op jit(solution)/shard_map/ppermute | solution.py:286
  10.2 4.2 %collective-permute-start.3 = (f32[304,128]{1,0:T(8,128)S(1)}, f32[304,128]{1,0:T(8,128)S(1)}, u32[]{:S(2)}, u32[]{:S(2)}) collective-permute-start(f32[304,128]{1,0:T(8,128)S(1)} %get-tuple-element.66.refs_8_), channel_id=1, source_target_pairs={{0,32},{32,64},{64,96},{96,128},{128,160},{160,192},{192,224},{224... | collective-permute-start | bytes 466952 | tf_op jit(solution)/shard_map/ppermute | solution.py:286
  14.5 2.7 %beside.3 = (f32[1216,128]{1,0:T(8,128)S(1)}, f32[1024,384]{1,0:T(8,128)S(1)}, f32[1024,256]{1,0:T(8,128)S(1)}, f32[1024,256]{1,0:T(8,128)S(1)}) custom-call(bf16[4,1024,256]{2,1,0:T(8,128)(2,1)} %refs_0_.5, f32[608,128]{1,0:T(8,128)S(1)} %get-tuple-element.53.refs_0_.refs_1_, f32[608,128]{1,0:T(8,128)S(1)} %get-tuple-element.54.refs_0_.refs_2_, ...), custom_call_target="tpu_custom_call" | custom-call | flops 4294967296 | bytes 1024 | tf_op jit(solution)/shard_map/beside/pallas_call | solution.py:40
  17.2 4.3 %collective-permute-start = (f32[1216,128]{1,0:T(8,128)S(1)}, f32[1216,128]{1,0:T(8,128)S(1)}, u32[]{:S(2)}, u32[]{:S(2)}) collective-permute-start(f32[1216,128]{1,0:T(8,128)S(1)} %get-tuple-element.68), channel_id=1, source_target_pairs={{0,64},{32,96},{64,128},{96,160},{128,192},{160,224},{192,256},{22... | collective-permute-start | bytes 1867784 | tf_op jit(solution)/shard_map/ppermute | solution.py:286
  21.4 7.7 %collective-permute-done.1.refs_0_.refs_1_ = f32[304,128]{1,0:T(8,128)S(1)} collective-permute-done((f32[304,128]{1,0:T(8,128)S(1)}, f32[304,128]{1,0:T(8,128)S(1)}, u32[]{:S(2)}, u32[]{:S(2)}) %collective-permute-start.1) | collective-permute-done | bytes 155680 | tf_op jit(solution)/shard_map/ppermute | solution.py:286
  30.2 1.9 %collective-permute-start.2 = (f32[304,128]{1,0:T(8,128)S(1)}, f32[304,128]{1,0:T(8,128)S(1)}, u32[]{:S(2)}, u32[]{:S(2)}) collective-permute-start(f32[304,128]{1,0:T(8,128)S(1)} %get-tuple-element.71), channel_id=1, source_target_pairs={{0,32},{32,64},{64,96},{96,128},{128,160},{160,192},{192,224},{224... | collective-permute-start | bytes 466952 | tf_op jit(solution)/shard_map/ppermute | solution.py:286
  33.3 1.9 %collective-permute-start.5 = (f32[304,128]{1,0:T(8,128)S(1)}, f32[304,128]{1,0:T(8,128)S(1)}, u32[]{:S(2)}, u32[]{:S(2)}) collective-permute-start(f32[304,128]{1,0:T(8,128)S(1)} %get-tuple-element.78), channel_id=1, source_target_pairs={{0,32},{32,64},{64,96},{96,128},{128,160},{160,192},{192,224},{224... | collective-permute-start | bytes 466952 | tf_op jit(solution)/shard_map/ppermute | solution.py:286
  35.2 1.8 %beside.4 = (f32[1024,384]{1,0:T(8,128)S(1)}, f32[1024,256]{1,0:T(8,128)S(1)}, f32[1024,256]{1,0:T(8,128)S(1)}) custom-call(bf16[4,1024,256]{2,1,0:T(8,128)(2,1)} %refs_0_.5, f32[304,128]{1,0:T(8,128)S(1)} %collective-permute-done.1.refs_0_.refs_1_, f32[304,128]{1,0:T(8,128)S(1)} %collective-permute-done.3.refs_0_.refs_2_, ...), custom_call_target="tpu_custom_call" | custom-call | flops 4294967296 | bytes 1024 | tf_op jit(solution)/shard_map/beside/pallas_call | solution.py:40
  37.0 13.7 %collective-permute-done.2.refs_1_ = f32[304,128]{1,0:T(8,128)S(1)} collective-permute-done((f32[304,128]{1,0:T(8,128)S(1)}, f32[304,128]{1,0:T(8,128)S(1)}, u32[]{:S(2)}, u32[]{:S(2)}) %collective-permute-start.2) | collective-permute-done | bytes 155680 | tf_op jit(solution)/shard_map/ppermute | solution.py:286
  51.9 1.9 %collective-permute-start.4 = (f32[304,128]{1,0:T(8,128)S(1)}, f32[304,128]{1,0:T(8,128)S(1)}, u32[]{:S(2)}, u32[]{:S(2)}) collective-permute-start(f32[304,128]{1,0:T(8,128)S(1)} %get-tuple-element.77), channel_id=1, source_target_pairs={{0,32},{32,64},{64,96},{96,128},{128,160},{160,192},{192,224},{224... | collective-permute-start | bytes 466952 | tf_op jit(solution)/shard_map/ppermute | solution.py:286
  55.0 2.1 %collective-permute-start.6 = (f32[304,128]{1,0:T(8,128)S(1)}, f32[304,128]{1,0:T(8,128)S(1)}, u32[]{:S(2)}, u32[]{:S(2)}) collective-permute-start(f32[304,128]{1,0:T(8,128)S(1)} %get-tuple-element.79), channel_id=1, source_target_pairs={{0,32},{32,64},{64,96},{96,128},{128,160},{160,192},{192,224},{224... | collective-permute-start | bytes 466952 | tf_op jit(solution)/shard_map/ppermute | solution.py:286
  57.1 1.8 %beside.5 = (f32[608,128]{1,0:T(8,128)S(1)}, f32[1024,384]{1,0:T(8,128)S(1)}, f32[1024,256]{1,0:T(8,128)S(1)}, f32[1024,256]{1,0:T(8,128)S(1)}) custom-call(bf16[4,1024,256]{2,1,0:T(8,128)(2,1)} %refs_0_.5, f32[304,128]{1,0:T(8,128)S(1)} %get-tuple-element.80.refs_1_, f32[304,128]{1,0:T(8,128)S(1)} %get-tuple-element.81.refs_2_, ...), custom_call_target="tpu_custom_call" | custom-call | flops 4294967296 | bytes 1024 | tf_op jit(solution)/shard_map/beside/pallas_call | solution.py:40
  58.9 1.9 %collective-permute-start.7 = (f32[608,128]{1,0:T(8,128)S(1)}, f32[608,128]{1,0:T(8,128)S(1)}, u32[]{:S(2)}, u32[]{:S(2)}) collective-permute-start(f32[608,128]{1,0:T(8,128)S(1)} %get-tuple-element.87), channel_id=1, source_target_pairs={{0,32},{32,64},{64,96},{96,128},{128,160},{160,192},{192,224},{224... | collective-permute-start | bytes 933896 | tf_op jit(solution)/shard_map/ppermute | solution.py:286
  60.8 2.7 %collective-permute-done.4.refs_0_.vecs_a_ref = f32[304,128]{1,0:T(8,128)S(1)} collective-permute-done((f32[304,128]{1,0:T(8,128)S(1)}, f32[304,128]{1,0:T(8,128)S(1)}, u32[]{:S(2)}, u32[]{:S(2)}) %collective-permute-start.4) | collective-permute-done | bytes 155680 | tf_op jit(solution)/shard_map/ppermute | solution.py:286
  63.5 1.3 %last_first.1 = (bf16[1024,256]{1,0:T(8,128)(2,1)S(1)}, f32[1024,384]{1,0:T(8,128)S(1)}) custom-call(f32[304,128]{1,0:T(8,128)S(1)} %collective-permute-done.4.refs_0_.vecs_a_ref, bf16[1024,384]{1,0:T(8,128)(2,1)S(1)} %get-tuple-element.55.refs_1_.refs_2_, bf16[1024,384]{1,0:T(8,128)(2,1)S(1)} %get-tuple-element.56.refs_2_.refs_3_, ...), custom_call_target="tpu_custom_call" | custom-call | flops 4294967296 | bytes 1024 | tf_op jit(solution)/shard_map/last_first/pallas_call | solution.py:40
  64.8 1.4 %collective-permute-done.6.refs_0_.vecs_b_ref = f32[304,128]{1,0:T(8,128)S(1)} collective-permute-done((f32[304,128]{1,0:T(8,128)S(1)}, f32[304,128]{1,0:T(8,128)S(1)}, u32[]{:S(2)}, u32[]{:S(2)}) %collective-permute-start.6) | collective-permute-done | bytes 155680 | tf_op jit(solution)/shard_map/ppermute | solution.py:286
  66.2 1.5 %last_second.1 = (bf16[1024,256]{1,0:T(8,128)(2,1)S(1)}, f32[640,256]{1,0:T(8,128)S(1)}, f32[640,256]{1,0:T(8,128)S(1)}) custom-call(f32[304,128]{1,0:T(8,128)S(1)} %collective-permute-done.6.refs_0_.vecs_b_ref, bf16[1024,384]{1,0:T(8,128)(2,1)S(1)} %get-tuple-element.55.refs_1_.refs_2_, bf16[1024,384]{1,0:T(8,128)(2,1)S(1)} %get-tuple-element.56.refs_2_.refs_3_, ...), custom_call_target="tpu_custom_call" | custom-call | flops 4294967296 | bytes 1024 | tf_op jit(solution)/shard_map/last_second/pallas_call | solution.py:40
  67.7 1.9 %collective-permute-start.8 = (f32[640,256]{1,0:T(8,128)S(1)}, f32[640,256]{1,0:T(8,128)S(1)}, u32[]{:S(2)}, u32[]{:S(2)}) collective-permute-start(f32[640,256]{1,0:T(8,128)S(1)} %get-tuple-element.97), channel_id=1, source_target_pairs={{0,1},{1,0},{2,3},{3,2},{4,5},{5,4},{6,7},{7,6},{8,9},{9,8},{10,11... | collective-permute-start | bytes 1966088 | tf_op jit(solution)/shard_map/ppermute | solution.py:291
  69.6 3.0 %collective-permute-done.7.moments_ref = f32[608,128]{1,0:T(8,128)S(1)} collective-permute-done((f32[608,128]{1,0:T(8,128)S(1)}, f32[608,128]{1,0:T(8,128)S(1)}, u32[]{:S(2)}, u32[]{:S(2)}) %collective-permute-start.7) | collective-permute-done | bytes 311328 | tf_op jit(solution)/shard_map/ppermute | solution.py:286
  72.6 1.7 %last_update.1 = (f32[300,256]{1,0:T(8,128)}, f32[300,256]{1,0:T(8,128)}) custom-call(f32[304,128]{1,0:T(8,128)S(1)} %collective-permute-done.4.refs_0_.vecs_a_ref, f32[304,128]{1,0:T(8,128)S(1)} %collective-permute-done.6.refs_0_.vecs_b_ref, f32[608,128]{1,0:T(8,128)S(1)} %collective-permute-done.7.moments_ref, ...), custom_call_target="tpu_custom_call" | custom-call | flops 8589934592 | bytes 1024 | tf_op jit(solution)/shard_map/last_update/pallas_call | solution.py:40
  75.3 7.6 %all-to-all-start = ((f32[16,40,256]{2,1,0:T(8,128)}), f32[16,40,256]{2,1,0:T(8,128)S(1)}, u32[]{:S(2)}, u32[]{:S(2)}) async-start(f32[16,40,256]{2,1,0:T(8,128)} %sum.1), calls=%async_computation | async-start | bytes 1310720 | tf_op jit(solution)/shard_map/all_to_all | solution.py:404
  82.8 1.2 %shares.1 = (f32[32,300]{1,0:T(8,128)S(1)}, f32[32,300]{1,0:T(8,128)S(1)}) custom-call(f32[300,1024]{1,0:T(8,128)} %row_hbm.3, f32[300,1024]{1,0:T(8,128)} %acc_hbm.1), custom_call_target="tpu_custom_call" | custom-call | flops 4294967296 | bytes 1024 | tf_op jit(solution)/shard_map/shares/pallas_call | solution.py:40
  84.1 14.9 %all-to-all-done.parts_ref = f32[16,40,256]{2,1,0:T(8,128)S(1)} async-done(((f32[16,40,256]{2,1,0:T(8,128)}), f32[16,40,256]{2,1,0:T(8,128)S(1)}, u32[]{:S(2)}, u32[]{:S(2)}) %all-to-all-start) | async-done | bytes 655392 | tf_op jit(solution)/shard_map/all_to_all | solution.py:404
  (12 shorter events, 8.4 us)
Async XLA Ops:
  4.2 24.9 %collective-permute-start.1 = (f32[304,128]{1,0:T(8,128)S(1)}, f32[304,128]{1,0:T(8,128)S(1)}, u32[]{:S(2)}, u32[]{:S(2)}) collective-permute-start(f32[304,128]{1,0:T(8,128)S(1)} %get-tuple-element.64.refs_6_), channel_id=1, source_target_pairs={{0,32},{32,64},{64,96},{96,128},{128,160},{160,192},{192,224},{224... | collective-permute-start | bytes 466952 | tf_op jit(solution)/shard_map/ppermute | solution.py:286
  10.2 22.0 %collective-permute-start.3 = (f32[304,128]{1,0:T(8,128)S(1)}, f32[304,128]{1,0:T(8,128)S(1)}, u32[]{:S(2)}, u32[]{:S(2)}) collective-permute-start(f32[304,128]{1,0:T(8,128)S(1)} %get-tuple-element.66.refs_8_), channel_id=1, source_target_pairs={{0,32},{32,64},{64,96},{96,128},{128,160},{160,192},{192,224},{224... | collective-permute-start | bytes 466952 | tf_op jit(solution)/shard_map/ppermute | solution.py:286
  17.2 33.6 %collective-permute-start = (f32[1216,128]{1,0:T(8,128)S(1)}, f32[1216,128]{1,0:T(8,128)S(1)}, u32[]{:S(2)}, u32[]{:S(2)}) collective-permute-start(f32[1216,128]{1,0:T(8,128)S(1)} %get-tuple-element.68), channel_id=1, source_target_pairs={{0,64},{32,96},{64,128},{96,160},{128,192},{160,224},{192,256},{22... | collective-permute-start | bytes 1867784 | tf_op jit(solution)/shard_map/ppermute | solution.py:286
  30.2 20.5 %collective-permute-start.2 = (f32[304,128]{1,0:T(8,128)S(1)}, f32[304,128]{1,0:T(8,128)S(1)}, u32[]{:S(2)}, u32[]{:S(2)}) collective-permute-start(f32[304,128]{1,0:T(8,128)S(1)} %get-tuple-element.71), channel_id=1, source_target_pairs={{0,32},{32,64},{64,96},{96,128},{128,160},{160,192},{192,224},{224... | collective-permute-start | bytes 466952 | tf_op jit(solution)/shard_map/ppermute | solution.py:286
  33.3 20.5 %collective-permute-start.5 = (f32[304,128]{1,0:T(8,128)S(1)}, f32[304,128]{1,0:T(8,128)S(1)}, u32[]{:S(2)}, u32[]{:S(2)}) collective-permute-start(f32[304,128]{1,0:T(8,128)S(1)} %get-tuple-element.78), channel_id=1, source_target_pairs={{0,32},{32,64},{64,96},{96,128},{128,160},{160,192},{192,224},{224... | collective-permute-start | bytes 466952 | tf_op jit(solution)/shard_map/ppermute | solution.py:286
  51.9 11.6 %collective-permute-start.4 = (f32[304,128]{1,0:T(8,128)S(1)}, f32[304,128]{1,0:T(8,128)S(1)}, u32[]{:S(2)}, u32[]{:S(2)}) collective-permute-start(f32[304,128]{1,0:T(8,128)S(1)} %get-tuple-element.77), channel_id=1, source_target_pairs={{0,32},{32,64},{64,96},{96,128},{128,160},{160,192},{192,224},{224... | collective-permute-start | bytes 466952 | tf_op jit(solution)/shard_map/ppermute | solution.py:286
  55.0 11.2 %collective-permute-start.6 = (f32[304,128]{1,0:T(8,128)S(1)}, f32[304,128]{1,0:T(8,128)S(1)}, u32[]{:S(2)}, u32[]{:S(2)}) collective-permute-start(f32[304,128]{1,0:T(8,128)S(1)} %get-tuple-element.79), channel_id=1, source_target_pairs={{0,32},{32,64},{64,96},{96,128},{128,160},{160,192},{192,224},{224... | collective-permute-start | bytes 466952 | tf_op jit(solution)/shard_map/ppermute | solution.py:286
  58.9 13.7 %collective-permute-start.7 = (f32[608,128]{1,0:T(8,128)S(1)}, f32[608,128]{1,0:T(8,128)S(1)}, u32[]{:S(2)}, u32[]{:S(2)}) collective-permute-start(f32[608,128]{1,0:T(8,128)S(1)} %get-tuple-element.87), channel_id=1, source_target_pairs={{0,32},{32,64},{64,96},{96,128},{128,160},{160,192},{192,224},{224... | collective-permute-start | bytes 933896 | tf_op jit(solution)/shard_map/ppermute | solution.py:286
  67.7 6.6 %collective-permute-start.8 = (f32[640,256]{1,0:T(8,128)S(1)}, f32[640,256]{1,0:T(8,128)S(1)}, u32[]{:S(2)}, u32[]{:S(2)}) collective-permute-start(f32[640,256]{1,0:T(8,128)S(1)} %get-tuple-element.97), channel_id=1, source_target_pairs={{0,1},{1,0},{2,3},{3,2},{4,5},{5,4},{6,7},{7,6},{8,9},{9,8},{10,11... | collective-permute-start | bytes 1966088 | tf_op jit(solution)/shard_map/ppermute | solution.py:291
  75.3 23.7 %all-to-all-start = ((f32[16,40,256]{2,1,0:T(8,128)}), f32[16,40,256]{2,1,0:T(8,128)S(1)}, u32[]{:S(2)}, u32[]{:S(2)}) async-start(f32[16,40,256]{2,1,0:T(8,128)} %sum.1), calls=%async_computation | async-start | bytes 1310720 | tf_op jit(solution)/shard_map/all_to_all | solution.py:404

commit v4 on v3

--- a/solution.py
+++ b/solution.py
@@ -174,7 +174,9 @@
 
 
 def third_visit_body(side, whole_ref, sent_ref, turned_hi_ref, turned_lo_ref, hi_ref, lo_ref, target_ref, weight_ref, *refs):
-    now_ref, vecs_ref, moment_ref, grad_ref, both_ref = refs
+    now_ref, vecs_ref, moment_ref, grad_ref, both_ref = refs[-5:]
+    if side:
+        moment_ref[0:PADW, :] = refs[0][...]
     at = side * 2 * PADW
     vecs, moment = updated(whole_ref[at : at + WIDTH, :], whole_ref[at + PADW : at + PADW + WIDTH, :], sent_ref[0:WIDTH, :])
     now_ref[0:WIDTH, :] = vecs
@@ -184,13 +186,13 @@
     vecs, moment = updated(now_ref[0:WIDTH, :], moment, col_grads(hi_ref, lo_ref, grad_ref))
     vecs_ref[0:WIDTH, :] = vecs
     vecs_ref[WIDTH:, :] = now_ref[WIDTH:, :]
-    moment_ref[0:WIDTH, :] = moment
-    moment_ref[WIDTH:, :] = jnp.zeros((PADW - WIDTH, HALF), f32)
-
-
-def last_update_body(vecs_a_ref, vecs_b_ref, moments_ref, grad_a_ref, grad_b_ref, hi_ref, lo_ref, new_ref, new_moment_ref):
-    for side, (vecs_ref, grad_ref) in enumerate(((vecs_a_ref, grad_a_ref), (vecs_b_ref, grad_b_ref))):
-        grad = col_grads(hi_ref, lo_ref, grad_ref)
+    moment_ref[side * PADW : side * PADW + WIDTH, :] = moment
+    moment_ref[side * PADW + WIDTH : (side + 1) * PADW, :] = jnp.zeros((PADW - WIDTH, HALF), f32)
+
+
+def last_update_body(vecs_a_ref, vecs_b_ref, moments_ref, col_grad_a_ref, grad_b_ref, hi_ref, lo_ref, new_ref, new_moment_ref):
+    for side, vecs_ref in enumerate((vecs_a_ref, vecs_b_ref)):
+        grad = col_grads(hi_ref, lo_ref, grad_b_ref) if side else col_grad_a_ref[...]
         vecs, moment = updated(vecs_ref[0:WIDTH, :], moments_ref[side * PADW : side * PADW + WIDTH, :], grad)
         new_ref[:, side * HALF : (side + 1) * HALF] = vecs
         new_moment_ref[:, side * HALF : (side + 1) * HALF] = moment
@@ -219,21 +221,25 @@
 SPREAD = [pltpu.VMEM((LANES, 2 * HALF), bf16), pltpu.VMEM((LANES, HALF), bf16)]
 
 
-def beside_body(turn, packs, counts_hbm, vecs_a_ref, vecs_b_ref, grad_a_ref, grad_b_ref, logs_ref, *refs):
-    before_ref = refs[packs] if turn else None
-    packed_ref = refs[-10] if packs else None
-    total_ref, target_ref, weight_ref, counts_ref, high_a_ref, low_a_ref, high_b_ref, low_b_ref, done = refs[-9:]
+def tables_body(turn, counts_hbm, logs_ref, after_ref, *refs):
+    packs = len(refs) - 4 - (1 if len(refs) > 4 else 0)
+    target_ref, weight_ref, counts_ref, done = refs[-4:]
     get_counts = fetch(counts_hbm.at[turn + 1], counts_ref, done)
     for at in range(packs):
-        packed_ref[at * PADW : (at + 1) * PADW, :] = refs[at][...]
+        refs[packs][at * PADW : (at + 1) * PADW, :] = refs[at][...]
+    get_counts.wait()
+    count_tables(counts_ref, logs_ref, target_ref, weight_ref)
+
+
+def rows_body(more, vecs_a_ref, vecs_b_ref, grad_a_ref, grad_b_ref, *refs):
+    before_ref = refs[0] if more else None
+    total_ref, high_a_ref, low_a_ref, high_b_ref, low_b_ref = refs[-5:]
     spread(vecs_a_ref, high_a_ref, low_a_ref)
     spread(vecs_b_ref, high_b_ref, low_b_ref)
     for at in range(0, ROWS, TILE):
         rows = slice(at, at + TILE)
         part = row_part(grad_a_ref, high_a_ref, low_a_ref, rows) + row_part(grad_b_ref, high_b_ref, low_b_ref, rows)
-        total_ref[rows, :] = before_ref[rows, :] + part if turn else part
-    get_counts.wait()
-    count_tables(counts_ref, logs_ref, target_ref, weight_ref)
+        total_ref[rows, :] = before_ref[rows, :] + part if more else part
 
 
 def last_half(side, vecs_ref, turned_hi_ref, turned_lo_ref, target_ref, weight_ref, before_ref, grad_ref, total_ref, both_ref, high_ref, low_ref):
@@ -243,6 +249,11 @@
     for at in range(0, ROWS, TILE):
         rows = slice(at, at + TILE)
         total_ref[rows, :] = before_ref[rows, :] + row_part(grad_ref, high_ref, low_ref, rows)
+
+
+def last_first_body(vecs_ref, turned_hi_ref, turned_lo_ref, target_ref, weight_ref, before_ref, hi_ref, lo_ref, total_ref, col_grad_ref, grad_ref, *scratch):
+    last_half(0, vecs_ref, turned_hi_ref, turned_lo_ref, target_ref, weight_ref, before_ref, grad_ref, total_ref, *scratch)
+    col_grad_ref[...] = col_grads(hi_ref, lo_ref, grad_ref)
 
 
 def last_body(side, vecs_ref, turned_hi_ref, turned_lo_ref, target_ref, weight_ref, before_ref, grad_ref, keep_ref, send_ref, total_ref, *scratch):
@@ -319,14 +330,24 @@
 
     def beside(turn, vecs, grads, packs, *more):
         packed = (near(len(packs) * PADW, HALF),) if packs else ()
-        return call(
-            "beside",
-            lambda *refs: beside_body(turn, len(packs), *refs),
-            (*packed, near(ROWS, LANES), table, table),
-            (counts, *vecs, *grads, row_logs, *packs, *more),
-            [pltpu.VMEM((ROWS, 2 * HALF), bf16)] + SPREAD * 2 + [pltpu.SemaphoreType.DMA(())],
+        *packed, target, weight = call(
+            "tables",
+            lambda *refs: tables_body(turn, *refs),
+            (*packed, table, table),
+            (counts, row_logs, grads[1], *packs),
+            [pltpu.VMEM((ROWS, 2 * HALF), bf16), pltpu.SemaphoreType.DMA(())],
             far=1,
+            flops=1 << 20,
         )
+        total = call(
+            "rows",
+            lambda *refs: rows_body(turn > 0, *refs),
+            near(ROWS, LANES),
+            (*vecs, *grads, *more),
+            SPREAD * 2,
+            flops=1 << 20,
+        )
+        return (*packed, total, target, weight)
 
     near_vecs = near(PADW, HALF)
     vecs, moments, grads = [None] * 2, [None] * 2, [None] * 2
@@ -354,25 +375,25 @@
         sent[side] = shifted(sent[side])
     total, target, weight = beside(1, vecs, grads, (), total)
 
-    now, vecs, grads = [None] * 2, [None] * 2, [None] * 2
+    now, vecs, grads, moments = [None] * 2, [None] * 2, [None] * 2, ()
     for side in range(2):
-        now[side], vecs[side], moments[side], grads[side] = call(
+        now[side], vecs[side], *moments, grads[side] = call(
             "third_visit",
             lambda *refs, side=side: third_visit_body(side, *refs),
-            (near_vecs, near_vecs, near_vecs, cell_half),
-            (whole, sent[side], *rows, target, weight),
+            (near_vecs, near_vecs, near((1 + side) * PADW, HALF), cell_half),
+            (whole, sent[side], *rows, target, weight, *moments),
             [both],
         )
         vecs[side] = shifted(vecs[side])
-    moments, total, target, weight = beside(2, now, grads, moments, total)
-    moments = shifted(moments)
-
-    grad_a, part = call(
+    moments = shifted(moments[0])
+    total, target, weight = beside(2, now, grads, (), total)
+
+    part, col_grad_a = call(
         "last_first",
-        lambda *refs: last_half(0, *refs),
-        (cell_half, near(ROWS, LANES)),
-        (vecs[0], turned_hi, turned_lo, target, weight, total),
-        [both] + SPREAD,
+        last_first_body,
+        (near(ROWS, LANES), near(WIDTH, HALF)),
+        (vecs[0], turned_hi, turned_lo, target, weight, total, hi, lo),
+        [pltpu.VMEM((ROWS, 2 * HALF), bf16), both] + SPREAD,
     )
     grad_b, keep, send = call(
         "last_second",
@@ -386,8 +407,8 @@
         "last_update",
         last_update_body,
         (free(WIDTH, 2 * HALF), free(WIDTH, 2 * HALF)),
-        (vecs[0], vecs[1], moments, grad_a, grad_b, hi, lo),
-        flops=1 << 33,
+        (vecs[0], vecs[1], moments, col_grad_a, grad_b, hi, lo),
+        flops=1 << 32,
     )
 
     own_vecs, own_moment = call(

time: 100 us -> 100 us (level)
  the two profiles are of different devices: /device:TPU:8 before, /device:TPU:10 now
where the time goes in v4:
time: 100 us; the launch traced here: 99.5 us
  waiting for transfers between devices  40.3 us (40%)
  starting transfers between devices  33.6 us (34%)
  Pallas kernels  24.8 us (25%)
    pallas_call x19, Pallas kernels, call(): pl.pallas_call(body, out_shape=out, in_specs=specs, out_specs=jax.tree.ma...  24.8 us
    ppermute x8, waiting for transfers between devices, shifted(): lax.ppermute(value, 'blk', [(source, (source + steps) % count) for source...  24.2 us
    ppermute x8, starting transfers between devices, shifted(): lax.ppermute(value, 'blk', [(source, (source + steps) % count) for source...  23.2 us
    all_to_all x1, waiting for transfers between devices, shards(): parts = lax.all_to_all(share, 'grp', 0, 0, axis_index_groups=chips)  16 us
    all_to_all x1, starting transfers between devices, shards(): parts = lax.all_to_all(share, 'grp', 0, 0, axis_index_groups=chips)  8.47 us
  transfers between devices with their start and end apart: 10, of which 7 were waited for; matrix products, arithmetic and copies ran while one was open for 0% of the time, Pallas kernels for 20%

profile of v4, /device:TPU:10, one launch (start us, length us, event | category | flops | bytes accessed | tf_op | source)
XLA Modules:
  0.0 99.5 jit_solution(8571655830575353989)
XLA Ops:
  0.6 2.5 %prep.1 = (bf16[300,1024]{1,0:T(8,128)(2,1)S(1)}, bf16[300,1024]{1,0:T(8,128)(2,1)S(1)}, bf16[1024,384]{1,0:T(8,128)(2,1)S(1)}, bf16[1024,384]{1,0:T(8,128)(2,1)...) custom-call(f32[300,1024]{1,0:T(8,128)} %row_hbm.3, ...), custom_call_target="tpu_custom_call" | custom-call | flops 4294967296 | bytes 1024 | tf_op jit(solution)/shard_map/prep/pallas_call | solution.py:40
  4.2 4.0 %collective-permute-start.1 = (f32[304,128]{1,0:T(8,128)S(1)}, f32[304,128]{1,0:T(8,128)S(1)}, u32[]{:S(2)}, u32[]{:S(2)}) collective-permute-start(f32[304,128]{1,0:T(8,128)S(1)} %get-tuple-element.59.refs_3_), channel_id=1, source_target_pairs={{0,32},{32,64},{64,96},{96,128},{128,160},{160,192},{192,224},{224... | collective-permute-start | bytes 466952 | tf_op jit(solution)/shard_map/ppermute | solution.py:297
  9.3 5.1 %collective-permute-start.3 = (f32[304,128]{1,0:T(8,128)S(1)}, f32[304,128]{1,0:T(8,128)S(1)}, u32[]{:S(2)}, u32[]{:S(2)}) collective-permute-start(f32[304,128]{1,0:T(8,128)S(1)} %get-tuple-element.61.refs_5_), channel_id=1, source_target_pairs={{0,32},{32,64},{64,96},{96,128},{128,160},{160,192},{192,224},{224... | collective-permute-start | bytes 466952 | tf_op jit(solution)/shard_map/ppermute | solution.py:297
  14.5 1.6 %tables.3 = (f32[1216,128]{1,0:T(8,128)S(1)}, f32[1024,256]{1,0:T(8,128)S(1)}, f32[1024,256]{1,0:T(8,128)S(1)}) custom-call(bf16[4,1024,256]{2,1,0:T(8,128)(2,1)} %refs_0_.5, f32[1024,128]{1,0:T(8,128)S(1)} %get-tuple-element.49.refs_1_, bf16[1024,256]{1,0:T(8,128)(2,1)S(1)} %get-tuple-element.57.refs_2_.refs_3_, f32[304,128]{1,0:T(8,128)S(1)} %get-tuple-element.59.refs_3_, ...), custom_call_target="tpu_custom_call" | custom-call | flops 1048576 | bytes 1024 | tf_op jit(solution)/shard_map/tables/pallas_call | solution.py:40
  16.1 4.3 %collective-permute-start = (f32[1216,128]{1,0:T(8,128)S(1)}, f32[1216,128]{1,0:T(8,128)S(1)}, u32[]{:S(2)}, u32[]{:S(2)}) collective-permute-start(f32[1216,128]{1,0:T(8,128)S(1)} %get-tuple-element.63), channel_id=1, source_target_pairs={{0,64},{32,96},{64,128},{96,160},{128,192},{160,224},{192,256},{22... | collective-permute-start | bytes 1867784 | tf_op jit(solution)/shard_map/ppermute | solution.py:297
  21.6 6.7 %collective-permute-done.1.refs_0_ = f32[304,128]{1,0:T(8,128)S(1)} collective-permute-done((f32[304,128]{1,0:T(8,128)S(1)}, f32[304,128]{1,0:T(8,128)S(1)}, u32[]{:S(2)}, u32[]{:S(2)}) %collective-permute-start.1) | collective-permute-done | bytes 155680 | tf_op jit(solution)/shard_map/ppermute | solution.py:297
  29.3 1.9 %collective-permute-start.2 = (f32[304,128]{1,0:T(8,128)S(1)}, f32[304,128]{1,0:T(8,128)S(1)}, u32[]{:S(2)}, u32[]{:S(2)}) collective-permute-start(f32[304,128]{1,0:T(8,128)S(1)} %get-tuple-element.66), channel_id=1, source_target_pairs={{0,32},{32,64},{64,96},{96,128},{128,160},{160,192},{192,224},{224... | collective-permute-start | bytes 466952 | tf_op jit(solution)/shard_map/ppermute | solution.py:297
  32.4 1.9 %collective-permute-start.5 = (f32[304,128]{1,0:T(8,128)S(1)}, f32[304,128]{1,0:T(8,128)S(1)}, u32[]{:S(2)}, u32[]{:S(2)}) collective-permute-start(f32[304,128]{1,0:T(8,128)S(1)} %get-tuple-element.71), channel_id=1, source_target_pairs={{0,32},{32,64},{64,96},{96,128},{128,160},{160,192},{192,224},{224... | collective-permute-start | bytes 466952 | tf_op jit(solution)/shard_map/ppermute | solution.py:297
  34.4 1.6 %tables.4 = (f32[1024,256]{1,0:T(8,128)S(1)}, f32[1024,256]{1,0:T(8,128)S(1)}) custom-call(bf16[4,1024,256]{2,1,0:T(8,128)(2,1)} %refs_0_.5, f32[1024,128]{1,0:T(8,128)S(1)} %get-tuple-element.49.refs_1_, bf16[1024,256]{1,0:T(8,128)(2,1)S(1)} %get-tuple-element.67.refs_2_.refs_3_), custom_call_target="tpu_custom_call" | custom-call | flops 1048576 | bytes 1024 | tf_op jit(solution)/shard_map/tables/pallas_call | solution.py:40
  37.2 11.6 %collective-permute-done.2.refs_1_ = f32[304,128]{1,0:T(8,128)S(1)} collective-permute-done((f32[304,128]{1,0:T(8,128)S(1)}, f32[304,128]{1,0:T(8,128)S(1)}, u32[]{:S(2)}, u32[]{:S(2)}) %collective-permute-start.2) | collective-permute-done | bytes 155680 | tf_op jit(solution)/shard_map/ppermute | solution.py:297
  50.0 1.9 %collective-permute-start.4 = (f32[304,128]{1,0:T(8,128)S(1)}, f32[304,128]{1,0:T(8,128)S(1)}, u32[]{:S(2)}, u32[]{:S(2)}) collective-permute-start(f32[304,128]{1,0:T(8,128)S(1)} %get-tuple-element.70), channel_id=1, source_target_pairs={{0,32},{32,64},{64,96},{96,128},{128,160},{160,192},{192,224},{224... | collective-permute-start | bytes 466952 | tf_op jit(solution)/shard_map/ppermute | solution.py:297
  53.1 1.9 %collective-permute-start.6 = (f32[304,128]{1,0:T(8,128)S(1)}, f32[304,128]{1,0:T(8,128)S(1)}, u32[]{:S(2)}, u32[]{:S(2)}) collective-permute-start(f32[304,128]{1,0:T(8,128)S(1)} %get-tuple-element.73), channel_id=1, source_target_pairs={{0,32},{32,64},{64,96},{96,128},{128,160},{160,192},{192,224},{224... | collective-permute-start | bytes 466952 | tf_op jit(solution)/shard_map/ppermute | solution.py:297
  55.0 2.1 %collective-permute-start.7 = (f32[608,128]{1,0:T(8,128)S(1)}, f32[608,128]{1,0:T(8,128)S(1)}, u32[]{:S(2)}, u32[]{:S(2)}) collective-permute-start(f32[608,128]{1,0:T(8,128)S(1)} %get-tuple-element.74), channel_id=1, source_target_pairs={{0,32},{32,64},{64,96},{96,128},{128,160},{160,192},{192,224},{224... | collective-permute-start | bytes 933896 | tf_op jit(solution)/shard_map/ppermute | solution.py:297
  57.1 1.6 %tables.5 = (f32[1024,256]{1,0:T(8,128)S(1)}, f32[1024,256]{1,0:T(8,128)S(1)}) custom-call(bf16[4,1024,256]{2,1,0:T(8,128)(2,1)} %refs_0_.5, f32[1024,128]{1,0:T(8,128)S(1)} %get-tuple-element.49.refs_1_, bf16[1024,256]{1,0:T(8,128)(2,1)S(1)} %get-tuple-element.75.refs_2_.refs_3_), custom_call_target="tpu_custom_call" | custom-call | flops 1048576 | bytes 1024 | tf_op jit(solution)/shard_map/tables/pallas_call | solution.py:40
  59.9 1.5 %collective-permute-done.4.vecs_ref.vecs_a_ref = f32[304,128]{1,0:T(8,128)S(1)} collective-permute-done((f32[304,128]{1,0:T(8,128)S(1)}, f32[304,128]{1,0:T(8,128)S(1)}, u32[]{:S(2)}, u32[]{:S(2)}) %collective-permute-start.4) | collective-permute-done | bytes 155680 | tf_op jit(solution)/shard_map/ppermute | solution.py:297
  61.4 1.6 %last_first.1 = (f32[1024,384]{1,0:T(8,128)S(1)}, f32[300,128]{1,0:T(8,128)S(1)}) custom-call(f32[304,128]{1,0:T(8,128)S(1)} %collective-permute-done.4.vecs_ref.vecs_a_ref, bf16[1024,384]{1,0:T(8,128)(2,1)S(1)} %get-tuple-element.51.refs_1_.refs_2_.turned_hi_ref, bf16[1024,384]{1,0:T(8,128)(2,1)S(1)} %get-tuple-element.52.refs_2_.refs_3_.turned_lo_ref, ...), custom_call_target="tpu_custom_call" | custom-call | flops 4294967296 | bytes 1024 | tf_op jit(solution)/shard_map/last_first/pallas_call | solution.py:40
  63.0 2.6 %collective-permute-done.6.refs_0_.vecs_b_ref = f32[304,128]{1,0:T(8,128)S(1)} collective-permute-done((f32[304,128]{1,0:T(8,128)S(1)}, f32[304,128]{1,0:T(8,128)S(1)}, u32[]{:S(2)}, u32[]{:S(2)}) %collective-permute-start.6) | collective-permute-done | bytes 155680 | tf_op jit(solution)/shard_map/ppermute | solution.py:297
  65.6 1.5 %last_second.1 = (bf16[1024,256]{1,0:T(8,128)(2,1)S(1)}, f32[640,256]{1,0:T(8,128)S(1)}, f32[640,256]{1,0:T(8,128)S(1)}) custom-call(f32[304,128]{1,0:T(8,128)S(1)} %collective-permute-done.6.refs_0_.vecs_b_ref, bf16[1024,384]{1,0:T(8,128)(2,1)S(1)} %get-tuple-element.51.refs_1_.refs_2_.turned_hi_ref, ...), custom_call_target="tpu_custom_call" | custom-call | flops 4294967296 | bytes 1024 | tf_op jit(solution)/shard_map/last_second/pallas_call | solution.py:40
  67.0 1.9 %collective-permute-start.8 = (f32[640,256]{1,0:T(8,128)S(1)}, f32[640,256]{1,0:T(8,128)S(1)}, u32[]{:S(2)}, u32[]{:S(2)}) collective-permute-start(f32[640,256]{1,0:T(8,128)S(1)} %get-tuple-element.89), channel_id=1, source_target_pairs={{0,1},{1,0},{2,3},{3,2},{4,5},{5,4},{6,7},{7,6},{8,9},{9,8},{10,11... | collective-permute-start | bytes 1966088 | tf_op jit(solution)/shard_map/ppermute | solution.py:302
  68.9 1.8 %collective-permute-done.7.moments_ref = f32[608,128]{1,0:T(8,128)S(1)} collective-permute-done((f32[608,128]{1,0:T(8,128)S(1)}, f32[608,128]{1,0:T(8,128)S(1)}, u32[]{:S(2)}, u32[]{:S(2)}) %collective-permute-start.7) | collective-permute-done | bytes 311328 | tf_op jit(solution)/shard_map/ppermute | solution.py:297
  70.7 1.4 %last_update.1 = (f32[300,256]{1,0:T(8,128)}, f32[300,256]{1,0:T(8,128)}) custom-call(f32[304,128]{1,0:T(8,128)S(1)} %collective-permute-done.4.vecs_ref.vecs_a_ref, f32[304,128]{1,0:T(8,128)S(1)} %collective-permute-done.6.refs_0_.vecs_b_ref, f32[608,128]{1,0:T(8,128)S(1)} %collective-permute-done.7.moments_ref, ...), custom_call_target="tpu_custom_call" | custom-call | flops 4294967296 | bytes 1024 | tf_op jit(solution)/shard_map/last_update/pallas_call | solution.py:40
  73.0 8.5 %all-to-all-start = ((f32[16,40,256]{2,1,0:T(8,128)}), f32[16,40,256]{2,1,0:T(8,128)S(1)}, u32[]{:S(2)}, u32[]{:S(2)}) async-start(f32[16,40,256]{2,1,0:T(8,128)} %sum.1), calls=%async_computation | async-start | bytes 1310720 | tf_op jit(solution)/shard_map/all_to_all | solution.py:425
  81.5 1.2 %shares.1 = (f32[32,300]{1,0:T(8,128)S(1)}, f32[32,300]{1,0:T(8,128)S(1)}) custom-call(f32[300,1024]{1,0:T(8,128)} %row_hbm.3, f32[300,1024]{1,0:T(8,128)} %acc_hbm.1), custom_call_target="tpu_custom_call" | custom-call | flops 4294967296 | bytes 1024 | tf_op jit(solution)/shard_map/shares/pallas_call | solution.py:40
  82.7 16.0 %all-to-all-done.parts_ref = f32[16,40,256]{2,1,0:T(8,128)S(1)} async-done(((f32[16,40,256]{2,1,0:T(8,128)}), f32[16,40,256]{2,1,0:T(8,128)S(1)}, u32[]{:S(2)}, u32[]{:S(2)}) %all-to-all-start) | async-done | bytes 655392 | tf_op jit(solution)/shard_map/all_to_all | solution.py:425
  (15 shorter events, 11.9 us)
Async XLA Ops:
  4.2 24.0 %collective-permute-start.1 = (f32[304,128]{1,0:T(8,128)S(1)}, f32[304,128]{1,0:T(8,128)S(1)}, u32[]{:S(2)}, u32[]{:S(2)}) collective-permute-start(f32[304,128]{1,0:T(8,128)S(1)} %get-tuple-element.59.refs_3_), channel_id=1, source_target_pairs={{0,32},{32,64},{64,96},{96,128},{128,160},{160,192},{192,224},{224... | collective-permute-start | bytes 466952 | tf_op jit(solution)/shard_map/ppermute | solution.py:297
  9.3 22.0 %collective-permute-start.3 = (f32[304,128]{1,0:T(8,128)S(1)}, f32[304,128]{1,0:T(8,128)S(1)}, u32[]{:S(2)}, u32[]{:S(2)}) collective-permute-start(f32[304,128]{1,0:T(8,128)S(1)} %get-tuple-element.61.refs_5_), channel_id=1, source_target_pairs={{0,32},{32,64},{64,96},{96,128},{128,160},{160,192},{192,224},{224... | collective-permute-start | bytes 466952 | tf_op jit(solution)/shard_map/ppermute | solution.py:297
  16.1 32.7 %collective-permute-start = (f32[1216,128]{1,0:T(8,128)S(1)}, f32[1216,128]{1,0:T(8,128)S(1)}, u32[]{:S(2)}, u32[]{:S(2)}) collective-permute-start(f32[1216,128]{1,0:T(8,128)S(1)} %get-tuple-element.63), channel_id=1, source_target_pairs={{0,64},{32,96},{64,128},{96,160},{128,192},{160,224},{192,256},{22... | collective-permute-start | bytes 1867784 | tf_op jit(solution)/shard_map/ppermute | solution.py:297
  29.3 19.5 %collective-permute-start.2 = (f32[304,128]{1,0:T(8,128)S(1)}, f32[304,128]{1,0:T(8,128)S(1)}, u32[]{:S(2)}, u32[]{:S(2)}) collective-permute-start(f32[304,128]{1,0:T(8,128)S(1)} %get-tuple-element.66), channel_id=1, source_target_pairs={{0,32},{32,64},{64,96},{96,128},{128,160},{160,192},{192,224},{224... | collective-permute-start | bytes 466952 | tf_op jit(solution)/shard_map/ppermute | solution.py:297
  32.4 19.5 %collective-permute-start.5 = (f32[304,128]{1,0:T(8,128)S(1)}, f32[304,128]{1,0:T(8,128)S(1)}, u32[]{:S(2)}, u32[]{:S(2)}) collective-permute-start(f32[304,128]{1,0:T(8,128)S(1)} %get-tuple-element.71), channel_id=1, source_target_pairs={{0,32},{32,64},{64,96},{96,128},{128,160},{160,192},{192,224},{224... | collective-permute-start | bytes 466952 | tf_op jit(solution)/shard_map/ppermute | solution.py:297
  50.0 11.5 %collective-permute-start.4 = (f32[304,128]{1,0:T(8,128)S(1)}, f32[304,128]{1,0:T(8,128)S(1)}, u32[]{:S(2)}, u32[]{:S(2)}) collective-permute-start(f32[304,128]{1,0:T(8,128)S(1)} %get-tuple-element.70), channel_id=1, source_target_pairs={{0,32},{32,64},{64,96},{96,128},{128,160},{160,192},{192,224},{224... | collective-permute-start | bytes 466952 | tf_op jit(solution)/shard_map/ppermute | solution.py:297
  53.1 12.5 %collective-permute-start.6 = (f32[304,128]{1,0:T(8,128)S(1)}, f32[304,128]{1,0:T(8,128)S(1)}, u32[]{:S(2)}, u32[]{:S(2)}) collective-permute-start(f32[304,128]{1,0:T(8,128)S(1)} %get-tuple-element.73), channel_id=1, source_target_pairs={{0,32},{32,64},{64,96},{96,128},{128,160},{160,192},{192,224},{224... | collective-permute-start | bytes 466952 | tf_op jit(solution)/shard_map/ppermute | solution.py:297
  55.0 15.7 %collective-permute-start.7 = (f32[608,128]{1,0:T(8,128)S(1)}, f32[608,128]{1,0:T(8,128)S(1)}, u32[]{:S(2)}, u32[]{:S(2)}) collective-permute-start(f32[608,128]{1,0:T(8,128)S(1)} %get-tuple-element.74), channel_id=1, source_target_pairs={{0,32},{32,64},{64,96},{96,128},{128,160},{160,192},{192,224},{224... | collective-permute-start | bytes 933896 | tf_op jit(solution)/shard_map/ppermute | solution.py:297
  67.0 5.1 %collective-permute-start.8 = (f32[640,256]{1,0:T(8,128)S(1)}, f32[640,256]{1,0:T(8,128)S(1)}, u32[]{:S(2)}, u32[]{:S(2)}) collective-permute-start(f32[640,256]{1,0:T(8,128)S(1)} %get-tuple-element.89), channel_id=1, source_target_pairs={{0,1},{1,0},{2,3},{3,2},{4,5},{5,4},{6,7},{7,6},{8,9},{9,8},{10,11... | collective-permute-start | bytes 1966088 | tf_op jit(solution)/shard_map/ppermute | solution.py:302
  73.0 25.7 %all-to-all-start = ((f32[16,40,256]{2,1,0:T(8,128)}), f32[16,40,256]{2,1,0:T(8,128)S(1)}, u32[]{:S(2)}, u32[]{:S(2)}) async-start(f32[16,40,256]{2,1,0:T(8,128)} %sum.1), calls=%async_computation | async-start | bytes 1310720 | tf_op jit(solution)/shard_map/all_to_all | solution.py:425

commit v5 on v4

--- a/solution.py
+++ b/solution.py
@@ -51,6 +51,10 @@
 
 def near(*dims, of=f32):
     return pltpu.VMEM(dims, of)
+
+
+def remote(*dims, of=f32):
+    return pltpu.HBM(dims, of)
 
 
 def free(*dims, of=f32):
@@ -190,10 +194,14 @@
     moment_ref[side * PADW + WIDTH : (side + 1) * PADW, :] = jnp.zeros((PADW - WIDTH, HALF), f32)
 
 
-def last_update_body(vecs_a_ref, vecs_b_ref, moments_ref, col_grad_a_ref, grad_b_ref, hi_ref, lo_ref, new_ref, new_moment_ref):
-    for side, vecs_ref in enumerate((vecs_a_ref, vecs_b_ref)):
-        grad = col_grads(hi_ref, lo_ref, grad_b_ref) if side else col_grad_a_ref[...]
-        vecs, moment = updated(vecs_ref[0:WIDTH, :], moments_ref[side * PADW : side * PADW + WIDTH, :], grad)
+def last_update_body(kept_a_hbm, kept_b_hbm, col_grad_a_hbm, col_grad_b_hbm, moments_ref, new_ref, new_moment_ref, *scratch):
+    *refs, done = scratch
+    sources = (kept_a_hbm, kept_b_hbm, col_grad_a_hbm, col_grad_b_hbm)
+    gets = [fetch(source, ref, done.at[at]) for at, (source, ref) in enumerate(zip(sources, refs))]
+    for get in gets:
+        get.wait()
+    for side in range(2):
+        vecs, moment = updated(refs[side][0:WIDTH, :], moments_ref[side * PADW : side * PADW + WIDTH, :], refs[2 + side][0:WIDTH, :])
         new_ref[:, side * HALF : (side + 1) * HALF] = vecs
         new_moment_ref[:, side * HALF : (side + 1) * HALF] = moment
 
@@ -221,12 +229,13 @@
 SPREAD = [pltpu.VMEM((LANES, 2 * HALF), bf16), pltpu.VMEM((LANES, HALF), bf16)]
 
 
-def tables_body(turn, counts_hbm, logs_ref, after_ref, *refs):
-    packs = len(refs) - 4 - (1 if len(refs) > 4 else 0)
-    target_ref, weight_ref, counts_ref, done = refs[-4:]
+def pack_body(*refs):
+    for at, ref in enumerate(refs[:-1]):
+        refs[-1][at * PADW : (at + 1) * PADW, :] = ref[...]
+
+
+def tables_body(turn, counts_hbm, logs_ref, after_ref, target_ref, weight_ref, counts_ref, done):
     get_counts = fetch(counts_hbm.at[turn + 1], counts_ref, done)
-    for at in range(packs):
-        refs[packs][at * PADW : (at + 1) * PADW, :] = refs[at][...]
     get_counts.wait()
     count_tables(counts_ref, logs_ref, target_ref, weight_ref)
 
@@ -251,9 +260,15 @@
         total_ref[rows, :] = before_ref[rows, :] + row_part(grad_ref, high_ref, low_ref, rows)
 
 
-def last_first_body(vecs_ref, turned_hi_ref, turned_lo_ref, target_ref, weight_ref, before_ref, hi_ref, lo_ref, total_ref, col_grad_ref, grad_ref, *scratch):
+def keep_columns(vecs_ref, hi_ref, lo_ref, grad_ref, kept_ref, col_grad_ref):
+    kept_ref[...] = vecs_ref[...]
+    col_grad_ref[0:WIDTH, :] = col_grads(hi_ref, lo_ref, grad_ref)
+    col_grad_ref[WIDTH:, :] = jnp.zeros((PADW - WIDTH, HALF), f32)
+
+
+def last_first_body(vecs_ref, turned_hi_ref, turned_lo_ref, target_ref, weight_ref, before_ref, hi_ref, lo_ref, total_ref, kept_ref, col_grad_ref, grad_ref, *scratch):
     last_half(0, vecs_ref, turned_hi_ref, turned_lo_ref, target_ref, weight_ref, before_ref, grad_ref, total_ref, *scratch)
-    col_grad_ref[...] = col_grads(hi_ref, lo_ref, grad_ref)
+    keep_columns(vecs_ref, hi_ref, lo_ref, grad_ref, kept_ref, col_grad_ref)
 
 
 def last_body(side, vecs_ref, turned_hi_ref, turned_lo_ref, target_ref, weight_ref, before_ref, grad_ref, keep_ref, send_ref, total_ref, *scratch):
@@ -271,7 +286,7 @@
                 ref[slot * PACK + SHARE : (slot + 1) * PACK, pair * 128 : (pair + 1) * 128] = jnp.where(left, upper, lower)
 
 
-def sum_body(new_ref, new_moment_ref, keep_ref, got_ref, out_ref):
+def sum_body(kept_ref, keep_ref, got_ref, out_ref):
     for slot in range(16):
         rows = slice(slot * PACK, (slot + 1) * PACK)
         out_ref[slot] = keep_ref[rows, :] + got_ref[rows, :]
@@ -328,13 +343,12 @@
 
     rows = (turned_hi, turned_lo, hi, lo)
 
-    def beside(turn, vecs, grads, packs, *more):
-        packed = (near(len(packs) * PADW, HALF),) if packs else ()
-        *packed, target, weight = call(
+    def beside(turn, vecs, grads, after, *more):
+        target, weight = call(
             "tables",
             lambda *refs: tables_body(turn, *refs),
-            (*packed, table, table),
-            (counts, row_logs, grads[1], *packs),
+            (table, table),
+            (counts, row_logs, after),
             [pltpu.VMEM((ROWS, 2 * HALF), bf16), pltpu.SemaphoreType.DMA(())],
             far=1,
             flops=1 << 20,
@@ -347,7 +361,7 @@
             SPREAD * 2,
             flops=1 << 20,
         )
-        return (*packed, total, target, weight)
+        return total, target, weight
 
     near_vecs = near(PADW, HALF)
     vecs, moments, grads = [None] * 2, [None] * 2, [None] * 2
@@ -359,7 +373,8 @@
             (states[side], *rows, target, weight),
             [both],
         )
-    whole, total, target, weight = beside(0, states, grads, (vecs[0], moments[0], vecs[1], moments[1]))
+    whole = call("pack", pack_body, near(4 * PADW, HALF), (vecs[0], moments[0], vecs[1], moments[1]), flops=1 << 20)
+    total, target, weight = beside(0, states, grads, whole)
     whole = shifted(whole, 2)
     vecs = [shifted(each) for each in vecs]
 
@@ -373,7 +388,7 @@
             [both],
         )
         sent[side] = shifted(sent[side])
-    total, target, weight = beside(1, vecs, grads, (), total)
+    total, target, weight = beside(1, vecs, grads, grads[1], total)
 
     now, vecs, grads, moments = [None] * 2, [None] * 2, [None] * 2, ()
     for side in range(2):
@@ -386,12 +401,12 @@
         )
         vecs[side] = shifted(vecs[side])
     moments = shifted(moments[0])
-    total, target, weight = beside(2, now, grads, (), total)
-
-    part, col_grad_a = call(
+    total, target, weight = beside(2, now, grads, grads[1], total)
+
+    part, kept_a, col_grad_a = call(
         "last_first",
         last_first_body,
-        (near(ROWS, LANES), near(WIDTH, HALF)),
+        (near(ROWS, LANES), remote(PADW, HALF), remote(PADW, HALF)),
         (vecs[0], turned_hi, turned_lo, target, weight, total, hi, lo),
         [pltpu.VMEM((ROWS, 2 * HALF), bf16), both] + SPREAD,
     )
@@ -403,12 +418,22 @@
         [pltpu.VMEM((ROWS, LANES), f32), both] + SPREAD,
         room=6,
     )
+    kept_b, col_grad_b = call(
+        "last_columns",
+        keep_columns,
+        (remote(PADW, HALF), remote(PADW, HALF)),
+        (vecs[1], hi, lo, grad_b),
+        flops=1 << 20,
+    )
+    small = pltpu.VMEM((PADW, HALF), f32)
     new_col_emb, new_col_acc = call(
         "last_update",
         last_update_body,
         (free(WIDTH, 2 * HALF), free(WIDTH, 2 * HALF)),
-        (vecs[0], vecs[1], moments, col_grad_a, grad_b, hi, lo),
-        flops=1 << 32,
+        (kept_a, kept_b, col_grad_a, col_grad_b, moments),
+        [small] * 4 + [pltpu.SemaphoreType.DMA((4,))],
+        far=4,
+        flops=1 << 20,
     )
 
     own_vecs, own_moment = call(
@@ -420,7 +445,7 @@
         far=2,
     )
     got = swapped(send, 1)
-    share = call("sum", sum_body, near(16, PACK, 256), (new_col_emb, new_col_acc, keep, got), far=2)
+    share = call("sum", sum_body, near(16, PACK, 256), (kept_b, keep, got), far=1)
     chips = [[2 * chip + core for chip in range(16)] for core in range(2)]
     parts = lax.all_to_all(share, "grp", 0, 0, axis_index_groups=chips)
 

time: 100 us -> 99.5 us (level)
  the two profiles are of different devices: /device:TPU:10 before, /device:TPU:8 now
where the time goes in v5:
time: 99.5 us; the launch traced here: 98.9 us
  waiting for transfers between devices  37.9 us (38%)
  starting transfers between devices  32.7 us (33%)
  Pallas kernels  27.4 us (28%)
    ppermute x8, waiting for transfers between devices, shifted(): lax.ppermute(value, 'blk', [(source, (source + steps) % count) for source...  37 us
    pallas_call x21, Pallas kernels, call(): pl.pallas_call(body, out_shape=out, in_specs=specs, out_specs=jax.tree.ma...  27.4 us
    ppermute x8, starting transfers between devices, shifted(): lax.ppermute(value, 'blk', [(source, (source + steps) % count) for source...  23.2 us
    all_to_all x1, starting transfers between devices, shards(): parts = lax.all_to_all(share, 'grp', 0, 0, axis_index_groups=chips)  7.59 us
  transfers between devices with their start and end apart: 10, of which 7 were waited for; matrix products, arithmetic and copies ran while one was open for 0% of the time, Pallas kernels for 21%

profile of v5, /device:TPU:8, one launch (start us, length us, event | category | flops | bytes accessed | tf_op | source)
XLA Modules:
  0.0 98.9 jit_solution(4377286819877055202)
XLA Ops:
  0.6 2.5 %prep.1 = (bf16[300,1024]{1,0:T(8,128)(2,1)S(1)}, bf16[300,1024]{1,0:T(8,128)(2,1)S(1)}, bf16[1024,384]{1,0:T(8,128)(2,1)S(1)}, bf16[1024,384]{1,0:T(8,128)(2,1)...) custom-call(f32[300,1024]{1,0:T(8,128)} %row_hbm.3, ...), custom_call_target="tpu_custom_call" | custom-call | flops 4294967296 | bytes 1024 | tf_op jit(solution)/shard_map/prep/pallas_call | solution.py:40
  4.2 4.9 %collective-permute-start.3 = (f32[304,128]{1,0:T(8,128)S(1)}, f32[304,128]{1,0:T(8,128)S(1)}, u32[]{:S(2)}, u32[]{:S(2)}) collective-permute-start(f32[304,128]{1,0:T(8,128)S(1)} %get-tuple-element.58.refs_0_), channel_id=1, source_target_pairs={{0,32},{32,64},{64,96},{96,128},{128,160},{160,192},{192,224},{224... | collective-permute-start | bytes 466952 | tf_op jit(solution)/shard_map/ppermute | solution.py:312
  10.2 4.2 %collective-permute-start.1 = (f32[304,128]{1,0:T(8,128)S(1)}, f32[304,128]{1,0:T(8,128)S(1)}, u32[]{:S(2)}, u32[]{:S(2)}) collective-permute-start(f32[304,128]{1,0:T(8,128)S(1)} %get-tuple-element.61.refs_2_), channel_id=1, source_target_pairs={{0,32},{32,64},{64,96},{96,128},{128,160},{160,192},{192,224},{224... | collective-permute-start | bytes 466952 | tf_op jit(solution)/shard_map/ppermute | solution.py:312
  14.5 4.3 %collective-permute-start = (f32[1216,128]{1,0:T(8,128)S(1)}, f32[1216,128]{1,0:T(8,128)S(1)}, u32[]{:S(2)}, u32[]{:S(2)}) collective-permute-start(f32[1216,128]{1,0:T(8,128)S(1)} %pack.1.refs_2_), channel_id=1, source_target_pairs={{0,64},{32,96},{64,128},{96,160},{128,192},{160,224},{192,256},{22... | collective-permute-start | bytes 1867784 | tf_op jit(solution)/shard_map/ppermute | solution.py:312
  18.8 1.6 %tables.3 = (f32[1024,256]{1,0:T(8,128)S(1)}, f32[1024,256]{1,0:T(8,128)S(1)}) custom-call(bf16[4,1024,256]{2,1,0:T(8,128)(2,1)} %refs_0_.5, f32[1024,128]{1,0:T(8,128)S(1)} %get-tuple-element.63.refs_1_, f32[1216,128]{1,0:T(8,128)S(1)} %pack.1.refs_2_), custom_call_target="tpu_custom_call" | custom-call | flops 1048576 | bytes 1024 | tf_op jit(solution)/shard_map/tables/pallas_call | solution.py:40
  21.6 7.6 %collective-permute-done.3.refs_0_ = f32[304,128]{1,0:T(8,128)S(1)} collective-permute-done((f32[304,128]{1,0:T(8,128)S(1)}, f32[304,128]{1,0:T(8,128)S(1)}, u32[]{:S(2)}, u32[]{:S(2)}) %collective-permute-start.3) | collective-permute-done | bytes 155680 | tf_op jit(solution)/shard_map/ppermute | solution.py:312
  30.2 1.9 %collective-permute-start.4 = (f32[304,128]{1,0:T(8,128)S(1)}, f32[304,128]{1,0:T(8,128)S(1)}, u32[]{:S(2)}, u32[]{:S(2)}) collective-permute-start(f32[304,128]{1,0:T(8,128)S(1)} %get-tuple-element.70), channel_id=1, source_target_pairs={{0,32},{32,64},{64,96},{96,128},{128,160},{160,192},{192,224},{224... | collective-permute-start | bytes 466952 | tf_op jit(solution)/shard_map/ppermute | solution.py:312
  33.8 1.9 %collective-permute-start.2 = (f32[304,128]{1,0:T(8,128)S(1)}, f32[304,128]{1,0:T(8,128)S(1)}, u32[]{:S(2)}, u32[]{:S(2)}) collective-permute-start(f32[304,128]{1,0:T(8,128)S(1)} %get-tuple-element.66), channel_id=1, source_target_pairs={{0,32},{32,64},{64,96},{96,128},{128,160},{160,192},{192,224},{224... | collective-permute-start | bytes 466952 | tf_op jit(solution)/shard_map/ppermute | solution.py:312
  35.7 1.6 %tables.4 = (f32[1024,256]{1,0:T(8,128)S(1)}, f32[1024,256]{1,0:T(8,128)S(1)}) custom-call(bf16[4,1024,256]{2,1,0:T(8,128)(2,1)} %refs_0_.5, f32[1024,128]{1,0:T(8,128)S(1)} %get-tuple-element.63.refs_1_, bf16[1024,256]{1,0:T(8,128)(2,1)S(1)} %get-tuple-element.67.refs_2_.refs_3_), custom_call_target="tpu_custom_call" | custom-call | flops 1048576 | bytes 1024 | tf_op jit(solution)/shard_map/tables/pallas_call | solution.py:40
  38.6 10.9 %collective-permute-done.4.refs_1_ = f32[304,128]{1,0:T(8,128)S(1)} collective-permute-done((f32[304,128]{1,0:T(8,128)S(1)}, f32[304,128]{1,0:T(8,128)S(1)}, u32[]{:S(2)}, u32[]{:S(2)}) %collective-permute-start.4) | collective-permute-done | bytes 155680 | tf_op jit(solution)/shard_map/ppermute | solution.py:312
  49.4 1.2 %third_visit.2 = (f32[304,128]{1,0:T(8,128)S(1)}, f32[304,128]{1,0:T(8,128)S(1)}, f32[304,128]{1,0:T(8,128)S(1)}, bf16[1024,256]{1,0:T(8,128)(2,1)S(1)}) custom-call(f32[1216,128]{1,0:T(8,128)S(1)} %collective-permute-done.refs_0_, f32[304,128]{1,0:T(8,128)S(1)} %collective-permute-done.4.refs_1_, ...), custom_call_target="tpu_custom_call" | custom-call | flops 4294967296 | bytes 1024 | tf_op jit(solution)/shard_map/third_visit/pallas_call | solution.py:40
  50.6 1.9 %collective-permute-start.6 = (f32[304,128]{1,0:T(8,128)S(1)}, f32[304,128]{1,0:T(8,128)S(1)}, u32[]{:S(2)}, u32[]{:S(2)}) collective-permute-start(f32[304,128]{1,0:T(8,128)S(1)} %get-tuple-element.76), channel_id=1, source_target_pairs={{0,32},{32,64},{64,96},{96,128},{128,160},{160,192},{192,224},{224... | collective-permute-start | bytes 466952 | tf_op jit(solution)/shard_map/ppermute | solution.py:312
  53.7 2.1 %collective-permute-start.5 = (f32[304,128]{1,0:T(8,128)S(1)}, f32[304,128]{1,0:T(8,128)S(1)}, u32[]{:S(2)}, u32[]{:S(2)}) collective-permute-start(f32[304,128]{1,0:T(8,128)S(1)} %get-tuple-element.72), channel_id=1, source_target_pairs={{0,32},{32,64},{64,96},{96,128},{128,160},{160,192},{192,224},{224... | collective-permute-start | bytes 466952 | tf_op jit(solution)/shard_map/ppermute | solution.py:312
  55.8 1.6 %tables.5 = (f32[1024,256]{1,0:T(8,128)S(1)}, f32[1024,256]{1,0:T(8,128)S(1)}) custom-call(bf16[4,1024,256]{2,1,0:T(8,128)(2,1)} %refs_0_.5, f32[1024,128]{1,0:T(8,128)S(1)} %get-tuple-element.63.refs_1_, bf16[1024,256]{1,0:T(8,128)(2,1)S(1)} %get-tuple-element.73.refs_2_.refs_3_), custom_call_target="tpu_custom_call" | custom-call | flops 1048576 | bytes 1024 | tf_op jit(solution)/shard_map/tables/pallas_call | solution.py:40
  58.7 2.9 %collective-permute-done.6.vecs_ref = f32[304,128]{1,0:T(8,128)S(1)} collective-permute-done((f32[304,128]{1,0:T(8,128)S(1)}, f32[304,128]{1,0:T(8,128)S(1)}, u32[]{:S(2)}, u32[]{:S(2)}) %collective-permute-start.6) | collective-permute-done | bytes 155680 | tf_op jit(solution)/shard_map/ppermute | solution.py:312
  61.5 2.2 %last_first.1 = (f32[1024,384]{1,0:T(8,128)S(1)}, f32[304,128]{1,0:T(8,128)}, f32[304,128]{1,0:T(8,128)}) custom-call(f32[304,128]{1,0:T(8,128)S(1)} %collective-permute-done.6.vecs_ref, bf16[1024,384]{1,0:T(8,128)(2,1)S(1)} %get-tuple-element.52.refs_1_.refs_2_.turned_hi_ref, bf16[1024,384]{1,0:T(8,128)(2,1)S(1)} %get-tuple-element.53.refs_2_.refs_3_.turned_lo_ref, ...), custom_call_target="tpu_custom_call" | custom-call | flops 4294967296 | bytes 1024 | tf_op jit(solution)/shard_map/last_first/pallas_call | solution.py:40
  64.7 1.5 %last_second.1 = (bf16[1024,256]{1,0:T(8,128)(2,1)S(1)}, f32[640,256]{1,0:T(8,128)S(1)}, f32[640,256]{1,0:T(8,128)S(1)}) custom-call(f32[304,128]{1,0:T(8,128)S(1)} %collective-permute-done.5.refs_0_.vecs_ref, bf16[1024,384]{1,0:T(8,128)(2,1)S(1)} %get-tuple-element.52.refs_1_.refs_2_.turned_hi_ref, ...), custom_call_target="tpu_custom_call" | custom-call | flops 4294967296 | bytes 1024 | tf_op jit(solution)/shard_map/last_second/pallas_call | solution.py:40
  66.2 1.9 %collective-permute-start.7 = (f32[640,256]{1,0:T(8,128)S(1)}, f32[640,256]{1,0:T(8,128)S(1)}, u32[]{:S(2)}, u32[]{:S(2)}) collective-permute-start(f32[640,256]{1,0:T(8,128)S(1)} %get-tuple-element.87), channel_id=1, source_target_pairs={{0,1},{1,0},{2,3},{3,2},{4,5},{5,4},{6,7},{7,6},{8,9},{9,8},{10,11... | collective-permute-start | bytes 1966088 | tf_op jit(solution)/shard_map/ppermute | solution.py:317
  68.1 1.2 %last_columns.1 = (f32[304,128]{1,0:T(8,128)}, f32[304,128]{1,0:T(8,128)}) custom-call(f32[304,128]{1,0:T(8,128)S(1)} %collective-permute-done.5.refs_0_.vecs_ref, bf16[300,1024]{1,0:T(8,128)(2,1)S(1)} %get-tuple-element.54.refs_3_.refs_4_.hi_ref, bf16[300,1024]{1,0:T(8,128)(2,1)S(1)} %get-tuple-element.55.refs_4_.refs_5_.lo_ref, ...), custom_call_target="tpu_custom_call" | custom-call | flops 1048576 | bytes 1024 | tf_op jit(solution)/shard_map/last_columns/pallas_call | solution.py:40
  71.1 7.6 %all-to-all-start = ((f32[16,40,256]{2,1,0:T(8,128)}), f32[16,40,256]{2,1,0:T(8,128)S(1)}, u32[]{:S(2)}, u32[]{:S(2)}) async-start(f32[16,40,256]{2,1,0:T(8,128)} %sum.1), calls=%async_computation | async-start | bytes 1310720 | tf_op jit(solution)/shard_map/all_to_all | solution.py:450
  78.7 1.9 %collective-permute-start.8 = (f32[608,128]{1,0:T(8,128)S(1)}, f32[608,128]{1,0:T(8,128)S(1)}, u32[]{:S(2)}, u32[]{:S(2)}) collective-permute-start(f32[608,128]{1,0:T(8,128)S(1)} %get-tuple-element.95), channel_id=1, source_target_pairs={{0,32},{32,64},{64,96},{96,128},{128,160},{160,192},{192,224},{224... | collective-permute-start | bytes 933896 | tf_op jit(solution)/shard_map/ppermute | solution.py:312
  80.6 1.2 %shares.1 = (f32[32,300]{1,0:T(8,128)S(1)}, f32[32,300]{1,0:T(8,128)S(1)}) custom-call(f32[300,1024]{1,0:T(8,128)} %row_hbm.3, f32[300,1024]{1,0:T(8,128)} %acc_hbm.1), custom_call_target="tpu_custom_call" | custom-call | flops 4294967296 | bytes 1024 | tf_op jit(solution)/shard_map/shares/pallas_call | solution.py:40
  81.8 14.2 %collective-permute-done.8.moments_ref = f32[608,128]{1,0:T(8,128)S(1)} collective-permute-done((f32[608,128]{1,0:T(8,128)S(1)}, f32[608,128]{1,0:T(8,128)S(1)}, u32[]{:S(2)}, u32[]{:S(2)}) %collective-permute-start.8) | collective-permute-done | bytes 311328 | tf_op jit(solution)/shard_map/ppermute | solution.py:312
  96.0 2.1 %last_update.1 = (f32[300,256]{1,0:T(8,128)}, f32[300,256]{1,0:T(8,128)}) custom-call(f32[304,128]{1,0:T(8,128)} %get-tuple-element.92.kept_a_hbm, f32[304,128]{1,0:T(8,128)} %get-tuple-element.85.kept_ref.kept_b_hbm, f32[304,128]{1,0:T(8,128)} %get-tuple-element.93.col_grad_a_hbm, f32[304,128]{1,0:T(8,128)} %get-tuple-element.94.col_grad_b_hbm, ...), custom_call_target="tpu_custom_call" | custom-call | flops 1048576 | bytes 1024 | tf_op jit(solution)/shard_map/last_update/pallas_call | solution.py:40
  (17 shorter events, 13.0 us)
Async XLA Ops:
  4.2 25.0 %collective-permute-start.3 = (f32[304,128]{1,0:T(8,128)S(1)}, f32[304,128]{1,0:T(8,128)S(1)}, u32[]{:S(2)}, u32[]{:S(2)}) collective-permute-start(f32[304,128]{1,0:T(8,128)S(1)} %get-tuple-element.58.refs_0_), channel_id=1, source_target_pairs={{0,32},{32,64},{64,96},{96,128},{128,160},{160,192},{192,224},{224... | collective-permute-start | bytes 466952 | tf_op jit(solution)/shard_map/ppermute | solution.py:312
  10.2 22.5 %collective-permute-start.1 = (f32[304,128]{1,0:T(8,128)S(1)}, f32[304,128]{1,0:T(8,128)S(1)}, u32[]{:S(2)}, u32[]{:S(2)}) collective-permute-start(f32[304,128]{1,0:T(8,128)S(1)} %get-tuple-element.61.refs_2_), channel_id=1, source_target_pairs={{0,32},{32,64},{64,96},{96,128},{128,160},{160,192},{192,224},{224... | collective-permute-start | bytes 466952 | tf_op jit(solution)/shard_map/ppermute | solution.py:312
  14.5 34.9 %collective-permute-start = (f32[1216,128]{1,0:T(8,128)S(1)}, f32[1216,128]{1,0:T(8,128)S(1)}, u32[]{:S(2)}, u32[]{:S(2)}) collective-permute-start(f32[1216,128]{1,0:T(8,128)S(1)} %pack.1.refs_2_), channel_id=1, source_target_pairs={{0,64},{32,96},{64,128},{96,160},{128,192},{160,224},{192,256},{22... | collective-permute-start | bytes 1867784 | tf_op jit(solution)/shard_map/ppermute | solution.py:312
  30.2 19.2 %collective-permute-start.4 = (f32[304,128]{1,0:T(8,128)S(1)}, f32[304,128]{1,0:T(8,128)S(1)}, u32[]{:S(2)}, u32[]{:S(2)}) collective-permute-start(f32[304,128]{1,0:T(8,128)S(1)} %get-tuple-element.70), channel_id=1, source_target_pairs={{0,32},{32,64},{64,96},{96,128},{128,160},{160,192},{192,224},{224... | collective-permute-start | bytes 466952 | tf_op jit(solution)/shard_map/ppermute | solution.py:312
  33.8 18.7 %collective-permute-start.2 = (f32[304,128]{1,0:T(8,128)S(1)}, f32[304,128]{1,0:T(8,128)S(1)}, u32[]{:S(2)}, u32[]{:S(2)}) collective-permute-start(f32[304,128]{1,0:T(8,128)S(1)} %get-tuple-element.66), channel_id=1, source_target_pairs={{0,32},{32,64},{64,96},{96,128},{128,160},{160,192},{192,224},{224... | collective-permute-start | bytes 466952 | tf_op jit(solution)/shard_map/ppermute | solution.py:312
  50.6 10.9 %collective-permute-start.6 = (f32[304,128]{1,0:T(8,128)S(1)}, f32[304,128]{1,0:T(8,128)S(1)}, u32[]{:S(2)}, u32[]{:S(2)}) collective-permute-start(f32[304,128]{1,0:T(8,128)S(1)} %get-tuple-element.76), channel_id=1, source_target_pairs={{0,32},{32,64},{64,96},{96,128},{128,160},{160,192},{192,224},{224... | collective-permute-start | bytes 466952 | tf_op jit(solution)/shard_map/ppermute | solution.py:312
  53.7 11.0 %collective-permute-start.5 = (f32[304,128]{1,0:T(8,128)S(1)}, f32[304,128]{1,0:T(8,128)S(1)}, u32[]{:S(2)}, u32[]{:S(2)}) collective-permute-start(f32[304,128]{1,0:T(8,128)S(1)} %get-tuple-element.72), channel_id=1, source_target_pairs={{0,32},{32,64},{64,96},{96,128},{128,160},{160,192},{192,224},{224... | collective-permute-start | bytes 466952 | tf_op jit(solution)/shard_map/ppermute | solution.py:312
  66.2 4.0 %collective-permute-start.7 = (f32[640,256]{1,0:T(8,128)S(1)}, f32[640,256]{1,0:T(8,128)S(1)}, u32[]{:S(2)}, u32[]{:S(2)}) collective-permute-start(f32[640,256]{1,0:T(8,128)S(1)} %get-tuple-element.87), channel_id=1, source_target_pairs={{0,1},{1,0},{2,3},{3,2},{4,5},{5,4},{6,7},{7,6},{8,9},{9,8},{10,11... | collective-permute-start | bytes 1966088 | tf_op jit(solution)/shard_map/ppermute | solution.py:317
  71.1 27.1 %all-to-all-start = ((f32[16,40,256]{2,1,0:T(8,128)}), f32[16,40,256]{2,1,0:T(8,128)S(1)}, u32[]{:S(2)}, u32[]{:S(2)}) async-start(f32[16,40,256]{2,1,0:T(8,128)} %sum.1), calls=%async_computation | async-start | bytes 1310720 | tf_op jit(solution)/shard_map/all_to_all | solution.py:450
  78.7 17.3 %collective-permute-start.8 = (f32[608,128]{1,0:T(8,128)S(1)}, f32[608,128]{1,0:T(8,128)S(1)}, u32[]{:S(2)}, u32[]{:S(2)}) collective-permute-start(f32[608,128]{1,0:T(8,128)S(1)} %get-tuple-element.95), channel_id=1, source_target_pairs={{0,32},{32,64},{64,96},{96,128},{128,160},{160,192},{192,224},{224... | collective-permute-start | bytes 933896 | tf_op jit(solution)/shard_map/ppermute | solution.py:312

commit v6 on v5

--- a/solution.py
+++ b/solution.py
@@ -286,7 +286,7 @@
                 ref[slot * PACK + SHARE : (slot + 1) * PACK, pair * 128 : (pair + 1) * 128] = jnp.where(left, upper, lower)
 
 
-def sum_body(kept_ref, keep_ref, got_ref, out_ref):
+def sum_body(kept_ref, moments_ref, keep_ref, got_ref, out_ref):
     for slot in range(16):
         rows = slice(slot * PACK, (slot + 1) * PACK)
         out_ref[slot] = keep_ref[rows, :] + got_ref[rows, :]
@@ -423,7 +423,7 @@
         keep_columns,
         (remote(PADW, HALF), remote(PADW, HALF)),
         (vecs[1], hi, lo, grad_b),
-        flops=1 << 20,
+        flops=1 << 33,
     )
     small = pltpu.VMEM((PADW, HALF), f32)
     new_col_emb, new_col_acc = call(
@@ -445,7 +445,7 @@
         far=2,
     )
     got = swapped(send, 1)
-    share = call("sum", sum_body, near(16, PACK, 256), (kept_b, keep, got), far=1)
+    share = call("sum", sum_body, near(16, PACK, 256), (kept_b, moments, keep, got), far=1)
     chips = [[2 * chip + core for chip in range(16)] for core in range(2)]
     parts = lax.all_to_all(share, "grp", 0, 0, axis_index_groups=chips)
 

time: 99.5 us -> 99.9 us (level)
    all_to_all x1, waiting for transfers between devices: 0.01 us -> 14.9 us  [shards(): parts = lax.all_to_all(share, 'grp', 0, 0, axis_index_groups=chips)]
    ppermute x8, waiting for transfers between devices: 37 us -> 23 us  [shifted(): lax.ppermute(value, 'blk', [(source, (source + steps) % count) for source...]
  transfers between devices with their start and end apart: 10 -> 10, of which waited for: 7 -> 8; matrix products, arithmetic and copies ran while one was open for 0% -> 0% of each run, Pallas kernels for 21% -> 22%
where the time goes in v6:
time: 99.9 us; the launch traced here: 99.2 us
  waiting for transfers between devices  38.3 us (38%)
  starting transfers between devices  32.7 us (33%)
  Pallas kernels  27.4 us (27%)
    pallas_call x21, Pallas kernels, call(): pl.pallas_call(body, out_shape=out, in_specs=specs, out_specs=jax.tree.ma...  27.4 us
    ppermute x8, starting transfers between devices, shifted(): lax.ppermute(value, 'blk', [(source, (source + steps) % count) for source...  23.2 us
    ppermute x8, waiting for transfers between devices, shifted(): lax.ppermute(value, 'blk', [(source, (source + steps) % count) for source...  23 us
    all_to_all x1, waiting for transfers between devices, shards(): parts = lax.all_to_all(share, 'grp', 0, 0, axis_index_groups=chips)  14.9 us
    all_to_all x1, starting transfers between devices, shards(): parts = lax.all_to_all(share, 'grp', 0, 0, axis_index_groups=chips)  7.59 us
  transfers between devices with their start and end apart: 10, of which 8 were waited for; matrix products, arithmetic and copies ran while one was open for 0% of the time, Pallas kernels for 22%

profile of v6, /device:TPU:8, one launch (start us, length us, event | category | flops | bytes accessed | tf_op | source)
XLA Modules:
  0.0 99.2 jit_solution(11388900717738269345)
XLA Ops:
  0.6 2.5 %prep.1 = (bf16[300,1024]{1,0:T(8,128)(2,1)S(1)}, bf16[300,1024]{1,0:T(8,128)(2,1)S(1)}, bf16[1024,384]{1,0:T(8,128)(2,1)S(1)}, bf16[1024,384]{1,0:T(8,128)(2,1)...) custom-call(f32[300,1024]{1,0:T(8,128)} %row_hbm.3, ...), custom_call_target="tpu_custom_call" | custom-call | flops 4294967296 | bytes 1024 | tf_op jit(solution)/shard_map/prep/pallas_call | solution.py:40
  4.2 4.9 %collective-permute-start.3 = (f32[304,128]{1,0:T(8,128)S(1)}, f32[304,128]{1,0:T(8,128)S(1)}, u32[]{:S(2)}, u32[]{:S(2)}) collective-permute-start(f32[304,128]{1,0:T(8,128)S(1)} %get-tuple-element.58.refs_0_), channel_id=1, source_target_pairs={{0,32},{32,64},{64,96},{96,128},{128,160},{160,192},{192,224},{224... | collective-permute-start | bytes 466952 | tf_op jit(solution)/shard_map/ppermute | solution.py:312
  10.3 4.2 %collective-permute-start.1 = (f32[304,128]{1,0:T(8,128)S(1)}, f32[304,128]{1,0:T(8,128)S(1)}, u32[]{:S(2)}, u32[]{:S(2)}) collective-permute-start(f32[304,128]{1,0:T(8,128)S(1)} %get-tuple-element.61.refs_2_), channel_id=1, source_target_pairs={{0,32},{32,64},{64,96},{96,128},{128,160},{160,192},{192,224},{224... | collective-permute-start | bytes 466952 | tf_op jit(solution)/shard_map/ppermute | solution.py:312
  14.6 4.3 %collective-permute-start = (f32[1216,128]{1,0:T(8,128)S(1)}, f32[1216,128]{1,0:T(8,128)S(1)}, u32[]{:S(2)}, u32[]{:S(2)}) collective-permute-start(f32[1216,128]{1,0:T(8,128)S(1)} %pack.1.refs_2_), channel_id=1, source_target_pairs={{0,64},{32,96},{64,128},{96,160},{128,192},{160,224},{192,256},{22... | collective-permute-start | bytes 1867784 | tf_op jit(solution)/shard_map/ppermute | solution.py:312
  18.9 1.6 %tables.3 = (f32[1024,256]{1,0:T(8,128)S(1)}, f32[1024,256]{1,0:T(8,128)S(1)}) custom-call(bf16[4,1024,256]{2,1,0:T(8,128)(2,1)} %refs_0_.5, f32[1024,128]{1,0:T(8,128)S(1)} %get-tuple-element.63.refs_1_, f32[1216,128]{1,0:T(8,128)S(1)} %pack.1.refs_2_), custom_call_target="tpu_custom_call" | custom-call | flops 1048576 | bytes 1024 | tf_op jit(solution)/shard_map/tables/pallas_call | solution.py:40
  21.6 7.5 %collective-permute-done.3.refs_0_ = f32[304,128]{1,0:T(8,128)S(1)} collective-permute-done((f32[304,128]{1,0:T(8,128)S(1)}, f32[304,128]{1,0:T(8,128)S(1)}, u32[]{:S(2)}, u32[]{:S(2)}) %collective-permute-start.3) | collective-permute-done | bytes 155680 | tf_op jit(solution)/shard_map/ppermute | solution.py:312
  30.2 1.9 %collective-permute-start.4 = (f32[304,128]{1,0:T(8,128)S(1)}, f32[304,128]{1,0:T(8,128)S(1)}, u32[]{:S(2)}, u32[]{:S(2)}) collective-permute-start(f32[304,128]{1,0:T(8,128)S(1)} %get-tuple-element.70), channel_id=1, source_target_pairs={{0,32},{32,64},{64,96},{96,128},{128,160},{160,192},{192,224},{224... | collective-permute-start | bytes 466952 | tf_op jit(solution)/shard_map/ppermute | solution.py:312
  33.9 1.9 %collective-permute-start.2 = (f32[304,128]{1,0:T(8,128)S(1)}, f32[304,128]{1,0:T(8,128)S(1)}, u32[]{:S(2)}, u32[]{:S(2)}) collective-permute-start(f32[304,128]{1,0:T(8,128)S(1)} %get-tuple-element.66), channel_id=1, source_target_pairs={{0,32},{32,64},{64,96},{96,128},{128,160},{160,192},{192,224},{224... | collective-permute-start | bytes 466952 | tf_op jit(solution)/shard_map/ppermute | solution.py:312
  35.8 1.6 %tables.4 = (f32[1024,256]{1,0:T(8,128)S(1)}, f32[1024,256]{1,0:T(8,128)S(1)}) custom-call(bf16[4,1024,256]{2,1,0:T(8,128)(2,1)} %refs_0_.5, f32[1024,128]{1,0:T(8,128)S(1)} %get-tuple-element.63.refs_1_, bf16[1024,256]{1,0:T(8,128)(2,1)S(1)} %get-tuple-element.67.refs_2_.refs_3_), custom_call_target="tpu_custom_call" | custom-call | flops 1048576 | bytes 1024 | tf_op jit(solution)/shard_map/tables/pallas_call | solution.py:40
  38.6 10.9 %collective-permute-done.4.refs_1_ = f32[304,128]{1,0:T(8,128)S(1)} collective-permute-done((f32[304,128]{1,0:T(8,128)S(1)}, f32[304,128]{1,0:T(8,128)S(1)}, u32[]{:S(2)}, u32[]{:S(2)}) %collective-permute-start.4) | collective-permute-done | bytes 155680 | tf_op jit(solution)/shard_map/ppermute | solution.py:312
  49.5 1.2 %third_visit.2 = (f32[304,128]{1,0:T(8,128)S(1)}, f32[304,128]{1,0:T(8,128)S(1)}, f32[304,128]{1,0:T(8,128)S(1)}, bf16[1024,256]{1,0:T(8,128)(2,1)S(1)}) custom-call(f32[1216,128]{1,0:T(8,128)S(1)} %collective-permute-done.refs_0_, f32[304,128]{1,0:T(8,128)S(1)} %collective-permute-done.4.refs_1_, ...), custom_call_target="tpu_custom_call" | custom-call | flops 4294967296 | bytes 1024 | tf_op jit(solution)/shard_map/third_visit/pallas_call | solution.py:40
  50.7 1.9 %collective-permute-start.6 = (f32[304,128]{1,0:T(8,128)S(1)}, f32[304,128]{1,0:T(8,128)S(1)}, u32[]{:S(2)}, u32[]{:S(2)}) collective-permute-start(f32[304,128]{1,0:T(8,128)S(1)} %get-tuple-element.76), channel_id=1, source_target_pairs={{0,32},{32,64},{64,96},{96,128},{128,160},{160,192},{192,224},{224... | collective-permute-start | bytes 466952 | tf_op jit(solution)/shard_map/ppermute | solution.py:312
  52.6 1.2 %third_visit.3 = (f32[304,128]{1,0:T(8,128)S(1)}, f32[304,128]{1,0:T(8,128)S(1)}, f32[608,128]{1,0:T(8,128)S(1)}, bf16[1024,256]{1,0:T(8,128)(2,1)S(1)}) custom-call(f32[1216,128]{1,0:T(8,128)S(1)} %collective-permute-done.refs_0_, f32[304,128]{1,0:T(8,128)S(1)} %collective-permute-done.2.refs_1_, ...), custom_call_target="tpu_custom_call" | custom-call | flops 4294967296 | bytes 1024 | tf_op jit(solution)/shard_map/third_visit/pallas_call | solution.py:40
  53.8 1.9 %collective-permute-start.5 = (f32[304,128]{1,0:T(8,128)S(1)}, f32[304,128]{1,0:T(8,128)S(1)}, u32[]{:S(2)}, u32[]{:S(2)}) collective-permute-start(f32[304,128]{1,0:T(8,128)S(1)} %get-tuple-element.72), channel_id=1, source_target_pairs={{0,32},{32,64},{64,96},{96,128},{128,160},{160,192},{192,224},{224... | collective-permute-start | bytes 466952 | tf_op jit(solution)/shard_map/ppermute | solution.py:312
  55.7 2.1 %collective-permute-start.7 = (f32[608,128]{1,0:T(8,128)S(1)}, f32[608,128]{1,0:T(8,128)S(1)}, u32[]{:S(2)}, u32[]{:S(2)}) collective-permute-start(f32[608,128]{1,0:T(8,128)S(1)} %get-tuple-element.86), channel_id=1, source_target_pairs={{0,32},{32,64},{64,96},{96,128},{128,160},{160,192},{192,224},{224... | collective-permute-start | bytes 933896 | tf_op jit(solution)/shard_map/ppermute | solution.py:312
  57.8 1.6 %tables.5 = (f32[1024,256]{1,0:T(8,128)S(1)}, f32[1024,256]{1,0:T(8,128)S(1)}) custom-call(bf16[4,1024,256]{2,1,0:T(8,128)(2,1)} %refs_0_.5, f32[1024,128]{1,0:T(8,128)S(1)} %get-tuple-element.63.refs_1_, bf16[1024,256]{1,0:T(8,128)(2,1)S(1)} %get-tuple-element.73.refs_2_.refs_3_), custom_call_target="tpu_custom_call" | custom-call | flops 1048576 | bytes 1024 | tf_op jit(solution)/shard_map/tables/pallas_call | solution.py:40
  61.6 2.2 %last_first.1 = (f32[1024,384]{1,0:T(8,128)S(1)}, f32[304,128]{1,0:T(8,128)}, f32[304,128]{1,0:T(8,128)}) custom-call(f32[304,128]{1,0:T(8,128)S(1)} %collective-permute-done.6.vecs_ref, bf16[1024,384]{1,0:T(8,128)(2,1)S(1)} %get-tuple-element.52.refs_1_.refs_2_.turned_hi_ref, bf16[1024,384]{1,0:T(8,128)(2,1)S(1)} %get-tuple-element.53.refs_2_.refs_3_.turned_lo_ref, ...), custom_call_target="tpu_custom_call" | custom-call | flops 4294967296 | bytes 1024 | tf_op jit(solution)/shard_map/last_first/pallas_call | solution.py:40
  63.8 2.4 %collective-permute-done.5.refs_0_.vecs_ref = f32[304,128]{1,0:T(8,128)S(1)} collective-permute-done((f32[304,128]{1,0:T(8,128)S(1)}, f32[304,128]{1,0:T(8,128)S(1)}, u32[]{:S(2)}, u32[]{:S(2)}) %collective-permute-start.5) | collective-permute-done | bytes 155680 | tf_op jit(solution)/shard_map/ppermute | solution.py:312
  66.2 1.5 %last_second.1 = (bf16[1024,256]{1,0:T(8,128)(2,1)S(1)}, f32[640,256]{1,0:T(8,128)S(1)}, f32[640,256]{1,0:T(8,128)S(1)}) custom-call(f32[304,128]{1,0:T(8,128)S(1)} %collective-permute-done.5.refs_0_.vecs_ref, bf16[1024,384]{1,0:T(8,128)(2,1)S(1)} %get-tuple-element.52.refs_1_.refs_2_.turned_hi_ref, ...), custom_call_target="tpu_custom_call" | custom-call | flops 4294967296 | bytes 1024 | tf_op jit(solution)/shard_map/last_second/pallas_call | solution.py:40
  67.7 1.9 %collective-permute-start.8 = (f32[640,256]{1,0:T(8,128)S(1)}, f32[640,256]{1,0:T(8,128)S(1)}, u32[]{:S(2)}, u32[]{:S(2)}) collective-permute-start(f32[640,256]{1,0:T(8,128)S(1)} %get-tuple-element.88), channel_id=1, source_target_pairs={{0,1},{1,0},{2,3},{3,2},{4,5},{5,4},{6,7},{7,6},{8,9},{9,8},{10,11... | collective-permute-start | bytes 1966088 | tf_op jit(solution)/shard_map/ppermute | solution.py:317
  72.6 7.6 %all-to-all-start = ((f32[16,40,256]{2,1,0:T(8,128)}), f32[16,40,256]{2,1,0:T(8,128)S(1)}, u32[]{:S(2)}, u32[]{:S(2)}) async-start(f32[16,40,256]{2,1,0:T(8,128)} %sum.1), calls=%async_computation | async-start | bytes 1310720 | tf_op jit(solution)/shard_map/all_to_all | solution.py:450
  80.2 1.2 %shares.1 = (f32[32,300]{1,0:T(8,128)S(1)}, f32[32,300]{1,0:T(8,128)S(1)}) custom-call(f32[300,1024]{1,0:T(8,128)} %row_hbm.3, f32[300,1024]{1,0:T(8,128)} %acc_hbm.1), custom_call_target="tpu_custom_call" | custom-call | flops 4294967296 | bytes 1024 | tf_op jit(solution)/shard_map/shares/pallas_call | solution.py:40
  81.4 2.1 %last_update.1 = (f32[300,256]{1,0:T(8,128)}, f32[300,256]{1,0:T(8,128)}) custom-call(f32[304,128]{1,0:T(8,128)} %get-tuple-element.93.kept_a_hbm, f32[304,128]{1,0:T(8,128)} %get-tuple-element.85.kept_ref.kept_b_hbm, f32[304,128]{1,0:T(8,128)} %get-tuple-element.94.col_grad_a_hbm, f32[304,128]{1,0:T(8,128)} %get-tuple-element.95.col_grad_b_hbm, ...), custom_call_target="tpu_custom_call" | custom-call | flops 1048576 | bytes 1024 | tf_op jit(solution)/shard_map/last_update/pallas_call | solution.py:40
  83.6 14.9 %all-to-all-done.parts_ref = f32[16,40,256]{2,1,0:T(8,128)S(1)} async-done(((f32[16,40,256]{2,1,0:T(8,128)}), f32[16,40,256]{2,1,0:T(8,128)S(1)}, u32[]{:S(2)}, u32[]{:S(2)}) %all-to-all-start) | async-done | bytes 655392 | tf_op jit(solution)/shard_map/all_to_all | solution.py:450
  (17 shorter events, 13.2 us)
Async XLA Ops:
  4.2 24.9 %collective-permute-start.3 = (f32[304,128]{1,0:T(8,128)S(1)}, f32[304,128]{1,0:T(8,128)S(1)}, u32[]{:S(2)}, u32[]{:S(2)}) collective-permute-start(f32[304,128]{1,0:T(8,128)S(1)} %get-tuple-element.58.refs_0_), channel_id=1, source_target_pairs={{0,32},{32,64},{64,96},{96,128},{128,160},{160,192},{192,224},{224... | collective-permute-start | bytes 466952 | tf_op jit(solution)/shard_map/ppermute | solution.py:312
  10.3 22.5 %collective-permute-start.1 = (f32[304,128]{1,0:T(8,128)S(1)}, f32[304,128]{1,0:T(8,128)S(1)}, u32[]{:S(2)}, u32[]{:S(2)}) collective-permute-start(f32[304,128]{1,0:T(8,128)S(1)} %get-tuple-element.61.refs_2_), channel_id=1, source_target_pairs={{0,32},{32,64},{64,96},{96,128},{128,160},{160,192},{192,224},{224... | collective-permute-start | bytes 466952 | tf_op jit(solution)/shard_map/ppermute | solution.py:312
  14.6 34.9 %collective-permute-start = (f32[1216,128]{1,0:T(8,128)S(1)}, f32[1216,128]{1,0:T(8,128)S(1)}, u32[]{:S(2)}, u32[]{:S(2)}) collective-permute-start(f32[1216,128]{1,0:T(8,128)S(1)} %pack.1.refs_2_), channel_id=1, source_target_pairs={{0,64},{32,96},{64,128},{96,160},{128,192},{160,224},{192,256},{22... | collective-permute-start | bytes 1867784 | tf_op jit(solution)/shard_map/ppermute | solution.py:312
  30.2 19.2 %collective-permute-start.4 = (f32[304,128]{1,0:T(8,128)S(1)}, f32[304,128]{1,0:T(8,128)S(1)}, u32[]{:S(2)}, u32[]{:S(2)}) collective-permute-start(f32[304,128]{1,0:T(8,128)S(1)} %get-tuple-element.70), channel_id=1, source_target_pairs={{0,32},{32,64},{64,96},{96,128},{128,160},{160,192},{192,224},{224... | collective-permute-start | bytes 466952 | tf_op jit(solution)/shard_map/ppermute | solution.py:312
  33.9 18.7 %collective-permute-start.2 = (f32[304,128]{1,0:T(8,128)S(1)}, f32[304,128]{1,0:T(8,128)S(1)}, u32[]{:S(2)}, u32[]{:S(2)}) collective-permute-start(f32[304,128]{1,0:T(8,128)S(1)} %get-tuple-element.66), channel_id=1, source_target_pairs={{0,32},{32,64},{64,96},{96,128},{128,160},{160,192},{192,224},{224... | collective-permute-start | bytes 466952 | tf_op jit(solution)/shard_map/ppermute | solution.py:312
  50.7 10.9 %collective-permute-start.6 = (f32[304,128]{1,0:T(8,128)S(1)}, f32[304,128]{1,0:T(8,128)S(1)}, u32[]{:S(2)}, u32[]{:S(2)}) collective-permute-start(f32[304,128]{1,0:T(8,128)S(1)} %get-tuple-element.76), channel_id=1, source_target_pairs={{0,32},{32,64},{64,96},{96,128},{128,160},{160,192},{192,224},{224... | collective-permute-start | bytes 466952 | tf_op jit(solution)/shard_map/ppermute | solution.py:312
  53.8 12.5 %collective-permute-start.5 = (f32[304,128]{1,0:T(8,128)S(1)}, f32[304,128]{1,0:T(8,128)S(1)}, u32[]{:S(2)}, u32[]{:S(2)}) collective-permute-start(f32[304,128]{1,0:T(8,128)S(1)} %get-tuple-element.72), channel_id=1, source_target_pairs={{0,32},{32,64},{64,96},{96,128},{128,160},{160,192},{192,224},{224... | collective-permute-start | bytes 466952 | tf_op jit(solution)/shard_map/ppermute | solution.py:312
  55.7 15.7 %collective-permute-start.7 = (f32[608,128]{1,0:T(8,128)S(1)}, f32[608,128]{1,0:T(8,128)S(1)}, u32[]{:S(2)}, u32[]{:S(2)}) collective-permute-start(f32[608,128]{1,0:T(8,128)S(1)} %get-tuple-element.86), channel_id=1, source_target_pairs={{0,32},{32,64},{64,96},{96,128},{128,160},{160,192},{192,224},{224... | collective-permute-start | bytes 933896 | tf_op jit(solution)/shard_map/ppermute | solution.py:312
  67.7 4.0 %collective-permute-start.8 = (f32[640,256]{1,0:T(8,128)S(1)}, f32[640,256]{1,0:T(8,128)S(1)}, u32[]{:S(2)}, u32[]{:S(2)}) collective-permute-start(f32[640,256]{1,0:T(8,128)S(1)} %get-tuple-element.88), channel_id=1, source_target_pairs={{0,1},{1,0},{2,3},{3,2},{4,5},{5,4},{6,7},{7,6},{8,9},{9,8},{10,11... | collective-permute-start | bytes 1966088 | tf_op jit(solution)/shard_map/ppermute | solution.py:317
  72.6 25.9 %all-to-all-start = ((f32[16,40,256]{2,1,0:T(8,128)}), f32[16,40,256]{2,1,0:T(8,128)S(1)}, u32[]{:S(2)}, u32[]{:S(2)}) async-start(f32[16,40,256]{2,1,0:T(8,128)} %sum.1), calls=%async_computation | async-start | bytes 1310720 | tf_op jit(solution)/shard_map/all_to_all | solution.py:450

commit v7 on v5

--- a/solution.py
+++ b/solution.py
@@ -289,7 +289,12 @@
 def sum_body(kept_ref, keep_ref, got_ref, out_ref):
     for slot in range(16):
         rows = slice(slot * PACK, (slot + 1) * PACK)
-        out_ref[slot] = keep_ref[rows, :] + got_ref[rows, :]
+        out_ref[2 * (slot >> 3) + (slot & 1), (slot >> 1) & 3] = keep_ref[rows, :] + got_ref[rows, :]
+
+
+def four_body(parts_ref, out_ref):
+    for at in range(4):
+        out_ref[at] = (parts_ref[0, at] + parts_ref[1, at]) + (parts_ref[2, at] + parts_ref[3, at])
 
 
 def finish_body(parts_ref, vecs_ref, moment_ref, new_ref, new_moment_ref, grad_ref):
@@ -445,9 +450,14 @@
         far=2,
     )
     got = swapped(send, 1)
-    share = call("sum", sum_body, near(16, PACK, 256), (kept_b, keep, got), far=1)
-    chips = [[2 * chip + core for chip in range(16)] for core in range(2)]
-    parts = lax.all_to_all(share, "grp", 0, 0, axis_index_groups=chips)
+    share = call("sum", sum_body, near(4, 4, PACK, 256), (kept_b, keep, got), far=1)
+    spots = [(along_x, low, high, core) for along_x in range(2) for low in range(2) for high in range(4) for core in range(2)]
+    number = {spot: spot[0] * 16 + spot[2] * 4 + spot[1] * 2 + spot[3] for spot in spots}
+    squares = [[number[x, low, high, core] for x in range(2) for low in range(2)] for high in range(4) for core in range(2)]
+    lines = [[number[x, low, high, core] for high in range(4)] for x in range(2) for low in range(2) for core in range(2)]
+    share = lax.all_to_all(share, "grp", 0, 0, axis_index_groups=squares)
+    share = call("four", four_body, near(4, PACK, 256), (share,))
+    parts = lax.all_to_all(share, "grp", 0, 0, axis_index_groups=lines)
 
     new_rows, new_row_moment = call(
         "finish",

time: 99.5 us -> 103 us (1.035)
  the two profiles are of different devices: /device:TPU:8 before, /device:TPU:2 now
where the time goes in v7:
time: 103 us; the launch traced here: 102 us
  starting transfers between devices  37.1 us (36%)
  waiting for transfers between devices  36.3 us (35%)
  Pallas kernels  28.1 us (27%)
    pallas_call x22, Pallas kernels, call(): pl.pallas_call(body, out_shape=out, in_specs=specs, out_specs=jax.tree.ma...  28.1 us
    ppermute x8, starting transfers between devices, shifted(): lax.ppermute(value, 'blk', [(source, (source + steps) % count) for source...  23.2 us
    ppermute x8, waiting for transfers between devices, shifted(): lax.ppermute(value, 'blk', [(source, (source + steps) % count) for source...  21.9 us
    all_to_all x1, waiting for transfers between devices, shards(): share = lax.all_to_all(share, 'grp', 0, 0, axis_index_groups=squares)  7.53 us
    all_to_all x1, starting transfers between devices, shards(): parts = lax.all_to_all(share, 'grp', 0, 0, axis_index_groups=lines)  7.09 us
    all_to_all x1, waiting for transfers between devices, shards(): parts = lax.all_to_all(share, 'grp', 0, 0, axis_index_groups=lines)  5.94 us
    all_to_all x1, starting transfers between devices, shards(): share = lax.all_to_all(share, 'grp', 0, 0, axis_index_groups=squares)  4.89 us
  transfers between devices with their start and end apart: 11, of which 8 were waited for; matrix products, arithmetic and copies ran while one was open for 0% of the time, Pallas kernels for 21%

profile of v7, /device:TPU:2, one launch (start us, length us, event | category | flops | bytes accessed | tf_op | source)
XLA Modules:
  0.0 102.3 jit_solution(5593020619861466799)
XLA Ops:
  0.6 2.5 %prep.1 = (bf16[300,1024]{1,0:T(8,128)(2,1)S(1)}, bf16[300,1024]{1,0:T(8,128)(2,1)S(1)}, bf16[1024,384]{1,0:T(8,128)(2,1)S(1)}, bf16[1024,384]{1,0:T(8,128)(2,1)...) custom-call(f32[300,1024]{1,0:T(8,128)} %row_hbm.3, ...), custom_call_target="tpu_custom_call" | custom-call | flops 4294967296 | bytes 1024 | tf_op jit(solution)/shard_map/prep/pallas_call | solution.py:40
  4.2 4.0 %collective-permute-start.3 = (f32[304,128]{1,0:T(8,128)S(1)}, f32[304,128]{1,0:T(8,128)S(1)}, u32[]{:S(2)}, u32[]{:S(2)}) collective-permute-start(f32[304,128]{1,0:T(8,128)S(1)} %get-tuple-element.58.refs_0_), channel_id=1, source_target_pairs={{0,32},{32,64},{64,96},{96,128},{128,160},{160,192},{192,224},{224... | collective-permute-start | bytes 466952 | tf_op jit(solution)/shard_map/ppermute | solution.py:317
  9.3 5.1 %collective-permute-start.1 = (f32[304,128]{1,0:T(8,128)S(1)}, f32[304,128]{1,0:T(8,128)S(1)}, u32[]{:S(2)}, u32[]{:S(2)}) collective-permute-start(f32[304,128]{1,0:T(8,128)S(1)} %get-tuple-element.61.refs_2_), channel_id=1, source_target_pairs={{0,32},{32,64},{64,96},{96,128},{128,160},{160,192},{192,224},{224... | collective-permute-start | bytes 466952 | tf_op jit(solution)/shard_map/ppermute | solution.py:317
  14.5 4.3 %collective-permute-start = (f32[1216,128]{1,0:T(8,128)S(1)}, f32[1216,128]{1,0:T(8,128)S(1)}, u32[]{:S(2)}, u32[]{:S(2)}) collective-permute-start(f32[1216,128]{1,0:T(8,128)S(1)} %pack.1.refs_2_), channel_id=1, source_target_pairs={{0,64},{32,96},{64,128},{96,160},{128,192},{160,224},{192,256},{22... | collective-permute-start | bytes 1867784 | tf_op jit(solution)/shard_map/ppermute | solution.py:317
  18.8 1.6 %tables.3 = (f32[1024,256]{1,0:T(8,128)S(1)}, f32[1024,256]{1,0:T(8,128)S(1)}) custom-call(bf16[4,1024,256]{2,1,0:T(8,128)(2,1)} %refs_0_.5, f32[1024,128]{1,0:T(8,128)S(1)} %get-tuple-element.63.refs_1_, f32[1216,128]{1,0:T(8,128)S(1)} %pack.1.refs_2_), custom_call_target="tpu_custom_call" | custom-call | flops 1048576 | bytes 1024 | tf_op jit(solution)/shard_map/tables/pallas_call | solution.py:40
  21.6 6.7 %collective-permute-done.3.refs_0_ = f32[304,128]{1,0:T(8,128)S(1)} collective-permute-done((f32[304,128]{1,0:T(8,128)S(1)}, f32[304,128]{1,0:T(8,128)S(1)}, u32[]{:S(2)}, u32[]{:S(2)}) %collective-permute-start.3) | collective-permute-done | bytes 155680 | tf_op jit(solution)/shard_map/ppermute | solution.py:317
  29.3 1.9 %collective-permute-start.4 = (f32[304,128]{1,0:T(8,128)S(1)}, f32[304,128]{1,0:T(8,128)S(1)}, u32[]{:S(2)}, u32[]{:S(2)}) collective-permute-start(f32[304,128]{1,0:T(8,128)S(1)} %get-tuple-element.70), channel_id=1, source_target_pairs={{0,32},{32,64},{64,96},{96,128},{128,160},{160,192},{192,224},{224... | collective-permute-start | bytes 466952 | tf_op jit(solution)/shard_map/ppermute | solution.py:317
  32.9 1.9 %collective-permute-start.2 = (f32[304,128]{1,0:T(8,128)S(1)}, f32[304,128]{1,0:T(8,128)S(1)}, u32[]{:S(2)}, u32[]{:S(2)}) collective-permute-start(f32[304,128]{1,0:T(8,128)S(1)} %get-tuple-element.66), channel_id=1, source_target_pairs={{0,32},{32,64},{64,96},{96,128},{128,160},{160,192},{192,224},{224... | collective-permute-start | bytes 466952 | tf_op jit(solution)/shard_map/ppermute | solution.py:317
  34.8 1.6 %tables.4 = (f32[1024,256]{1,0:T(8,128)S(1)}, f32[1024,256]{1,0:T(8,128)S(1)}) custom-call(bf16[4,1024,256]{2,1,0:T(8,128)(2,1)} %refs_0_.5, f32[1024,128]{1,0:T(8,128)S(1)} %get-tuple-element.63.refs_1_, bf16[1024,256]{1,0:T(8,128)(2,1)S(1)} %get-tuple-element.67.refs_2_.refs_3_), custom_call_target="tpu_custom_call" | custom-call | flops 1048576 | bytes 1024 | tf_op jit(solution)/shard_map/tables/pallas_call | solution.py:40
  37.7 10.9 %collective-permute-done.4.refs_1_ = f32[304,128]{1,0:T(8,128)S(1)} collective-permute-done((f32[304,128]{1,0:T(8,128)S(1)}, f32[304,128]{1,0:T(8,128)S(1)}, u32[]{:S(2)}, u32[]{:S(2)}) %collective-permute-start.4) | collective-permute-done | bytes 155680 | tf_op jit(solution)/shard_map/ppermute | solution.py:317
  49.7 1.9 %collective-permute-start.6 = (f32[304,128]{1,0:T(8,128)S(1)}, f32[304,128]{1,0:T(8,128)S(1)}, u32[]{:S(2)}, u32[]{:S(2)}) collective-permute-start(f32[304,128]{1,0:T(8,128)S(1)} %get-tuple-element.76), channel_id=1, source_target_pairs={{0,32},{32,64},{64,96},{96,128},{128,160},{160,192},{192,224},{224... | collective-permute-start | bytes 466952 | tf_op jit(solution)/shard_map/ppermute | solution.py:317
  52.8 2.1 %collective-permute-start.5 = (f32[304,128]{1,0:T(8,128)S(1)}, f32[304,128]{1,0:T(8,128)S(1)}, u32[]{:S(2)}, u32[]{:S(2)}) collective-permute-start(f32[304,128]{1,0:T(8,128)S(1)} %get-tuple-element.72), channel_id=1, source_target_pairs={{0,32},{32,64},{64,96},{96,128},{128,160},{160,192},{192,224},{224... | collective-permute-start | bytes 466952 | tf_op jit(solution)/shard_map/ppermute | solution.py:317
  54.9 1.6 %tables.5 = (f32[1024,256]{1,0:T(8,128)S(1)}, f32[1024,256]{1,0:T(8,128)S(1)}) custom-call(bf16[4,1024,256]{2,1,0:T(8,128)(2,1)} %refs_0_.5, f32[1024,128]{1,0:T(8,128)S(1)} %get-tuple-element.63.refs_1_, bf16[1024,256]{1,0:T(8,128)(2,1)S(1)} %get-tuple-element.73.refs_2_.refs_3_), custom_call_target="tpu_custom_call" | custom-call | flops 1048576 | bytes 1024 | tf_op jit(solution)/shard_map/tables/pallas_call | solution.py:40
  57.7 2.9 %collective-permute-done.6.vecs_ref = f32[304,128]{1,0:T(8,128)S(1)} collective-permute-done((f32[304,128]{1,0:T(8,128)S(1)}, f32[304,128]{1,0:T(8,128)S(1)}, u32[]{:S(2)}, u32[]{:S(2)}) %collective-permute-start.6) | collective-permute-done | bytes 155680 | tf_op jit(solution)/shard_map/ppermute | solution.py:317
  60.6 2.2 %last_first.1 = (f32[1024,384]{1,0:T(8,128)S(1)}, f32[304,128]{1,0:T(8,128)}, f32[304,128]{1,0:T(8,128)}) custom-call(f32[304,128]{1,0:T(8,128)S(1)} %collective-permute-done.6.vecs_ref, bf16[1024,384]{1,0:T(8,128)(2,1)S(1)} %get-tuple-element.52.refs_1_.refs_2_.turned_hi_ref, bf16[1024,384]{1,0:T(8,128)(2,1)S(1)} %get-tuple-element.53.refs_2_.refs_3_.turned_lo_ref, ...), custom_call_target="tpu_custom_call" | custom-call | flops 4294967296 | bytes 1024 | tf_op jit(solution)/shard_map/last_first/pallas_call | solution.py:40
  63.8 1.5 %last_second.1 = (bf16[1024,256]{1,0:T(8,128)(2,1)S(1)}, f32[640,256]{1,0:T(8,128)S(1)}, f32[640,256]{1,0:T(8,128)S(1)}) custom-call(f32[304,128]{1,0:T(8,128)S(1)} %collective-permute-done.5.refs_0_.vecs_ref, bf16[1024,384]{1,0:T(8,128)(2,1)S(1)} %get-tuple-element.52.refs_1_.refs_2_.turned_hi_ref, ...), custom_call_target="tpu_custom_call" | custom-call | flops 4294967296 | bytes 1024 | tf_op jit(solution)/shard_map/last_second/pallas_call | solution.py:40
  65.3 1.9 %collective-permute-start.7 = (f32[640,256]{1,0:T(8,128)S(1)}, f32[640,256]{1,0:T(8,128)S(1)}, u32[]{:S(2)}, u32[]{:S(2)}) collective-permute-start(f32[640,256]{1,0:T(8,128)S(1)} %get-tuple-element.87), channel_id=1, source_target_pairs={{0,1},{1,0},{2,3},{3,2},{4,5},{5,4},{6,7},{7,6},{8,9},{9,8},{10,11... | collective-permute-start | bytes 1966088 | tf_op jit(solution)/shard_map/ppermute | solution.py:322
  70.2 4.9 %all-to-all-start = ((f32[4,4,40,256]{3,2,1,0:T(8,128)}), f32[4,4,40,256]{3,2,1,0:T(8,128)S(1)}, u32[]{:S(2)}, u32[]{:S(2)}) async-start(f32[4,4,40,256]{3,2,1,0:T(8,128)} %sum.1), calls=%async_computation | async-start | bytes 1310720 | tf_op jit(solution)/shard_map/all_to_all | solution.py:458
  75.1 1.9 %collective-permute-start.8 = (f32[608,128]{1,0:T(8,128)S(1)}, f32[608,128]{1,0:T(8,128)S(1)}, u32[]{:S(2)}, u32[]{:S(2)}) collective-permute-start(f32[608,128]{1,0:T(8,128)S(1)} %get-tuple-element.95), channel_id=1, source_target_pairs={{0,32},{32,64},{64,96},{96,128},{128,160},{160,192},{192,224},{224... | collective-permute-start | bytes 933896 | tf_op jit(solution)/shard_map/ppermute | solution.py:317
  77.0 7.5 %all-to-all-done.parts_ref = f32[4,4,40,256]{3,2,1,0:T(8,128)S(1)} async-done(((f32[4,4,40,256]{3,2,1,0:T(8,128)}), f32[4,4,40,256]{3,2,1,0:T(8,128)S(1)}, u32[]{:S(2)}, u32[]{:S(2)}) %all-to-all-start) | async-done | bytes 655392 | tf_op jit(solution)/shard_map/all_to_all | solution.py:458
  85.2 7.1 %all-to-all-start.1 = ((f32[4,40,256]{2,1,0:T(8,128)}), f32[4,40,256]{2,1,0:T(8,128)S(1)}, u32[]{:S(2)}, u32[]{:S(2)}) async-start(f32[4,40,256]{2,1,0:T(8,128)} %four.1), calls=%async_computation.1 | async-start | bytes 327680 | tf_op jit(solution)/shard_map/all_to_all | solution.py:460
  92.3 1.2 %shares.1 = (f32[32,300]{1,0:T(8,128)S(1)}, f32[32,300]{1,0:T(8,128)S(1)}) custom-call(f32[300,1024]{1,0:T(8,128)} %row_hbm.3, f32[300,1024]{1,0:T(8,128)} %acc_hbm.1), custom_call_target="tpu_custom_call" | custom-call | flops 4294967296 | bytes 1024 | tf_op jit(solution)/shard_map/shares/pallas_call | solution.py:40
  93.5 2.1 %last_update.1 = (f32[300,256]{1,0:T(8,128)}, f32[300,256]{1,0:T(8,128)}) custom-call(f32[304,128]{1,0:T(8,128)} %get-tuple-element.92.kept_a_hbm, f32[304,128]{1,0:T(8,128)} %get-tuple-element.85.kept_ref.kept_b_hbm, f32[304,128]{1,0:T(8,128)} %get-tuple-element.93.col_grad_a_hbm, f32[304,128]{1,0:T(8,128)} %get-tuple-element.94.col_grad_b_hbm, ...), custom_call_target="tpu_custom_call" | custom-call | flops 1048576 | bytes 1024 | tf_op jit(solution)/shard_map/last_update/pallas_call | solution.py:40
  95.7 5.9 %all-to-all-done.1.parts_ref = f32[4,40,256]{2,1,0:T(8,128)S(1)} async-done(((f32[4,40,256]{2,1,0:T(8,128)}), f32[4,40,256]{2,1,0:T(8,128)S(1)}, u32[]{:S(2)}, u32[]{:S(2)}) %all-to-all-start.1) | async-done | bytes 163872 | tf_op jit(solution)/shard_map/all_to_all | solution.py:460
  (20 shorter events, 16.1 us)
Async XLA Ops:
  4.2 24.1 %collective-permute-start.3 = (f32[304,128]{1,0:T(8,128)S(1)}, f32[304,128]{1,0:T(8,128)S(1)}, u32[]{:S(2)}, u32[]{:S(2)}) collective-permute-start(f32[304,128]{1,0:T(8,128)S(1)} %get-tuple-element.58.refs_0_), channel_id=1, source_target_pairs={{0,32},{32,64},{64,96},{96,128},{128,160},{160,192},{192,224},{224... | collective-permute-start | bytes 466952 | tf_op jit(solution)/shard_map/ppermute | solution.py:317
  9.3 22.5 %collective-permute-start.1 = (f32[304,128]{1,0:T(8,128)S(1)}, f32[304,128]{1,0:T(8,128)S(1)}, u32[]{:S(2)}, u32[]{:S(2)}) collective-permute-start(f32[304,128]{1,0:T(8,128)S(1)} %get-tuple-element.61.refs_2_), channel_id=1, source_target_pairs={{0,32},{32,64},{64,96},{96,128},{128,160},{160,192},{192,224},{224... | collective-permute-start | bytes 466952 | tf_op jit(solution)/shard_map/ppermute | solution.py:317
  14.5 34.0 %collective-permute-start = (f32[1216,128]{1,0:T(8,128)S(1)}, f32[1216,128]{1,0:T(8,128)S(1)}, u32[]{:S(2)}, u32[]{:S(2)}) collective-permute-start(f32[1216,128]{1,0:T(8,128)S(1)} %pack.1.refs_2_), channel_id=1, source_target_pairs={{0,64},{32,96},{64,128},{96,160},{128,192},{160,224},{192,256},{22... | collective-permute-start | bytes 1867784 | tf_op jit(solution)/shard_map/ppermute | solution.py:317
  29.3 19.2 %collective-permute-start.4 = (f32[304,128]{1,0:T(8,128)S(1)}, f32[304,128]{1,0:T(8,128)S(1)}, u32[]{:S(2)}, u32[]{:S(2)}) collective-permute-start(f32[304,128]{1,0:T(8,128)S(1)} %get-tuple-element.70), channel_id=1, source_target_pairs={{0,32},{32,64},{64,96},{96,128},{128,160},{160,192},{192,224},{224... | collective-permute-start | bytes 466952 | tf_op jit(solution)/shard_map/ppermute | solution.py:317
  32.9 18.7 %collective-permute-start.2 = (f32[304,128]{1,0:T(8,128)S(1)}, f32[304,128]{1,0:T(8,128)S(1)}, u32[]{:S(2)}, u32[]{:S(2)}) collective-permute-start(f32[304,128]{1,0:T(8,128)S(1)} %get-tuple-element.66), channel_id=1, source_target_pairs={{0,32},{32,64},{64,96},{96,128},{128,160},{160,192},{192,224},{224... | collective-permute-start | bytes 466952 | tf_op jit(solution)/shard_map/ppermute | solution.py:317
  49.7 10.9 %collective-permute-start.6 = (f32[304,128]{1,0:T(8,128)S(1)}, f32[304,128]{1,0:T(8,128)S(1)}, u32[]{:S(2)}, u32[]{:S(2)}) collective-permute-start(f32[304,128]{1,0:T(8,128)S(1)} %get-tuple-element.76), channel_id=1, source_target_pairs={{0,32},{32,64},{64,96},{96,128},{128,160},{160,192},{192,224},{224... | collective-permute-start | bytes 466952 | tf_op jit(solution)/shard_map/ppermute | solution.py:317
  52.8 11.0 %collective-permute-start.5 = (f32[304,128]{1,0:T(8,128)S(1)}, f32[304,128]{1,0:T(8,128)S(1)}, u32[]{:S(2)}, u32[]{:S(2)}) collective-permute-start(f32[304,128]{1,0:T(8,128)S(1)} %get-tuple-element.72), channel_id=1, source_target_pairs={{0,32},{32,64},{64,96},{96,128},{128,160},{160,192},{192,224},{224... | collective-permute-start | bytes 466952 | tf_op jit(solution)/shard_map/ppermute | solution.py:317
  65.3 4.0 %collective-permute-start.7 = (f32[640,256]{1,0:T(8,128)S(1)}, f32[640,256]{1,0:T(8,128)S(1)}, u32[]{:S(2)}, u32[]{:S(2)}) collective-permute-start(f32[640,256]{1,0:T(8,128)S(1)} %get-tuple-element.87), channel_id=1, source_target_pairs={{0,1},{1,0},{2,3},{3,2},{4,5},{5,4},{6,7},{7,6},{8,9},{9,8},{10,11... | collective-permute-start | bytes 1966088 | tf_op jit(solution)/shard_map/ppermute | solution.py:322
  70.2 14.3 %all-to-all-start = ((f32[4,4,40,256]{3,2,1,0:T(8,128)}), f32[4,4,40,256]{3,2,1,0:T(8,128)S(1)}, u32[]{:S(2)}, u32[]{:S(2)}) async-start(f32[4,4,40,256]{3,2,1,0:T(8,128)} %sum.1), calls=%async_computation | async-start | bytes 1310720 | tf_op jit(solution)/shard_map/all_to_all | solution.py:458
  75.1 18.5 %collective-permute-start.8 = (f32[608,128]{1,0:T(8,128)S(1)}, f32[608,128]{1,0:T(8,128)S(1)}, u32[]{:S(2)}, u32[]{:S(2)}) collective-permute-start(f32[608,128]{1,0:T(8,128)S(1)} %get-tuple-element.95), channel_id=1, source_target_pairs={{0,32},{32,64},{64,96},{96,128},{128,160},{160,192},{192,224},{224... | collective-permute-start | bytes 933896 | tf_op jit(solution)/shard_map/ppermute | solution.py:317
  85.2 16.4 %all-to-all-start.1 = ((f32[4,40,256]{2,1,0:T(8,128)}), f32[4,40,256]{2,1,0:T(8,128)S(1)}, u32[]{:S(2)}, u32[]{:S(2)}) async-start(f32[4,40,256]{2,1,0:T(8,128)} %four.1), calls=%async_computation.1 | async-start | bytes 327680 | tf_op jit(solution)/shard_map/all_to_all | solution.py:460
